TPU v7x, 512 devices: a whole 4x8x8 slice. The times are simulated.
512 devices in a mesh: grp: 16 (over y, core), seq: 32 (over z, x).
Axes of the slice: x: 4, y: 8, z: 8, core: 2. Of those that a mesh axis runs over, the one named last changes fastest.
Arguments:
- conv_input: bfloat16 [65536, 9216], P(('grp', 'seq')), may hold values from -6 to 6
- conv_weight: float32 [4, 9216], replicated, may hold values from -3 to 3
- step_raw: float32 [65536, 128], P(('grp', 'seq')), may hold values from -30 to 1
- decay_log: float32 [128], replicated, may hold values from -12 to 6
- skip_gain: float32 [128], replicated, may hold values from 0.5 to 2
Outputs:
- mixer_output: bfloat16 [65536, 8192], P(('grp', 'seq'))
All inputs are finite; a program needn't handle non-finite values.
Results may differ from a plain program's by a relative error of at most 0.005.
The roundings to bfloat16 on the way count: a program that leaves them out, or rounds other values in their place, can miss the bound.
Values may be sent and summed in bfloat16 or wider, within the bound.
No kernel may reach another device: no remote copies, remote signals or barrier semaphores. Data moves between devices by JAX's collectives and lax.ppermute only.
A program may use at most 64 MiB of HBM per device.

v0:
```python
import jax
import jax.numpy as jnp
from jax import lax
from jax.sharding import PartitionSpec as P

HEADS = 128
HEAD_DIM = 64
STATE = 128
GROUPS = 4
KERNEL = 4


def passed_along(value, axis, steps):
    count = lax.axis_size(axis)
    initial, last = (max(0, -steps), min(count, count - steps))
    return lax.ppermute(value, axis, [(source, source + steps) for source in range(initial, last)])


def carried_in(part, axis, combine, identity):
    place = lax.axis_index(axis)
    gathered = jax.tree.map(lambda a: lax.all_gather(a, axis), part)
    state = jax.tree.map(lambda a, e: jnp.zeros_like(a) + jnp.asarray(e, a.dtype), part, identity)

    def one(turn, state):
        return combine(
            state, jax.tree.map(lambda a: lax.dynamic_index_in_dim(a, turn, 0, False), gathered)
        )

    return lax.fori_loop(0, place, one, state)


def as_sent(shard):

    def short(part):
        return part.astype(jnp.bfloat16) if part.dtype == jnp.float32 else part

    return jax.tree.map(short, shard)


def combine(earlier, later):
    return (earlier[0] * later[0], later[0] * earlier[1] + later[1])


def body(conv_input, conv_weight, step_raw, decay_log, skip_gain):
    length = conv_input.shape[0]
    per_group = HEADS // GROUPS
    head_cols = HEADS * HEAD_DIM
    group_cols = GROUPS * STATE
    entries = HEAD_DIM * STATE
    shards = lax.axis_size("seq")
    share = entries // shards
    edge_rows = passed_along(conv_input[length - KERNEL + 1 :], ("grp", "seq"), 1)
    widened = jnp.concatenate([edge_rows, conv_input], 0).astype(jnp.float32)
    convolved = jnp.zeros((length, conv_input.shape[1]), jnp.float32)
    for tap in range(KERNEL):
        convolved = convolved + widened[tap : tap + length] * conv_weight[tap]
    values = (
        convolved[:, :head_cols].astype(jnp.bfloat16).reshape(length, GROUPS, per_group, HEAD_DIM)
    )
    writers = (
        convolved[:, head_cols : head_cols + group_cols]
        .astype(jnp.bfloat16)
        .reshape(length, GROUPS, STATE)
    )
    readers = (
        convolved[:, head_cols + group_cols :].astype(jnp.bfloat16).reshape(length, GROUPS, STATE)
    )
    step_size = jax.nn.softplus(step_raw)
    cumulative = jnp.cumsum(-jnp.exp(decay_log) * step_size, axis=0)
    last = cumulative[length - 1]
    factor = (jnp.exp(last - cumulative) * step_size).reshape(length, GROUPS, per_group, 1)
    weighted = (values.astype(jnp.float32) * factor).astype(jnp.bfloat16)
    block_state = jnp.einsum(
        "ugkp,ugn->gkpn", weighted, writers, preferred_element_type=jnp.float32
    )
    growth = jnp.exp(cumulative)
    states_flat = block_state.reshape(1, HEADS, entries)
    log_tiled = jnp.broadcast_to(last.reshape(1, HEADS, 1), (1, HEADS, shards))
    log_rows, state_rows = (
        lax.all_to_all(log_tiled, "seq", split_axis=2, concat_axis=0, tiled=True),
        lax.all_to_all(states_flat, "seq", split_axis=2, concat_axis=0, tiled=True),
    )
    log_rows = log_rows.reshape(shards, HEADS)
    affinity = jnp.einsum("tgn,ugn->gtu", readers, writers, preferred_element_type=jnp.float32)
    cum_heads = cumulative.T.reshape(GROUPS, per_group, length)
    differences = cum_heads[:, :, :, None] - cum_heads[:, :, None, :]
    positions = jnp.arange(length, dtype=jnp.int32)
    causal = positions[:, None] >= positions[None, :]
    weights = jnp.exp(jnp.where(causal, differences, -jnp.inf)) * step_size.T.reshape(
        GROUPS, per_group, 1, length
    )
    scores = (weights * affinity[:, None]).astype(jnp.bfloat16)
    local_part = jnp.einsum("gktu,ugkp->tgkp", scores, values, preferred_element_type=jnp.float32)
    inclusive = jnp.cumsum(log_rows, axis=0)
    exclusive = jnp.concatenate([jnp.zeros((1, HEADS), jnp.float32), inclusive], 0)
    row_index = jnp.arange(shards + 1, dtype=jnp.int32)
    col_index = jnp.arange(shards, dtype=jnp.int32)
    earlier_mask = col_index[None, :, None] < row_index[:, None, None]
    spans = jnp.where(earlier_mask, exclusive[:, None, :] - inclusive[None, :, :], -jnp.inf)
    carry_weights = jnp.exp(spans)
    summed = jnp.einsum("jih,ihe->jhe", carry_weights, state_rows, precision=lax.Precision.HIGHEST)
    before_state = summed[:shards]
    before_decay = jnp.exp(exclusive[:shards])
    total_log = exclusive[shards]
    total_state = summed[shards]
    neutral = (jnp.ones((HEADS, 1), jnp.float32), jnp.zeros((HEADS, share), jnp.float32))
    group_total = (jnp.exp(total_log).reshape(HEADS, 1), total_state)
    group_entry = carried_in(group_total, "grp", combine, neutral)[1]
    entering_rows = before_decay[:, :, None] * group_entry[None] + before_state
    entering_back = lax.all_to_all(
        as_sent(entering_rows), "seq", split_axis=0, concat_axis=2, tiled=True
    ).astype(entering_rows.dtype)
    entering_low = entering_back.reshape(GROUPS, per_group, HEAD_DIM, STATE).astype(jnp.bfloat16)
    carried_part = jnp.einsum(
        "tgn,gkpn->tgkp", readers, entering_low, preferred_element_type=jnp.float32
    )
    carried_part = carried_part * growth.reshape(length, GROUPS, per_group, 1)
    result = (
        local_part
        + carried_part
        + skip_gain.reshape(GROUPS, per_group, 1) * values.astype(jnp.float32)
    )
    return result.reshape(length, head_cols).astype(jnp.bfloat16)


def solution(mesh):
    in_specs = (P(("grp", "seq"), None), P(), P(("grp", "seq"), None), P(), P())
    out_specs = P(("grp", "seq"), None)
    return jax.shard_map(body, mesh=mesh, in_specs=in_specs, out_specs=out_specs, check_vma=False)
```

profile of v0, /device:TPU:59, one launch (start us, length us, event | category | flops | bytes accessed | tf_op | source)
XLA Modules:
  0.0 330.7 jit_solution(9986968943279861682)
XLA Ops:
  6.5 0.9 slice.54
  7.5 3.1 collective-permute-start
  10.6 0.7 exponential_negate_fusion
  11.3 0.9 broadcast_multiply_fusion
  12.2 0.2 reduce_window_sum.22
  12.3 0.6 broadcast_in_dim.45
  13.0 12.6 %all-to-all-start = ((f32[1,128,32]{1,0,2:T(1,128)}), f32[1,128,32]{1,0,2:T(1,128)S(1)}, u32[]{:S(2)}, u32[]{:S(2)}) async-start(f32[1,128,32]{1,0,2:T(1,128)} %broadcast_in_dim.45), calls=%async_computation | async-start | bytes 32768 | tf_op jit(solution)/shard_map/all_to_all | solution.py:80
  25.6 1.3 fusion.36
  26.9 0.9 fusion.37
  27.8 4.3 %copy.33 = bf16[128,9216]{0,1:T(8,128)(2,1)} copy(bf16[128,9216]{1,0:T(8,128)(2,1)} %param.7) | data formatting | bytes 4718592 | tf_op args[0]
  32.0 0.1 copy.39
  32.1 2.0 copy.32
  34.1 3.4 %maximum_convert_fusion = f32[131,9216]{0,1:T(8,128)S(1)} fusion(bf16[128,9216]{0,1:T(8,128)(2,1)} %copy.33, bf16[3,9216]{0,1:T(8,128)(2,1)} %copy.32), kind=kLoop, calls=%fused_computation.13 | loop fusion | flops 4829184 | bytes 7243776 | tf_op jit(solution)/shard_map/convert_element_type | solution.py:53
  37.5 9.8 %fusion.1 = bf16[128,9216]{0,1:T(8,128)(2,1)S(1)} fusion(f32[131,9216]{0,1:T(8,128)S(1)} %maximum_convert_fusion, f32[9216]{0:T(1024)S(1)} %bitcast.87, f32[9216]{0:T(1024)S(1)} %bitcast.88, f32[9216]{0:T(1024)S(1)} %bitcast.86, f32[9216]{0:T(1024)S(1)} %bitcast.85), kind=kLoop, calls=%fused_computation.7 | loop fusion | flops 9437184 | bytes 21381120 | tf_op jit(solution)/shard_map/convert.2
  47.4 0.1 slice.75
  47.6 2.7 fusion.21
  50.3 4.9 %reshape.77 = f32[1,128,8192]{2,1,0:T(8,128)} reshape(f32[4,32,64,128]{3,2,1,0:T(8,128)} %fusion.21) | data formatting | bytes 8388608 | tf_op jit(solution)/shard_map/reshape | solution.py:77
  55.2 9.7 %copy.41 = f32[1,128,8192]{1,0,2:T(1,128)} copy(f32[1,128,8192]{2,1,0:T(8,128)} %reshape.77) | data formatting | bytes 8388608 | tf_op jit(solution)/shard_map/reshape | solution.py:77
  64.9 9.3 %all-to-all-start.1 = ((f32[1,128,8192]{1,0,2:T(1,128)}), f32[1,128,8192]{1,0,2:T(1,128)}, u32[]{:S(2)}, u32[]{:S(2)}) async-start(f32[1,128,8192]{1,0,2:T(1,128)} %copy.41), calls=%async_computation.1 | async-start | bytes 8388608 | tf_op jit(solution)/shard_map/all_to_all | solution.py:81
  74.2 0.0 all-gather.4.cloned.1.call-start
  74.2 0.1 reduce_window_sum.23
  74.3 0.1 copy.44
  74.4 0.1 concatenate.7.clone
  74.5 92.8 %all-to-all-done.1 = f32[1,128,8192]{1,0,2:T(1,128)} async-done(((f32[1,128,8192]{1,0,2:T(1,128)}), f32[1,128,8192]{1,0,2:T(1,128)}, u32[]{:S(2)}, u32[]{:S(2)}) %all-to-all-start.1) | async-done | bytes 4194336 | tf_op jit(solution)/shard_map/all_to_all | solution.py:81
  167.2 5.5 %copy.58 = f32[1,128,32,256]{3,2,1,0:T(8,128)} copy(f32[1,128,32,256]{1,3,2,0:T(8,128)} %bitcast.23) | data formatting | bytes 8388608 | tf_op jit(solution)/shard_map/all_to_all | solution.py:81
  172.7 7.3 %fusion.18 = f32[33,128,256]{2,0,1:T(8,128)S(1)} fusion(f32[1,128,32,256]{3,2,1,0:T(8,128)} %copy.58, f32[32,128]{0,1:T(8,128)S(1)} %copy.44, f32[33,128]{0,1:T(8,128)S(1)} %concatenate.7.clone, pred[33,32]{0,1:T(8,128)(4,1)S(1)} %iota_compare_fusion.1), kind=kOutput, calls=%fused_computation.30 | convolution fusion | flops 415506432 | bytes 8554016 | tf_op jit(solution)/shard_map/jih,ihe->jhe/dot_general | solution.py:101
  180.0 2.3 copy-done
  182.3 0.1 slice.80
  182.4 0.7 copy.45
  183.0 0.0 all-gather.4.cloned.1.call-update
  183.1 0.1 copy.38
  183.2 15.9 %all-gather.1 = f32[16,1,128]{2,1,0:T(1,128)S(1)} all-gather(f32[1,1,128]{2,1,0:T(1,128)S(1)} %fusion.32), channel_id=2, replica_groups=mesh['grp'=16,'seq'=32] {'grp'}, dimensions={0}, use_global_device_ids=true | all-gather | bytes 8704 | tf_op jit(solution)/shard_map/all_gather | solution.py:21
  199.1 24.6 %all-gather.4.cloned.1.call-done = f32[16,128,256]{2,1,0:T(8,128)} async-done(((f32[1,128,256]{2,1,0:T(8,128)}), f32[16,128,256]{2,1,0:T(8,128)}) %all-gather.4.cloned.1.call-update) | async-done | bytes 2097168 | tf_op jit(solution)/shard_map/all_gather | solution.py:21
  223.8 15.7 %while.12 = (s32[]{:T(128)}, f32[128,256]{1,0:T(8,128)S(1)}, s32[]{:T(128)}, f32[16,128,1]{1,2,0:T(1,128)S(1)}, f32[16,128,256]{2,1,0:T(8,128)}, /*index=5*/s32[]{:T(128)}, s32[]{:T(128)}, s32[]{:T(128)}) while((s32[]{:T(128)}, f32[128,256]{1,0:T(8,128)S(1)}, s32[]{:T(128)}, f32[16,128,1]{1,2,0:T(1,128)S(1)}, f32[16,128,256]{2,1,0:T(8,128)}, ...), condition=%wide.region_3.4_spmd, body=%wide.region_2.3_spmd.sunk | while | flops 65541 | bytes 394879 | solution.py:29
  223.8 1.0 bitcast_add_fusion.2
  224.9 1.0 bitcast_add_fusion.2
  225.9 1.0 bitcast_add_fusion.2
  227.0 1.0 bitcast_add_fusion.2
  228.0 1.0 bitcast_add_fusion.2
  229.0 1.0 bitcast_add_fusion.2
  230.1 1.0 bitcast_add_fusion.2
  231.1 1.0 bitcast_add_fusion.2
  232.2 1.0 bitcast_add_fusion.2
  233.2 1.0 bitcast_add_fusion.2
  234.3 1.0 bitcast_add_fusion.2
  235.3 1.0 bitcast_add_fusion.2
  236.4 1.0 bitcast_add_fusion.2
  237.4 1.0 bitcast_add_fusion.2
  238.5 1.0 bitcast_add_fusion.2
  239.5 2.6 fusion.8
  242.1 0.0 copy-start.1
  242.1 2.5 copy.47
  244.6 10.0 %all-to-all-start.2 = ((bf16[32,128,256]{2,1,0:T(8,128)(2,1)}), bf16[32,128,256]{2,1,0:T(8,128)(2,1)}, u32[]{:S(2)}, u32[]{:S(2)}) async-start(bf16[32,128,256]{2,1,0:T(8,128)(2,1)} %copy.47), calls=%async_computation.2 | async-start | bytes 4194304 | tf_op jit(solution)/shard_map/all_to_all | solution.py:110
  254.7 0.1 copy.35
  254.8 0.1 copy.34
  254.9 0.1 copy.50
  255.0 0.1 mul.153
  255.1 0.2 fusion.38
  255.3 6.0 %fusion.4 = f32[4,32,64,128]{3,2,1,0:T(8,128)} fusion(bf16[128,4,32,64]{0,3,2,1:T(8,128)(2,1)S(1)} %bitcast.75, f32[4,128,128]{2,1,0:T(8,128)S(1)} %fusion.38, f32[4,32,128]{2,1,0:T(8,128)S(1)} %bitcast.89, f32[4,32,128]{2,1,0:T(8,128)S(1)} %bitcast.90, pred[128,128]{1,0:T(8,128)(4,1)S(1)} %iota_compare_fusion), kind=kOutput, calls=%fused_computation.14 | convolution fusion | flops 278921216 | bytes 6701056 | tf_op jit(solution)/shard_map/gktu,ugkp->tgkp/dot_general | solution.py:93
  261.3 45.2 %all-to-all-done.2 = bf16[32,128,256]{2,1,0:T(8,128)(2,1)} async-done(((bf16[32,128,256]{2,1,0:T(8,128)(2,1)}), bf16[32,128,256]{2,1,0:T(8,128)(2,1)}, u32[]{:S(2)}, u32[]{:S(2)}) %all-to-all-start.2) | async-done | bytes 2097184 | tf_op jit(solution)/shard_map/all_to_all | solution.py:110
  306.5 4.1 %copy.48 = bf16[1,128,32,256]{3,2,1,0:T(8,128)(2,1)} copy(bf16[1,128,32,256]{3,1,2,0:T(8,128)(2,1)} %bitcast.28) | data formatting | bytes 4194304 | tf_op jit(solution)/shard_map/all_to_all | solution.py:110
  310.6 4.1 %all_to_all.47 = bf16[4,32,64,128]{3,2,1,0:T(8,128)(2,1)} reshape(bf16[1,128,32,256]{3,2,1,0:T(8,128)(2,1)} %copy.48) | data formatting | bytes 4194304 | tf_op jit(solution)/shard_map/all_to_all | solution.py:110
  314.7 5.1 %fusion.7 = bf16[128,4,32,64]{0,3,2,1:T(8,128)(2,1)} fusion(bf16[128,4,32,64]{0,3,2,1:T(8,128)(2,1)S(1)} %bitcast.76, f32[4,32,64,128]{3,2,1,0:T(8,128)} %fusion.4, bf16[4,32,64,128]{3,2,1,0:T(8,128)(2,1)} %all_to_all.47, bf16[128,4,128,1]{0,2,3,1:T(8,128)(2,1)S(1)} %bitcast.79, f32[4,32]{1,0:T(4,128)S(1)} %mul.153, f32[128,4,32]{0,2,1:T(8,128)S(1)} %bitcast.84), kind=kOutput, calls=%fused_computation.17 | convolution fusion | flops 274726912 | bytes 10682880 | tf_op jit(solution)/shard_map/tgn,gkpn->tgkp/dot_general | solution.py:114
  319.8 4.1 %copy.51 = bf16[128,8192]{1,0:T(8,128)(2,1)} copy(bf16[128,8192]{0,1:T(8,128)(2,1)} %bitcast.77) | data formatting | bytes 4194304 | tf_op jit(solution)/shard_map/convert_element_type | solution.py:123
  (26 shorter events, 0.2 us)
Async XLA Ops:
  7.5 24.7 %collective-permute-start = (bf16[3,9216]{1,0:T(4,128)(2,1)S(1)}, bf16[3,9216]{1,0:T(4,128)(2,1)S(1)}, u32[]{:S(2)}, u32[]{:S(2)}) collective-permute-start(bf16[3,9216]{1,0:T(4,128)(2,1)S(1)} %slice.54), channel_id=1, source_target_pairs={{0,1},{1,2},{2,3},{3,4},{4,5},{5,6},{6,7},{7,8},{8,9},{9,10},{10,1... | collective-permute-start | bytes 165896 | tf_op jit(solution)/shard_map/ppermute | solution.py:16
  13.0 51.9 %all-to-all-start = ((f32[1,128,32]{1,0,2:T(1,128)}), f32[1,128,32]{1,0,2:T(1,128)S(1)}, u32[]{:S(2)}, u32[]{:S(2)}) async-start(f32[1,128,32]{1,0,2:T(1,128)} %broadcast_in_dim.45), calls=%async_computation | async-start | bytes 32768 | tf_op jit(solution)/shard_map/all_to_all | solution.py:80
  64.9 102.4 %all-to-all-start.1 = ((f32[1,128,8192]{1,0,2:T(1,128)}), f32[1,128,8192]{1,0,2:T(1,128)}, u32[]{:S(2)}, u32[]{:S(2)}) async-start(f32[1,128,8192]{1,0,2:T(1,128)} %copy.41), calls=%async_computation.1 | async-start | bytes 8388608 | tf_op jit(solution)/shard_map/all_to_all | solution.py:81
  74.2 149.6 %all-gather.4.cloned.1.call-start = ((), (), s32[]{:S(2)}) async-start(), calls=%async_computation.3 | async-start | bytes 2228224 | tf_op jit(solution)/shard_map/all_gather | solution.py:21
  180.0 2.3 copy-start
  242.1 12.8 %copy-start.1 = (f32[128]{0:T(128)S(1)}, f32[128]{0:T(128)}, u32[]{:S(2)}) copy-start(f32[128]{0:T(128)} %param.11) | copy-start | bytes 1540
  244.6 61.9 %all-to-all-start.2 = ((bf16[32,128,256]{2,1,0:T(8,128)(2,1)}), bf16[32,128,256]{2,1,0:T(8,128)(2,1)}, u32[]{:S(2)}, u32[]{:S(2)}) async-start(bf16[32,128,256]{2,1,0:T(8,128)(2,1)} %copy.47), calls=%async_computation.2 | async-start | bytes 4194304 | tf_op jit(solution)/shard_map/all_to_all | solution.py:110
Sparse Core Ops, SparseCore 0:
  183.2 40.5 all-gather.3
where the time goes:
time: 332 us; the launch traced here: 331 us
  waiting for transfers between devices  163 us (49%)
  local copies, waits for them, and re-layouts  48 us (14%)
  starting transfers between devices  35 us (11%)
  other arithmetic  33.6 us (10%)
  matrix products  21.4 us (6%)
  blocking collectives  15.9 us (5%)
  between operations  13.6 us (4%)
    all_to_all x1, waiting for transfers between devices, body(): lax.all_to_all(states_flat, 'seq', split_axis=2, concat_axis=0, tiled=True)  92.8 us
    all_to_all x1, waiting for transfers between devices, body(): lax.all_to_all(as_sent(entering_rows), 'seq', split_axis=0, concat_axis=2...  45.2 us
    all_gather x1, waiting for transfers between devices, carried_in(): gathered = jax.tree.map(lambda a: lax.all_gather(a, axis), part)  24.6 us
    all_gather x1, blocking collectives, carried_in(): gathered = jax.tree.map(lambda a: lax.all_gather(a, axis), part)  15.9 us
    add x15, other arithmetic, combine(): return (earlier[0] * later[0], later[0] * earlier[1] + later[1])  15 us
    reshape x2, local copies, waits for them, and re-layouts, body(): states_flat = block_state.reshape(1, HEADS, entries)  14.6 us
    all_to_all x1, starting transfers between devices, body(): lax.all_to_all(log_tiled, 'seq', split_axis=2, concat_axis=0, tiled=True)  12.6 us
    all_to_all x1, starting transfers between devices, body(): lax.all_to_all(as_sent(entering_rows), 'seq', split_axis=0, concat_axis=2...  10 us
  transfers between devices with their start and end apart: 5, of which 3 were waited for; matrix products, arithmetic and copies ran while one was open for 15% of the time, Pallas kernels for 0%

commit v1 on v0

v1 whole, which is shorter than its diff:
```python
import functools

import jax
import jax.numpy as jnp
from jax import lax
from jax.experimental import pallas as pl
from jax.experimental.pallas import tpu as pltpu
from jax.sharding import Mesh, PartitionSpec as P

HEADS = 128
HEAD_DIM = 64
STATE = 128
GROUPS = 4
KERNEL = 4
TOK = 128
PER = HEADS // GROUPS
GCOLS = PER * HEAD_DIM
NB = GCOLS // 128
HCOLS = HEADS * HEAD_DIM
ROWS = NB * STATE
PAY = ROWS + 3 * NB
SHARES = 64
SROWS = ROWS // SHARES
TROWS = SROWS + 8
NX, NY, NZ = 4, 8, 8
F32 = jnp.float32
BF16 = jnp.bfloat16
LIMIT = 32 * 1024 * 1024
AXES = ("y", "core", "z", "x")


def params():
    return pltpu.CompilerParams(vmem_limit_bytes=LIMIT)


def three(v):
    hi = v.astype(BF16).astype(F32)
    mid = (v - hi).astype(BF16).astype(F32)
    low = (v - hi - mid).astype(BF16).astype(F32)
    return hi, mid, low


def lanes_of(per_head, base, block, rows):
    lane = lax.broadcasted_iota(jnp.int32, (rows, 128), 1)
    pick = base + 2 * block + lane // HEAD_DIM
    return jnp.take_along_axis(per_head, pick, axis=1)


def prep_kernel(raw_ref, log_ref, cum_ref, factor_ref, growth_ref, cum_t_ref, step_t_ref, decay_ref):
    raw = raw_ref[...]
    step = jnp.maximum(raw, 0.0) + jnp.log1p(jnp.exp(-jnp.abs(raw)))
    cum = -jnp.exp(log_ref[...]) * step
    row = lax.broadcasted_iota(jnp.int32, (TOK, HEADS), 0)
    shift = 1
    while shift < TOK:
        cum = cum + jnp.where(row >= shift, pltpu.roll(cum, shift, 0), 0.0)
        shift *= 2
    last = cum[TOK - 1 :, :]
    cum_ref[...] = cum
    factor_ref[...] = jnp.exp(last - cum) * step
    growth_ref[...] = jnp.exp(cum)
    cum_t_ref[...] = cum.T
    step_t_ref[...] = step.T
    decay_ref[...] = jnp.broadcast_to(jnp.exp(last), (8, HEADS))


def prep(step_raw, decay_log):
    square = jax.ShapeDtypeStruct((TOK, HEADS), F32)
    return pl.pallas_call(
        prep_kernel,
        out_shape=[square] * 5 + [jax.ShapeDtypeStruct((8, HEADS), F32)],
        compiler_params=params(),
    )(step_raw, decay_log.reshape(1, HEADS))


def convolve(x_ref, edge_ref, w_ref, lo):
    cols = slice(lo, lo + 128)
    x = x_ref[:, cols].astype(F32)
    edge = edge_ref[:, cols].astype(F32)
    wide = jnp.concatenate([jnp.zeros((8 - KERNEL + 1, 128), F32), edge, x], 0)
    out = None
    for tap in range(KERNEL):
        at = 8 - KERNEL + 1 + tap
        term = wide[at : at + TOK] * w_ref[tap : tap + 1, cols]
        out = term if out is None else out + term
    return out.astype(BF16)


CHUNKS = 4
CB = NB // CHUNKS


def state_kernel(
    pick_ref, xv, xw, xr, ev, ew, er, wv, ww, wr, factor_ref, decay_ref,
    pay_ref, val_ref, wri_ref, rea_ref, wt_ref,
):
    step = pl.program_id(0)
    base = pick_ref[0] * PER

    @pl.when(step == 0)
    def _():
        writers = convolve(xw, ew, ww, 0)
        wri_ref[...] = writers
        wt_ref[...] = writers.astype(F32).T.astype(BF16)
        rea_ref[...] = convolve(xr, er, wr, 0)
        rows = [lanes_of(decay_ref[...], base, b, 8)[:1] for b in range(NB)]
        for at, term in enumerate(three(jnp.concatenate(rows, 0))):
            pay_ref[ROWS + at * NB : ROWS + (at + 1) * NB] = term.astype(BF16)

    factor = factor_ref[...]
    for pair in range(CB // 2):
        weighted = []
        for half in range(2):
            b = 2 * pair + half
            value = convolve(xv, ev, wv, b * 128)
            val_ref[:, b * 128 : (b + 1) * 128] = value
            fac = lanes_of(factor, base, step * CB + b, TOK)
            weighted.append((value.astype(F32) * fac).astype(BF16))
        state = jnp.dot(wt_ref[...], jnp.concatenate(weighted, 1), preferred_element_type=F32)
        for half in range(2):
            at = pl.multiple_of((step * CB + 2 * pair + half) * STATE, STATE)
            pay_ref[pl.ds(at, STATE)] = state[:, half * 128 : (half + 1) * 128].astype(BF16)


def states(pick, conv_input, edge, conv_weight, factor, decay):
    width = CB * 128
    head_blocks = HCOLS // 128

    def three_of(rows):
        return [
            pl.BlockSpec((rows, width), lambda i, p: (0, p[0] * CHUNKS + i)),
            pl.BlockSpec((rows, 128), lambda i, p: (0, head_blocks + p[0])),
            pl.BlockSpec((rows, 128), lambda i, p: (0, head_blocks + GROUPS + p[0])),
        ]

    whole = lambda shape: pl.BlockSpec(shape, lambda i, p: (0, 0))
    return pl.pallas_call(
        state_kernel,
        grid_spec=pltpu.PrefetchScalarGridSpec(
            num_scalar_prefetch=1,
            grid=(CHUNKS,),
            in_specs=three_of(TOK) + three_of(KERNEL - 1) + three_of(KERNEL)
            + [whole((TOK, HEADS)), whole((8, HEADS))],
            out_specs=[
                whole((PAY, 128)),
                pl.BlockSpec((TOK, width), lambda i, p: (0, i)),
                whole((TOK, STATE)),
                whole((TOK, STATE)),
            ],
            scratch_shapes=[pltpu.VMEM((STATE, TOK), BF16)],
        ),
        out_shape=[
            jax.ShapeDtypeStruct((PAY, 128), BF16),
            jax.ShapeDtypeStruct((TOK, GCOLS), BF16),
            jax.ShapeDtypeStruct((TOK, STATE), BF16),
            jax.ShapeDtypeStruct((TOK, STATE), BF16),
        ],
        compiler_params=params(),
        cost_estimate=pl.CostEstimate(flops=10**8, bytes_accessed=3 * 10**6, transcendentals=0),
    )(pick, *([conv_input] * 3), *([edge] * 3), *([conv_weight] * 3), factor, decay)


def local_kernel(pick_ref, val_ref, wri_ref, rea_ref, cum_ref, cum_t_ref, step_t_ref, gain_ref, out_ref):
    base = pick_ref[0] * PER
    affinity = lax.dot_general(
        rea_ref[...], wri_ref[...], (((1,), (1,)), ((), ())), preferred_element_type=F32
    )
    cum = cum_ref[...]
    gain = jnp.broadcast_to(gain_ref[...], (8, HEADS))
    row = lax.broadcasted_iota(jnp.int32, (TOK, TOK), 0)
    col = lax.broadcasted_iota(jnp.int32, (TOK, TOK), 1)
    causal = row >= col
    first = col < HEAD_DIM
    for b in range(NB):
        scores = []
        for half in range(2):
            h = 2 * b + half
            at = jnp.take_along_axis(cum, jnp.full((TOK, TOK), base + h, jnp.int32), axis=1)
            span = jnp.where(causal, at - cum_t_ref[h : h + 1], -1e30)
            weight = jnp.exp(span) * step_t_ref[h : h + 1]
            scores.append((weight * affinity).astype(BF16))
        value = val_ref[:, b * 128 : (b + 1) * 128]
        zero = jnp.zeros_like(value)
        apart = jnp.concatenate([jnp.where(first, value, zero), jnp.where(first, zero, value)], 0)
        part = jnp.dot(jnp.concatenate(scores, 1), apart, preferred_element_type=F32)
        skip = lanes_of(gain, base, b, 8)[:1]
        out_ref[:, b * 128 : (b + 1) * 128] = part + skip * value.astype(F32)


def local(pick, value, writers, readers, cum, cum_t, step_t, skip_gain):
    whole = lambda shape: pl.BlockSpec(shape, lambda i, p: (0, 0))
    mine = pl.BlockSpec((PER, TOK), lambda i, p: (p[0], 0))
    return pl.pallas_call(
        local_kernel,
        grid_spec=pltpu.PrefetchScalarGridSpec(
            num_scalar_prefetch=1,
            grid=(1,),
            in_specs=[whole((TOK, GCOLS)), whole((TOK, STATE)), whole((TOK, STATE)), whole((TOK, HEADS)),
                      mine, mine, whole((1, HEADS))],
            out_specs=whole((TOK, GCOLS)),
        ),
        out_shape=jax.ShapeDtypeStruct((TOK, GCOLS), F32),
        compiler_params=params(),
        cost_estimate=pl.CostEstimate(flops=10**9, bytes_accessed=8 * 10**6, transcendentals=0),
    )(pick, value, writers, readers, cum, cum_t, step_t, skip_gain.reshape(1, HEADS))


def decays_of(ref):
    terms = ref[ROWS:].astype(F32)
    return terms[:NB] + terms[NB : 2 * NB] + terms[2 * NB :]


def total_kernel(x_ref, *refs):
    pays, out_ref = refs[:NX], refs[NX]
    for mine in range(NX):

        @pl.when(x_ref[0] == mine)
        def _(mine=mine):
            order = [pays[(mine - source) % NX] for source in range(NX)]
            decays = [decays_of(ref) for ref in order]
            product = decays[0]
            for decay in decays[1:]:
                product = product * decay
            hi, mid, low = three(product)
            for b in range(NB):
                rows = slice(b * STATE, (b + 1) * STATE)
                total = order[0][rows].astype(F32)
                for source in range(1, NX):
                    total = decays[source][b : b + 1] * total + order[source][rows].astype(F32)
                total = total.astype(BF16)
                tail = jnp.concatenate(
                    [hi[b : b + 1], mid[b : b + 1], low[b : b + 1], jnp.zeros((5, 128), F32)], 0
                ).astype(BF16)
                for part in range(STATE // SROWS):
                    at = b * (STATE // SROWS) + part
                    out_ref[at, :SROWS] = total[part * SROWS : (part + 1) * SROWS]
                    out_ref[at, SROWS:] = tail


SMEM = pl.BlockSpec(memory_space=pltpu.SMEM)
VMEM = pl.BlockSpec(memory_space=pltpu.VMEM)


def row_total(x, pays):
    return pl.pallas_call(
        total_kernel,
        in_specs=[SMEM] + [VMEM] * NX,
        out_specs=VMEM,
        out_shape=jax.ShapeDtypeStruct((SHARES, TROWS, 128), BF16),
        compiler_params=params(),
    )(x, *pays)


def row_of(rows_ref, at):
    block = rows_ref[at].astype(F32)
    tail = block[SROWS:]
    return block[:SROWS], tail[:1] + tail[1:2] + tail[2:3]


def group_kernel(rows_ref, out_ref):
    for y in range(NY):
        total, product = row_of(rows_ref, y * NZ)
        for z in range(1, NZ):
            state, decay = row_of(rows_ref, y * NZ + z)
            total = decay * total + state
            product = decay * product
        out_ref[y, :SROWS] = total
        out_ref[y, SROWS:] = jnp.broadcast_to(product, (8, 128))


def group_total(rows):
    return pl.pallas_call(
        group_kernel,
        in_specs=[VMEM],
        out_specs=VMEM,
        out_shape=jax.ShapeDtypeStruct((NY, TROWS, 128), F32),
        compiler_params=params(),
    )(rows)


def scan_kernel(core_ref, rows_ref, own_ref, other_ref, out_ref):
    first = core_ref[0] == 0
    entry = jnp.zeros((SROWS, 128), F32)
    for y in range(NY):
        own, other = own_ref[y], other_ref[y]
        one = jnp.where(first, own, other)
        two = jnp.where(first, other, own)
        middle = one[SROWS : SROWS + 1] * entry + one[:SROWS]
        state = jnp.where(first, entry, middle)
        entry = two[SROWS : SROWS + 1] * middle + two[:SROWS]
        for z in range(NZ):
            out_ref[y * NZ + z] = state.astype(BF16)
            if z < NZ - 1:
                term, decay = row_of(rows_ref, y * NZ + z)
                state = decay * state + term


def scan(core, rows, own, other):
    return pl.pallas_call(
        scan_kernel,
        in_specs=[SMEM] + [VMEM] * 3,
        out_specs=VMEM,
        out_shape=jax.ShapeDtypeStruct((SHARES, SROWS, 128), BF16),
        compiler_params=params(),
    )(core, rows, own, other)


def enter_kernel(x_ref, entry_ref, *refs):
    pays, outs = refs[:NX], refs[NX:]
    for mine in range(NX):

        @pl.when(x_ref[0] == mine)
        def _(mine=mine):
            decays = [decays_of(pays[(mine - source) % NX]) for source in range(NX - 1)]
            for b in range(NB):
                rows = slice(b * STATE, (b + 1) * STATE)
                state = entry_ref[rows].astype(F32)
                for target in range(NX):
                    outs[(target - mine) % NX][rows] = state.astype(BF16)
                    if target < NX - 1:
                        term = pays[(mine - target) % NX][rows].astype(F32)
                        state = decays[target][b : b + 1] * state + term


def enter(x, entry, pays):
    return pl.pallas_call(
        enter_kernel,
        in_specs=[SMEM] + [VMEM] * (NX + 1),
        out_specs=[VMEM] * NX,
        out_shape=[jax.ShapeDtypeStruct((ROWS, 128), BF16)] * NX,
        compiler_params=params(),
    )(x, entry, *pays)


def final_kernel(pick_ref, rea_ref, state_ref, growth_ref, part_ref, *refs):
    out_ref = refs[-1]
    step = pl.program_id(0)
    base = pick_ref[0] * PER
    growth = growth_ref[...]
    for pair in range(CB // 2):
        at = 2 * pair * STATE
        both = jnp.concatenate([state_ref[at : at + STATE], state_ref[at + STATE : at + 2 * STATE]], 1)
        carried = jnp.dot(rea_ref[...], both, preferred_element_type=F32)
        for half in range(2):
            b = 2 * pair + half
            cols = slice(b * 128, (b + 1) * 128)
            grow = lanes_of(growth, base, step * CB + b, TOK)
            result = part_ref[:, cols] + carried[:, half * 128 : (half + 1) * 128] * grow
            out_ref[:, cols] = result.astype(BF16)


def final(pick, readers, state, growth, part, so_far):
    width = CB * 128
    whole = lambda shape: pl.BlockSpec(shape, lambda i, p: (0, 0))
    extra = [] if so_far is None else [so_far]
    return pl.pallas_call(
        final_kernel,
        grid_spec=pltpu.PrefetchScalarGridSpec(
            num_scalar_prefetch=1,
            grid=(CHUNKS,),
            in_specs=[
                whole((TOK, STATE)),
                pl.BlockSpec((CB * STATE, 128), lambda i, p: (i, 0)),
                whole((TOK, HEADS)),
                pl.BlockSpec((TOK, width), lambda i, p: (0, i)),
            ]
            + [pl.BlockSpec(memory_space=pl.ANY)] * len(extra),
            out_specs=pl.BlockSpec((TOK, width), lambda i, p: (0, p[0] * CHUNKS + i)),
        ),
        out_shape=jax.ShapeDtypeStruct((TOK, HCOLS), BF16),
        input_output_aliases={5: 0} if extra else {},
        compiler_params=params(),
        cost_estimate=pl.CostEstimate(flops=10**8, bytes_accessed=2 * 10**6, transcendentals=0),
    )(pick, readers, state, growth, part, *extra)


def turned(value, steps):
    return lax.ppermute(value, "x", [(i, (i + steps) % NX) for i in range(NX)])


def body(conv_input, conv_weight, step_raw, decay_log, skip_gain):
    count = lax.axis_size(AXES)
    edge = lax.ppermute(conv_input[TOK - KERNEL + 1 :], AXES, [(i, i + 1) for i in range(count - 1)])
    x = lax.axis_index("x").reshape(1)
    core = lax.axis_index("core").reshape(1)
    picks = [(x + ahead) % NX for ahead in range(NX)]
    cum, factor, growth, cum_t, step_t, decay = prep(step_raw, decay_log)
    made, pays = {}, {}
    for ahead in (1, 3, 2, 0):
        made[ahead] = states(picks[ahead], conv_input, edge, conv_weight, factor, decay)
        pays[ahead] = turned(made[ahead][0], ahead) if ahead else made[ahead][0]
    pays = [pays[d] for d in range(NX)]
    parts = [
        local(picks[d], *made[d][1:], cum, cum_t, step_t, skip_gain) for d in range(NX)
    ]
    rows = lax.all_to_all(row_total(x, pays), ("y", "z"), 0, 0, tiled=True)
    own = group_total(rows)
    other = lax.ppermute(own, "core", [(0, 1), (1, 0)])
    entry = lax.all_to_all(scan(core, rows, own, other), ("y", "z"), 0, 0, tiled=True)
    entering = enter(x, entry.reshape(ROWS, 128), pays)
    out = None
    for ahead in (0, 1, 3, 2):
        state = turned(entering[ahead], ahead) if ahead else entering[0]
        d = (NX - ahead) % NX
        out = final(picks[d], made[d][3], state, growth, parts[d], out)
    return out


def solution(mesh):
    fine = Mesh(mesh.devices.reshape(NY, 2, NZ, NX), AXES)
    in_specs = (P(AXES, None), P(), P(AXES, None), P(), P())
    return jax.shard_map(body, mesh=fine, in_specs=in_specs, out_specs=P(AXES, None), check_vma=False)
```

time: 332 us -> 148 us (0.45)
  the two profiles are of different devices: /device:TPU:59 before, /device:TPU:22 now
where the time goes in v1:
time: 148 us
  blocking collectives  54.9 us (37%)
  starting transfers between devices  31.1 us (21%)
  waiting for transfers between devices  30.2 us (20%)
  Pallas kernels  22.5 us (15%)
  local copies, waits for them, and re-layouts  8.48 us (6%)
    all_to_all x1, blocking collectives, body(): rows = lax.all_to_all(row_total(x, pays), ('y', 'z'), 0, 0, tiled=True)  29.9 us
    ppermute x6, waiting for transfers between devices, turned(): return lax.ppermute(value, 'x', [(i, (i + steps) % NX) for i in range(NX)])  28.5 us
    ppermute x6, starting transfers between devices, turned(): return lax.ppermute(value, 'x', [(i, (i + steps) % NX) for i in range(NX)])  25 us
    all_to_all x1, blocking collectives, body(): lax.all_to_all(scan(core, rows, own, other), ('y', 'z'), 0, 0, tiled=True)  24.9 us
    pallas_call x4, Pallas kernels, states(): pl.pallas_call(state_kernel, grid_spec=pltpu.PrefetchScalarGridSpec(num_s...  9.22 us
    pallas_call x4, Pallas kernels, final(): pl.pallas_call(final_kernel, grid_spec=pltpu.PrefetchScalarGridSpec(num_s...  7.86 us
    unnamed x42, local copies, waits for them, and re-layouts  7.53 us
    ppermute x1, starting transfers between devices, body(): lax.ppermute(conv_input[TOK - KERNEL + 1:], AXES, [(i, i + 1) for i in ra...  4.2 us
  transfers between devices with their start and end apart: 8, of which 5 were waited for; matrix products, arithmetic and copies ran while one was open for 0% of the time, Pallas kernels for 12%

profile of v1, /device:TPU:22, one launch (start us, length us, event | category | flops | bytes accessed | tf_op | source)
XLA Modules:
  0.0 147.7 jit_solution(16720109154129995079)
XLA Ops:
  0.0 0.9 slice.3
  1.0 4.2 %collective-permute-start = (bf16[3,9216]{1,0:T(4,128)(2,1)S(1)}, bf16[3,9216]{1,0:T(4,128)(2,1)S(1)}, u32[]{:S(2)}, u32[]{:S(2)}) collective-permute-start(bf16[3,9216]{1,0:T(4,128)(2,1)S(1)} %slice.3), channel_id=1, source_target_pairs={{0,1},{1,2},{2,3},{3,4},{4,5},{5,6},{6,7},{7,8},{8,9},{9,10},{10,1... | collective-permute-start | bytes 165896 | tf_op jit(solution)/shard_map/ppermute | solution.py:383
  5.2 0.0 copy-start.4
  5.2 0.8 copy-done.4
  6.0 0.7 copy-done.5
  6.7 0.1 shard_map.55
  6.8 0.4 collective-permute-done.ev.ew.er
  7.2 1.7 %copy-done = bf16[128,9216]{1,0:T(8,128)(2,1)S(1)} copy-done((bf16[128,9216]{1,0:T(8,128)(2,1)S(1)}, bf16[128,9216]{1,0:T(8,128)(2,1)}, u32[]{:S(2)}) %copy-start) | copy-done | bytes 2359320
  8.9 0.9 copy-done.2
  9.8 2.3 %shard_map.58 = (bf16[2096,128]{1,0:T(8,128)(2,1)S(1)}, bf16[128,2048]{1,0:T(8,128)(2,1)S(1)}, bf16[128,128]{1,0:T(8,128)(2,1)S(1)}, bf16[128,128]{1,0:T(8,128)(2,1)S(1)}) custom-call(s32[1]{0:T(128)S(6)} %select_n.21.pick_ref, bf16[128,9216]{1,0:T(8,128)(2,1)S(1)} %copy-done, bf16[128,9216]{1,0:T(8,128)(2,1)S(1)} %copy-done, bf16[128,9216]{1,0:T(8,128)(2,1)S(1)} %copy-done, ...), custom_call_target="tpu_custom_call" | custom-call | flops 100000000 | bytes 3000000 | tf_op jit(solution)/shard_map/pallas_call | solution.py:137
  12.1 0.0 copy-start.6
  12.1 0.0 copy-start.1
  12.1 0.0 copy-start.3
  12.1 10.9 %collective-permute-start.1 = (bf16[2096,128]{1,0:T(8,128)(2,1)S(1)}, bf16[2096,128]{1,0:T(8,128)(2,1)S(1)}, u32[]{:S(2)}, u32[]{:S(2)}) collective-permute-start(bf16[2096,128]{1,0:T(8,128)(2,1)S(1)} %get-tuple-element.35), channel_id=1, source_target_pairs={{0,1},{1,2},{2,3},{3,0},{4,5},{5,6},{6,7},{7,4},{8,9},{9,10},{10,1... | collective-permute-start | bytes 1609736 | tf_op jit(solution)/shard_map/ppermute | solution.py:378
  23.0 2.3 %shard_map.59 = (bf16[2096,128]{1,0:T(8,128)(2,1)S(1)}, bf16[128,2048]{1,0:T(8,128)(2,1)S(1)}, bf16[128,128]{1,0:T(8,128)(2,1)S(1)}, bf16[128,128]{1,0:T(8,128)(2,1)S(1)}) custom-call(s32[1]{0:T(128)S(6)} %select_n.22.pick_ref, bf16[128,9216]{1,0:T(8,128)(2,1)S(1)} %copy-done, bf16[128,9216]{1,0:T(8,128)(2,1)S(1)} %copy-done, bf16[128,9216]{1,0:T(8,128)(2,1)S(1)} %copy-done, ...), custom_call_target="tpu_custom_call" | custom-call | flops 100000000 | bytes 3000000 | tf_op jit(solution)/shard_map/pallas_call | solution.py:137
  25.3 0.0 copy-done.6
  25.3 0.0 copy-start.10
  25.3 0.8 copy-done.10
  26.1 0.6 copy-done.16
  26.7 1.9 %collective-permute-start.3 = (bf16[2096,128]{1,0:T(8,128)(2,1)S(1)}, bf16[2096,128]{1,0:T(8,128)(2,1)S(1)}, u32[]{:S(2)}, u32[]{:S(2)}) collective-permute-start(bf16[2096,128]{1,0:T(8,128)(2,1)S(1)} %get-tuple-element.37), channel_id=1, source_target_pairs={{0,3},{1,0},{2,1},{3,2},{4,7},{5,4},{6,5},{7,6},{8,11},{9,8},{10,9... | collective-permute-start | bytes 1609736 | tf_op jit(solution)/shard_map/ppermute | solution.py:378
  28.7 0.0 copy-done.1
  28.7 0.0 copy-done.3
  28.7 2.3 %shard_map.56 = (bf16[2096,128]{1,0:T(8,128)(2,1)S(1)}, bf16[128,2048]{1,0:T(8,128)(2,1)S(1)}, bf16[128,128]{1,0:T(8,128)(2,1)S(1)}, bf16[128,128]{1,0:T(8,128)(2,1)S(1)}) custom-call(s32[1]{0:T(128)S(6)} %select_n.19.pick_ref, bf16[128,9216]{1,0:T(8,128)(2,1)S(1)} %copy-done.1, bf16[128,9216]{1,0:T(8,128)(2,1)S(1)} %copy-done.1, ...), custom_call_target="tpu_custom_call" | custom-call | flops 100000000 | bytes 3000000 | tf_op jit(solution)/shard_map/pallas_call | solution.py:137
  31.0 0.0 copy-start.8
  31.0 0.8 copy-done.8
  31.8 0.6 copy-done.14
  32.4 3.4 %collective-permute-start.2 = (bf16[2096,128]{1,0:T(8,128)(2,1)S(1)}, bf16[2096,128]{1,0:T(8,128)(2,1)S(1)}, u32[]{:S(2)}, u32[]{:S(2)}) collective-permute-start(bf16[2096,128]{1,0:T(8,128)(2,1)S(1)} %get-tuple-element.36), channel_id=1, source_target_pairs={{0,2},{1,3},{2,0},{3,1},{4,6},{5,7},{6,4},{7,5},{8,10},{9,11},{10,... | collective-permute-start | bytes 1609736 | tf_op jit(solution)/shard_map/ppermute | solution.py:378
  35.8 2.3 %shard_map.57 = (bf16[2096,128]{1,0:T(8,128)(2,1)S(1)}, bf16[128,2048]{1,0:T(8,128)(2,1)S(1)}, bf16[128,128]{1,0:T(8,128)(2,1)S(1)}, bf16[128,128]{1,0:T(8,128)(2,1)S(1)}) custom-call(s32[1]{0:T(128)S(6)} %select_n.20.pick_ref, bf16[128,9216]{1,0:T(8,128)(2,1)S(1)} %copy-done.1, bf16[128,9216]{1,0:T(8,128)(2,1)S(1)} %copy-done.1, ...), custom_call_target="tpu_custom_call" | custom-call | flops 100000000 | bytes 3000000 | tf_op jit(solution)/shard_map/pallas_call | solution.py:137
  38.1 0.0 copy-start.18
  38.1 0.6 copy-done.18
  38.7 0.0 collective-permute-done.1.refs_1_
  38.7 17.2 %collective-permute-done.3.refs_3_ = bf16[2096,128]{1,0:T(8,128)(2,1)S(1)} collective-permute-done((bf16[2096,128]{1,0:T(8,128)(2,1)S(1)}, bf16[2096,128]{1,0:T(8,128)(2,1)S(1)}, u32[]{:S(2)}, u32[]{:S(2)}) %collective-permute-start.3) | collective-permute-done | bytes 536608 | tf_op jit(solution)/shard_map/ppermute | solution.py:378
  55.9 0.0 collective-permute-done.2.refs_2_
  55.9 0.4 shard_map.60
  56.3 29.9 %all_to_all.10.rows_ref = bf16[64,40,128]{2,1,0:T(8,128)(2,1)S(1)} all-to-all(bf16[64,40,128]{2,1,0:T(8,128)(2,1)S(1)} %shard_map.60), channel_id=1, replica_groups=mesh['y'=8,'core'=2,'z'=8,'x'=4] {'y','z'}, dimensions={0} | all-to-all | bytes 1310720 | tf_op jit(solution)/shard_map/all_to_all | solution.py:396
  86.3 0.2 shard_map.61.own_ref
  86.5 0.0 copy-done.12
  86.5 1.9 %collective-permute-start.4 = (f32[8,40,128]{2,1,0:T(8,128)S(1)}, f32[8,40,128]{2,1,0:T(8,128)S(1)}, u32[]{:S(2)}, u32[]{:S(2)}) collective-permute-start(f32[8,40,128]{2,1,0:T(8,128)S(1)} %shard_map.61.own_ref), channel_id=1, source_target_pairs={{0,32},{32,0},{1,33},{33,1},{2,34},{34,2},{3,35},{35,3},{4,36},{36... | collective-permute-start | bytes 491528 | tf_op jit(solution)/shard_map/ppermute | solution.py:398
  88.4 1.4 collective-permute-done.4.other_ref
  89.8 0.2 shard_map.62
  89.9 0.0 copy-start.13
  90.0 0.0 copy-start.19
  90.0 0.0 copy-start.20
  90.0 24.9 %all_to_all.11 = bf16[64,32,128]{2,1,0:T(8,128)(2,1)S(1)} all-to-all(bf16[64,32,128]{2,1,0:T(8,128)(2,1)S(1)} %shard_map.62), channel_id=1, replica_groups=mesh['y'=8,'core'=2,'z'=8,'x'=4] {'y','z'}, dimensions={0} | all-to-all | bytes 1048576 | tf_op jit(solution)/shard_map/all_to_all | solution.py:399
  114.9 0.4 shard_map.63
  115.4 0.0 copy-start.11
  115.4 0.0 copy-start.17
  115.4 2.1 %collective-permute-start.7 = (bf16[2048,128]{1,0:T(8,128)(2,1)S(1)}, bf16[2048,128]{1,0:T(8,128)(2,1)S(1)}, u32[]{:S(2)}, u32[]{:S(2)}) collective-permute-start(bf16[2048,128]{1,0:T(8,128)(2,1)S(1)} %get-tuple-element.50), channel_id=1, source_target_pairs={{0,1},{1,2},{2,3},{3,0},{4,5},{5,6},{6,7},{7,4},{8,9},{9,10},{10,1... | collective-permute-start | bytes 1572872 | tf_op jit(solution)/shard_map/ppermute | solution.py:378
  117.5 3.9 %collective-permute-start.6 = (bf16[2048,128]{1,0:T(8,128)(2,1)S(1)}, bf16[2048,128]{1,0:T(8,128)(2,1)S(1)}, u32[]{:S(2)}, u32[]{:S(2)}) collective-permute-start(bf16[2048,128]{1,0:T(8,128)(2,1)S(1)} %get-tuple-element.46), channel_id=1, source_target_pairs={{0,3},{1,0},{2,1},{3,2},{4,7},{5,4},{6,5},{7,6},{8,11},{9,8},{10,9... | collective-permute-start | bytes 1572872 | tf_op jit(solution)/shard_map/ppermute | solution.py:378
  121.4 2.9 %collective-permute-start.5 = (bf16[2048,128]{1,0:T(8,128)(2,1)S(1)}, bf16[2048,128]{1,0:T(8,128)(2,1)S(1)}, u32[]{:S(2)}, u32[]{:S(2)}) collective-permute-start(bf16[2048,128]{1,0:T(8,128)(2,1)S(1)} %get-tuple-element.38), channel_id=1, source_target_pairs={{0,2},{1,3},{2,0},{3,1},{4,6},{5,7},{6,4},{7,5},{8,10},{9,11},{10,... | collective-permute-start | bytes 1572872 | tf_op jit(solution)/shard_map/ppermute | solution.py:378
  124.3 1.0 shard_map.67.part_ref
  125.3 0.0 copy-start.7
  125.3 1.0 shard_map.66.part_ref
  126.4 0.0 copy-start.9
  126.4 1.0 shard_map.65.part_ref
  127.4 0.0 copy-done.9
  127.4 1.0 shard_map.64.part_ref
  128.5 2.0 %shard_map.68.refs_0_ = bf16[128,8192]{1,0:T(8,128)(2,1)} custom-call(s32[1]{0:T(128)S(6)} %select_n.20.pick_ref, bf16[128,128]{1,0:T(8,128)(2,1)S(1)} %get-tuple-element.53.rea_ref, bf16[2048,128]{1,0:T(8,128)(2,1)S(1)} %get-tuple-element.54.state_ref, f32[128,128]{1,0:T(8,128)S(1)} %get-tuple-element.39.growth_ref, f32[128,2048]{1,0:T(8,128)S(1)} %shard_map.67.part_ref), custom_call_target="tpu_custom_call" | custom-call | flops 100000000 | bytes 2000000 | tf_op jit(solution)/shard_map/pallas_call | solution.py:356
  130.5 1.8 %collective-permute-done.7.state_ref = bf16[2048,128]{1,0:T(8,128)(2,1)S(1)} collective-permute-done((bf16[2048,128]{1,0:T(8,128)(2,1)S(1)}, bf16[2048,128]{1,0:T(8,128)(2,1)S(1)}, u32[]{:S(2)}, u32[]{:S(2)}) %collective-permute-start.7) | collective-permute-done | bytes 524320 | tf_op jit(solution)/shard_map/ppermute | solution.py:378
  132.3 2.0 %shard_map.69.refs_0_ = bf16[128,8192]{1,0:T(8,128)(2,1)} custom-call(s32[1]{0:T(128)S(6)} %select_n.22.pick_ref, bf16[128,128]{1,0:T(8,128)(2,1)S(1)} %get-tuple-element.49.rea_ref, bf16[2048,128]{1,0:T(8,128)(2,1)S(1)} %collective-permute-done.7.state_ref, f32[128,128]{1,0:T(8,128)S(1)} %get-tuple-element.39.growth_ref, ...), custom_call_target="tpu_custom_call", output_to_operand_aliasing={{}: (5, {})} | custom-call | flops 100000000 | bytes 2000000 | tf_op jit(solution)/shard_map/pallas_call | solution.py:356
  134.2 9.5 %collective-permute-done.6.state_ref = bf16[2048,128]{1,0:T(8,128)(2,1)S(1)} collective-permute-done((bf16[2048,128]{1,0:T(8,128)(2,1)S(1)}, bf16[2048,128]{1,0:T(8,128)(2,1)S(1)}, u32[]{:S(2)}, u32[]{:S(2)}) %collective-permute-start.6) | collective-permute-done | bytes 524320 | tf_op jit(solution)/shard_map/ppermute | solution.py:378
  143.8 2.0 %shard_map.70.refs_0_ = bf16[128,8192]{1,0:T(8,128)(2,1)} custom-call(s32[1]{0:T(128)S(6)} %select_n.21.pick_ref, bf16[128,128]{1,0:T(8,128)(2,1)S(1)} %get-tuple-element.45.rea_ref, bf16[2048,128]{1,0:T(8,128)(2,1)S(1)} %collective-permute-done.6.state_ref, f32[128,128]{1,0:T(8,128)S(1)} %get-tuple-element.39.growth_ref, ...), custom_call_target="tpu_custom_call", output_to_operand_aliasing={{}: (5, {})} | custom-call | flops 100000000 | bytes 2000000 | tf_op jit(solution)/shard_map/pallas_call | solution.py:356
  145.7 0.0 collective-permute-done.5.state_ref
  145.7 2.0 %shard_map.71 = bf16[128,8192]{1,0:T(8,128)(2,1)} custom-call(s32[1]{0:T(128)S(6)} %select_n.19.pick_ref, bf16[128,128]{1,0:T(8,128)(2,1)S(1)} %get-tuple-element.33.rea_ref, bf16[2048,128]{1,0:T(8,128)(2,1)S(1)} %collective-permute-done.5.state_ref, f32[128,128]{1,0:T(8,128)S(1)} %get-tuple-element.39.growth_ref, ...), custom_call_target="tpu_custom_call", output_to_operand_aliasing={{}: (5, {})} | custom-call | flops 100000000 | bytes 2000000 | tf_op jit(solution)/shard_map/pallas_call | solution.py:356
  (14 shorter events, 0.0 us)
Async XLA Ops:
  1.0 6.2 %collective-permute-start = (bf16[3,9216]{1,0:T(4,128)(2,1)S(1)}, bf16[3,9216]{1,0:T(4,128)(2,1)S(1)}, u32[]{:S(2)}, u32[]{:S(2)}) collective-permute-start(bf16[3,9216]{1,0:T(4,128)(2,1)S(1)} %slice.3), channel_id=1, source_target_pairs={{0,1},{1,2},{2,3},{3,4},{4,5},{5,6},{6,7},{7,8},{8,9},{9,10},{10,1... | collective-permute-start | bytes 165896 | tf_op jit(solution)/shard_map/ppermute | solution.py:383
  5.2 0.8 copy-start.4
  6.0 0.7 copy-start.5
  7.2 1.7 %copy-start = (bf16[128,9216]{1,0:T(8,128)(2,1)S(1)}, bf16[128,9216]{1,0:T(8,128)(2,1)}, u32[]{:S(2)}) copy-start(bf16[128,9216]{1,0:T(8,128)(2,1)} %xr.7) | copy-start | bytes 7077892
  8.9 0.9 copy-start.2
  12.1 13.3 %copy-start.6 = (bf16[128,2048]{1,0:T(8,128)(2,1)}, bf16[128,2048]{1,0:T(8,128)(2,1)S(1)}, u32[]{:S(2)}) copy-start(bf16[128,2048]{1,0:T(8,128)(2,1)S(1)} %get-tuple-element.47.val_ref) | copy-start | bytes 1572868
  12.1 16.6 %copy-start.1 = (bf16[128,9216]{1,0:T(8,128)(2,1)S(1)}, bf16[128,9216]{1,0:T(8,128)(2,1)}, u32[]{:S(2)}) copy-start(bf16[128,9216]{1,0:T(8,128)(2,1)} %xr.7) | copy-start | bytes 7077892
  12.1 16.6 %copy-start.3 = (f32[4,9216]{1,0:T(4,128)S(1)}, f32[4,9216]{1,0:T(4,128)}, u32[]{:S(2)}) copy-start(f32[4,9216]{1,0:T(4,128)} %wr.7) | copy-start | bytes 442372
  12.1 26.6 %collective-permute-start.1 = (bf16[2096,128]{1,0:T(8,128)(2,1)S(1)}, bf16[2096,128]{1,0:T(8,128)(2,1)S(1)}, u32[]{:S(2)}, u32[]{:S(2)}) collective-permute-start(bf16[2096,128]{1,0:T(8,128)(2,1)S(1)} %get-tuple-element.35), channel_id=1, source_target_pairs={{0,1},{1,2},{2,3},{3,0},{4,5},{5,6},{6,7},{7,4},{8,9},{9,10},{10,1... | collective-permute-start | bytes 1609736 | tf_op jit(solution)/shard_map/ppermute | solution.py:378
  25.3 0.8 copy-start.10
  26.1 0.6 copy-start.16
  26.7 29.2 %collective-permute-start.3 = (bf16[2096,128]{1,0:T(8,128)(2,1)S(1)}, bf16[2096,128]{1,0:T(8,128)(2,1)S(1)}, u32[]{:S(2)}, u32[]{:S(2)}) collective-permute-start(bf16[2096,128]{1,0:T(8,128)(2,1)S(1)} %get-tuple-element.37), channel_id=1, source_target_pairs={{0,3},{1,0},{2,1},{3,2},{4,7},{5,4},{6,5},{7,6},{8,11},{9,8},{10,9... | collective-permute-start | bytes 1609736 | tf_op jit(solution)/shard_map/ppermute | solution.py:378
  31.0 0.8 copy-start.8
  31.8 0.6 copy-start.14
  32.4 23.5 %collective-permute-start.2 = (bf16[2096,128]{1,0:T(8,128)(2,1)S(1)}, bf16[2096,128]{1,0:T(8,128)(2,1)S(1)}, u32[]{:S(2)}, u32[]{:S(2)}) collective-permute-start(bf16[2096,128]{1,0:T(8,128)(2,1)S(1)} %get-tuple-element.36), channel_id=1, source_target_pairs={{0,2},{1,3},{2,0},{3,1},{4,6},{5,7},{6,4},{7,5},{8,10},{9,11},{10,... | collective-permute-start | bytes 1609736 | tf_op jit(solution)/shard_map/ppermute | solution.py:378
  38.1 0.6 copy-start.18
  38.7 47.7 %copy-start.12 = (bf16[128,2048]{1,0:T(8,128)(2,1)}, bf16[128,2048]{1,0:T(8,128)(2,1)S(1)}, u32[]{:S(2)}) copy-start(bf16[128,2048]{1,0:T(8,128)(2,1)S(1)} %get-tuple-element.55.val_ref) | copy-start | bytes 1572868
  86.5 3.3 %collective-permute-start.4 = (f32[8,40,128]{2,1,0:T(8,128)S(1)}, f32[8,40,128]{2,1,0:T(8,128)S(1)}, u32[]{:S(2)}, u32[]{:S(2)}) collective-permute-start(f32[8,40,128]{2,1,0:T(8,128)S(1)} %shard_map.61.own_ref), channel_id=1, source_target_pairs={{0,32},{32,0},{1,33},{33,1},{2,34},{34,2},{3,35},{35,3},{4,36},{36... | collective-permute-start | bytes 491528 | tf_op jit(solution)/shard_map/ppermute | solution.py:398
  89.9 34.3 %copy-start.13 = (bf16[128,2048]{1,0:T(8,128)(2,1)S(1)}, bf16[128,2048]{1,0:T(8,128)(2,1)}, u32[]{:S(2)}) copy-start(bf16[128,2048]{1,0:T(8,128)(2,1)} %copy-done.12) | copy-start | bytes 1572868
  90.0 34.3 %copy-start.19 = (bf16[128,128]{1,0:T(8,128)(2,1)S(1)}, bf16[128,128]{1,0:T(8,128)(2,1)}, u32[]{:S(2)}) copy-start(bf16[128,128]{1,0:T(8,128)(2,1)} %copy-done.18) | copy-start | bytes 98308
  90.0 34.3 %copy-start.20 = (f32[128]{0:T(128)S(1)}, f32[128]{0:T(128)}, u32[]{:S(2)}) copy-start(f32[128]{0:T(128)} %param.9) | copy-start | bytes 1540
  115.4 9.9 %copy-start.11 = (bf16[128,2048]{1,0:T(8,128)(2,1)S(1)}, bf16[128,2048]{1,0:T(8,128)(2,1)}, u32[]{:S(2)}) copy-start(bf16[128,2048]{1,0:T(8,128)(2,1)} %copy-done.10) | copy-start | bytes 1572868
  115.4 9.9 %copy-start.17 = (bf16[128,128]{1,0:T(8,128)(2,1)S(1)}, bf16[128,128]{1,0:T(8,128)(2,1)}, u32[]{:S(2)}) copy-start(bf16[128,128]{1,0:T(8,128)(2,1)} %copy-done.16) | copy-start | bytes 98308
  115.4 16.9 %collective-permute-start.7 = (bf16[2048,128]{1,0:T(8,128)(2,1)S(1)}, bf16[2048,128]{1,0:T(8,128)(2,1)S(1)}, u32[]{:S(2)}, u32[]{:S(2)}) collective-permute-start(bf16[2048,128]{1,0:T(8,128)(2,1)S(1)} %get-tuple-element.50), channel_id=1, source_target_pairs={{0,1},{1,2},{2,3},{3,0},{4,5},{5,6},{6,7},{7,4},{8,9},{9,10},{10,1... | collective-permute-start | bytes 1572872 | tf_op jit(solution)/shard_map/ppermute | solution.py:378
  117.5 26.3 %collective-permute-start.6 = (bf16[2048,128]{1,0:T(8,128)(2,1)S(1)}, bf16[2048,128]{1,0:T(8,128)(2,1)S(1)}, u32[]{:S(2)}, u32[]{:S(2)}) collective-permute-start(bf16[2048,128]{1,0:T(8,128)(2,1)S(1)} %get-tuple-element.46), channel_id=1, source_target_pairs={{0,3},{1,0},{2,1},{3,2},{4,7},{5,4},{6,5},{7,6},{8,11},{9,8},{10,9... | collective-permute-start | bytes 1572872 | tf_op jit(solution)/shard_map/ppermute | solution.py:378
  121.4 24.3 %collective-permute-start.5 = (bf16[2048,128]{1,0:T(8,128)(2,1)S(1)}, bf16[2048,128]{1,0:T(8,128)(2,1)S(1)}, u32[]{:S(2)}, u32[]{:S(2)}) collective-permute-start(bf16[2048,128]{1,0:T(8,128)(2,1)S(1)} %get-tuple-element.38), channel_id=1, source_target_pairs={{0,2},{1,3},{2,0},{3,1},{4,6},{5,7},{6,4},{7,5},{8,10},{9,11},{10,... | collective-permute-start | bytes 1572872 | tf_op jit(solution)/shard_map/ppermute | solution.py:378
  125.3 1.1 copy-start.7
  126.4 1.1 copy-start.9
  126.4 1.1 copy-start.15

commit v2 on v1

v2 whole, which is shorter than its diff:
```python
import functools

import jax
import jax.numpy as jnp
from jax import lax
from jax.experimental import pallas as pl
from jax.experimental.pallas import tpu as pltpu
from jax.sharding import Mesh, PartitionSpec as P

HEADS = 128
HEAD_DIM = 64
STATE = 128
GROUPS = 4
KERNEL = 4
TOK = 128
PER = HEADS // GROUPS
GCOLS = PER * HEAD_DIM
NB = GCOLS // 128
HCOLS = HEADS * HEAD_DIM
ROWS = NB * STATE
PAY = ROWS + 3 * NB
SHARES = 64
SROWS = ROWS // SHARES
TROWS = SROWS + 8
NX, NY, NZ = 4, 8, 8
F32 = jnp.float32
BF16 = jnp.bfloat16
LIMIT = 12 * 1024 * 1024
PREP_LIMIT = 12 * 1024 * 1024
AXES = ("y", "core", "z", "x")
SMEM = pl.BlockSpec(memory_space=pltpu.SMEM)
VMEM = pl.BlockSpec(memory_space=pltpu.VMEM)
HBM = pl.BlockSpec(memory_space=pltpu.HBM)
ANY = pl.BlockSpec(memory_space=pl.ANY)


def params(limit=LIMIT):
    return pltpu.CompilerParams(vmem_limit_bytes=limit)


def three(v):
    hi = v.astype(BF16).astype(F32)
    mid = (v - hi).astype(BF16).astype(F32)
    low = (v - hi - mid).astype(BF16).astype(F32)
    return hi, mid, low


def lanes_of(per_head, base, block, rows):
    lane = lax.broadcasted_iota(jnp.int32, (rows, 128), 1)
    pick = base + 2 * block + lane // HEAD_DIM
    return jnp.take_along_axis(per_head, pick, axis=1)


def prep_kernel(
    x_hbm, raw_hbm, log_hbm,
    x_ref, edge_ref, cum_ref, factor_ref, growth_ref, cum_t_ref, step_t_ref, decay_ref,
    raw_ref, log_ref, sems,
):
    raw_copy = pltpu.make_async_copy(raw_hbm, raw_ref, sems.at[0])
    log_copy = pltpu.make_async_copy(log_hbm, log_ref, sems.at[1])
    copy = pltpu.make_async_copy(x_hbm, x_ref, sems.at[2])
    raw_copy.start()
    log_copy.start()
    copy.start()
    raw_copy.wait()
    log_copy.wait()
    raw = raw_ref[...]
    step = jnp.maximum(raw, 0.0) + jnp.log1p(jnp.exp(-jnp.abs(raw)))
    cum = -jnp.exp(log_ref[...]) * step
    row = lax.broadcasted_iota(jnp.int32, (TOK, HEADS), 0)
    shift = 1
    while shift < TOK:
        cum = cum + jnp.where(row >= shift, pltpu.roll(cum, shift, 0), 0.0)
        shift *= 2
    last = cum[TOK - 1 :, :]
    cum_ref[...] = cum
    factor_ref[...] = jnp.exp(last - cum) * step
    growth_ref[...] = jnp.exp(cum)
    cum_t_ref[...] = cum.T
    step_t_ref[...] = step.T
    decay_ref[...] = jnp.broadcast_to(jnp.exp(last), (8, HEADS))
    copy.wait()
    edge_ref[...] = x_ref[TOK - 16 :, :].astype(F32)[16 - KERNEL + 1 :].astype(BF16)


def prep(conv_input, step_raw, decay_log):
    square = jax.ShapeDtypeStruct((TOK, HEADS), F32)
    channels = conv_input.shape[1]
    return pl.pallas_call(
        prep_kernel,
        in_specs=[HBM] * 3,
        out_specs=[VMEM] * 8,
        out_shape=[
            jax.ShapeDtypeStruct((TOK, channels), BF16),
            jax.ShapeDtypeStruct((KERNEL - 1, channels), BF16),
            *[square] * 5,
            jax.ShapeDtypeStruct((8, HEADS), F32),
        ],
        scratch_shapes=[
            pltpu.VMEM((TOK, HEADS), F32), pltpu.VMEM((1, HEADS), F32), pltpu.SemaphoreType.DMA((3,))
        ],
        compiler_params=params(PREP_LIMIT),
    )(conv_input, step_raw, decay_log.reshape(1, HEADS))


def convolve(x_ref, edge_ref, w_ref, at):
    cols = pl.ds(pl.multiple_of(at, 128), 128)
    x = x_ref[:, cols].astype(F32)
    edge = edge_ref[:, cols].astype(F32)
    weight = w_ref[:, cols]
    wide = jnp.concatenate([jnp.zeros((8 - KERNEL + 1, 128), F32), edge, x], 0)
    out = None
    for tap in range(KERNEL):
        first = 8 - KERNEL + 1 + tap
        term = wide[first : first + TOK] * weight[tap : tap + 1]
        out = term if out is None else out + term
    return out.astype(BF16)


def group_of(x_ref, ahead):
    return jnp.bitwise_and(x_ref[0] + ahead, NX - 1)


def state_kernel(
    ahead, x_ref, in_ref, edge_ref, w_ref, factor_ref, decay_ref, pay_ref, val_ref, wri_ref, rea_ref
):
    group = group_of(x_ref, ahead)
    base = group * PER
    writers = convolve(in_ref, edge_ref, w_ref, HCOLS + group * STATE)
    wri_ref[...] = writers
    turned_writers = writers.astype(F32).T.astype(BF16)
    rows = [lanes_of(decay_ref[...], base, b, 8)[:1] for b in range(NB)]
    for at, term in enumerate(three(jnp.concatenate(rows, 0))):
        pay_ref[ROWS + at * NB : ROWS + (at + 1) * NB] = term.astype(BF16)
    factor = factor_ref[...]
    for pair in range(NB // 2):
        weighted = []
        for b in (2 * pair, 2 * pair + 1):
            value = convolve(in_ref, edge_ref, w_ref, group * GCOLS + b * 128)
            val_ref[:, b * 128 : (b + 1) * 128] = value
            fac = lanes_of(factor, base, b, TOK)
            weighted.append((value.astype(F32) * fac).astype(BF16))
        state = jnp.dot(turned_writers, jnp.concatenate(weighted, 1), preferred_element_type=F32)
        for half in range(2):
            b = 2 * pair + half
            pay_ref[b * STATE : (b + 1) * STATE] = state[:, half * 128 : (half + 1) * 128].astype(BF16)
    rea_ref[...] = convolve(in_ref, edge_ref, w_ref, HCOLS + (GROUPS + group) * STATE)


def states(ahead, x, conv_input, edge, conv_weight, factor, decay):
    return pl.pallas_call(
        functools.partial(state_kernel, ahead),
        in_specs=[SMEM] + [VMEM] * 5,
        out_specs=[VMEM] * 4,
        out_shape=[
            jax.ShapeDtypeStruct((PAY, 128), BF16),
            jax.ShapeDtypeStruct((TOK, GCOLS), BF16),
            jax.ShapeDtypeStruct((TOK, STATE), BF16),
            jax.ShapeDtypeStruct((TOK, STATE), BF16),
        ],
        compiler_params=params(),
        cost_estimate=pl.CostEstimate(flops=10**8, bytes_accessed=3 * 10**6, transcendentals=0),
    )(x, conv_input, edge, conv_weight, factor, decay)


def local_kernel(
    ahead, x_ref, val_ref, wri_ref, rea_ref, cum_ref, cum_t_ref, step_t_ref, gain_ref, out_ref
):
    base = group_of(x_ref, ahead) * PER
    mine = pl.ds(pl.multiple_of(base, PER), PER)
    cum_t = cum_t_ref[mine]
    step_t = step_t_ref[mine]
    affinity = lax.dot_general(
        rea_ref[...], wri_ref[...], (((1,), (1,)), ((), ())), preferred_element_type=F32
    )
    cum = cum_ref[...]
    gain = jnp.broadcast_to(gain_ref[...], (8, HEADS))
    row = lax.broadcasted_iota(jnp.int32, (TOK, TOK), 0)
    col = lax.broadcasted_iota(jnp.int32, (TOK, TOK), 1)
    causal = row >= col
    first = col < HEAD_DIM
    for b in range(NB):
        scores = []
        for half in range(2):
            h = 2 * b + half
            at = jnp.take_along_axis(cum, jnp.full((TOK, TOK), base + h, jnp.int32), axis=1)
            span = jnp.where(causal, at - cum_t[h : h + 1], -1e30)
            weight = jnp.exp(span) * step_t[h : h + 1]
            scores.append((weight * affinity).astype(BF16))
        value = val_ref[:, b * 128 : (b + 1) * 128]
        zero = jnp.zeros_like(value)
        apart = jnp.concatenate([jnp.where(first, value, zero), jnp.where(first, zero, value)], 0)
        part = jnp.dot(jnp.concatenate(scores, 1), apart, preferred_element_type=F32)
        skip = lanes_of(gain, base, b, 8)[:1]
        out_ref[:, b * 128 : (b + 1) * 128] = part + skip * value.astype(F32)


def local(ahead, x, value, writers, readers, cum, cum_t, step_t, skip_gain):
    return pl.pallas_call(
        functools.partial(local_kernel, ahead),
        in_specs=[SMEM] + [VMEM] * 7,
        out_specs=VMEM,
        out_shape=jax.ShapeDtypeStruct((TOK, GCOLS), F32),
        compiler_params=params(),
        cost_estimate=pl.CostEstimate(flops=10**9, bytes_accessed=8 * 10**6, transcendentals=0),
    )(x, value, writers, readers, cum, cum_t, step_t, skip_gain.reshape(1, HEADS))


def decays_of(ref):
    terms = ref[ROWS:].astype(F32)
    return terms[:NB] + terms[NB : 2 * NB] + terms[2 * NB :]


def total_kernel(x_ref, *refs):
    pays, out_ref = refs[:NX], refs[NX]
    for mine in range(NX):

        @pl.when(x_ref[0] == mine)
        def _(mine=mine):
            order = [pays[(mine - source) % NX] for source in range(NX)]
            decays = [decays_of(ref) for ref in order]
            product = decays[0]
            for decay in decays[1:]:
                product = product * decay
            hi, mid, low = three(product)
            for b in range(NB):
                rows = slice(b * STATE, (b + 1) * STATE)
                total = order[0][rows].astype(F32)
                for source in range(1, NX):
                    total = decays[source][b : b + 1] * total + order[source][rows].astype(F32)
                total = total.astype(BF16)
                tail = jnp.concatenate(
                    [hi[b : b + 1], mid[b : b + 1], low[b : b + 1], jnp.zeros((5, 128), F32)], 0
                ).astype(BF16)
                for part in range(STATE // SROWS):
                    at = b * (STATE // SROWS) + part
                    out_ref[at, :SROWS] = total[part * SROWS : (part + 1) * SROWS]
                    out_ref[at, SROWS:] = tail


def row_total(x, pays):
    return pl.pallas_call(
        total_kernel,
        in_specs=[SMEM] + [VMEM] * NX,
        out_specs=VMEM,
        out_shape=jax.ShapeDtypeStruct((SHARES, TROWS, 128), BF16),
        compiler_params=params(),
    )(x, *pays)


def row_of(rows_ref, at):
    block = rows_ref[at].astype(F32)
    tail = block[SROWS:]
    return block[:SROWS], tail[:1] + tail[1:2] + tail[2:3]


def group_kernel(rows_ref, out_ref):
    for y in range(NY):
        total, product = row_of(rows_ref, y * NZ)
        for z in range(1, NZ):
            state, decay = row_of(rows_ref, y * NZ + z)
            total = decay * total + state
            product = decay * product
        out_ref[y, :SROWS] = total
        out_ref[y, SROWS:] = jnp.broadcast_to(product, (8, 128))


def group_total(rows):
    return pl.pallas_call(
        group_kernel,
        in_specs=[VMEM],
        out_specs=VMEM,
        out_shape=jax.ShapeDtypeStruct((NY, TROWS, 128), F32),
        compiler_params=params(),
    )(rows)


def scan_kernel(core_ref, rows_ref, own_ref, other_ref, out_ref):
    first = core_ref[0] == 0
    entry = jnp.zeros((SROWS, 128), F32)
    for y in range(NY):
        own, other = own_ref[y], other_ref[y]
        one = jnp.where(first, own, other)
        two = jnp.where(first, other, own)
        middle = one[SROWS : SROWS + 1] * entry + one[:SROWS]
        state = jnp.where(first, entry, middle)
        entry = two[SROWS : SROWS + 1] * middle + two[:SROWS]
        for z in range(NZ):
            out_ref[y * NZ + z] = state.astype(BF16)
            if z < NZ - 1:
                term, decay = row_of(rows_ref, y * NZ + z)
                state = decay * state + term


def scan(core, rows, own, other):
    return pl.pallas_call(
        scan_kernel,
        in_specs=[SMEM] + [VMEM] * 3,
        out_specs=VMEM,
        out_shape=jax.ShapeDtypeStruct((SHARES, SROWS, 128), BF16),
        compiler_params=params(),
    )(core, rows, own, other)


def enter_kernel(x_ref, entry_ref, *refs):
    pays, outs = refs[:NX], refs[NX:]
    for mine in range(NX):

        @pl.when(x_ref[0] == mine)
        def _(mine=mine):
            decays = [decays_of(pays[(mine - source) % NX]) for source in range(NX - 1)]
            for b in range(NB):
                rows = slice(b * STATE, (b + 1) * STATE)
                state = entry_ref[rows].astype(F32)
                for target in range(NX):
                    outs[(target - mine) % NX][rows] = state.astype(BF16)
                    if target < NX - 1:
                        term = pays[(mine - target) % NX][rows].astype(F32)
                        state = decays[target][b : b + 1] * state + term


def enter(x, entry, pays):
    return pl.pallas_call(
        enter_kernel,
        in_specs=[SMEM] + [VMEM] * (NX + 1),
        out_specs=[VMEM] * NX,
        out_shape=[jax.ShapeDtypeStruct((ROWS, 128), BF16)] * NX,
        compiler_params=params(),
    )(x, entry, *pays)


PIECES = 4


def final_kernel(ahead, x_ref, rea_ref, state_ref, growth_ref, part_ref, *refs):
    out_ref, buf, sems = refs[-3:]
    group = group_of(x_ref, ahead)
    growth = growth_ref[...]
    readers = rea_ref[...]
    copies = []
    for pair in range(NB // 2):
        at = 2 * pair * STATE
        both = jnp.concatenate([state_ref[at : at + STATE], state_ref[at + STATE : at + 2 * STATE]], 1)
        carried = jnp.dot(readers, both, preferred_element_type=F32)
        for half in range(2):
            b = 2 * pair + half
            cols = slice(b * 128, (b + 1) * 128)
            grow = lanes_of(growth, group * PER, b, TOK)
            result = part_ref[:, cols] + carried[:, half * 128 : (half + 1) * 128] * grow
            buf[:, cols] = result.astype(BF16)
        if (pair + 1) % (NB // 2 // PIECES) == 0:
            piece = len(copies)
            width = GCOLS // PIECES
            to = pl.multiple_of(group * GCOLS + piece * width, width)
            copies.append(
                pltpu.make_async_copy(
                    buf.at[:, pl.ds(piece * width, width)], out_ref.at[:, pl.ds(to, width)], sems.at[piece]
                )
            )
            copies[-1].start()
    for copy in copies:
        copy.wait()


def final(ahead, x, readers, state, growth, part, so_far):
    extra = [] if so_far is None else [so_far]
    return pl.pallas_call(
        functools.partial(final_kernel, ahead),
        in_specs=[SMEM] + [VMEM] * 4 + [ANY] * len(extra),
        out_specs=ANY,
        out_shape=jax.ShapeDtypeStruct((TOK, HCOLS), BF16),
        scratch_shapes=[pltpu.VMEM((TOK, GCOLS), BF16), pltpu.SemaphoreType.DMA((PIECES,))],
        input_output_aliases={5: 0} if extra else {},
        compiler_params=params(),
        cost_estimate=pl.CostEstimate(flops=10**8, bytes_accessed=2 * 10**6, transcendentals=0),
    )(x, readers, state, growth, part, *extra)


def turned(value, steps):
    return lax.ppermute(value, "x", [(i, (i + steps) % NX) for i in range(NX)])


def body(conv_input, conv_weight, step_raw, decay_log, skip_gain):
    count = lax.axis_size(AXES)
    x = lax.axis_index("x").reshape(1)
    core = lax.axis_index("core").reshape(1)
    held, edge, cum, factor, growth, cum_t, step_t, decay = prep(conv_input, step_raw, decay_log)
    edge = lax.ppermute(edge, AXES, [(i, i + 1) for i in range(count - 1)])
    made, pays = {}, {}
    for ahead in (2, 1, 3, 0):
        made[ahead] = states(ahead, x, held, edge, conv_weight, factor, decay)
        pays[ahead] = turned(made[ahead][0], ahead) if ahead else made[ahead][0]
    parts = {d: local(d, x, *made[d][1:], cum, cum_t, step_t, skip_gain) for d in (2, 1, 3, 0)}
    pays, parts = lax.optimization_barrier((pays, parts))
    pays = [pays[d] for d in range(NX)]
    rows = lax.all_to_all(row_total(x, pays), ("y", "z"), 0, 0, tiled=True)
    own = group_total(rows)
    other = lax.ppermute(own, "core", [(0, 1), (1, 0)])
    entry = lax.all_to_all(scan(core, rows, own, other), ("y", "z"), 0, 0, tiled=True)
    entering = enter(x, entry.reshape(ROWS, 128), pays)
    out = None
    for ahead in (0, 2, 1, 3):
        state = turned(entering[ahead], ahead) if ahead else entering[0]
        d = (NX - ahead) % NX
        out = final(d, x, made[d][3], state, growth, parts[d], out)
    return out


def solution(mesh):
    fine = Mesh(mesh.devices.reshape(NY, 2, NZ, NX), AXES)
    in_specs = (P(AXES, None), P(), P(AXES, None), P(), P())
    return jax.shard_map(body, mesh=fine, in_specs=in_specs, out_specs=P(AXES, None), check_vma=False)
```

time: 148 us -> 145 us (0.980)
  the two profiles are of different devices: /device:TPU:22 before, /device:TPU:17 now
where the time goes in v2:
time: 145 us; the launch traced here: 144 us
  blocking collectives  52.1 us (36%)
  waiting for transfers between devices  44.5 us (31%)
  starting transfers between devices  23.8 us (16%)
  Pallas kernels  16.6 us (11%)
  local copies, waits for them, and re-layouts  6.86 us (5%)
    ppermute x6, waiting for transfers between devices, turned(): return lax.ppermute(value, 'x', [(i, (i + steps) % NX) for i in range(NX)])  31.2 us
    all_to_all x1, blocking collectives, body(): rows = lax.all_to_all(row_total(x, pays), ('y', 'z'), 0, 0, tiled=True)  29.3 us
    all_to_all x1, blocking collectives, body(): lax.all_to_all(scan(core, rows, own, other), ('y', 'z'), 0, 0, tiled=True)  22.9 us
    ppermute x6, starting transfers between devices, turned(): return lax.ppermute(value, 'x', [(i, (i + steps) % NX) for i in range(NX)])  15.9 us
    ppermute x1, waiting for transfers between devices, body(): edge = lax.ppermute(edge, AXES, [(i, i + 1) for i in range(count - 1)])  12.3 us
    unnamed x42, local copies, waits for them, and re-layouts  6.86 us
    pallas_call x4, Pallas kernels, states(): pl.pallas_call(functools.partial(state_kernel, ahead), in_specs=[SMEM] +...  6.03 us
    ppermute x1, starting transfers between devices, body(): other = lax.ppermute(own, 'core', [(0, 1), (1, 0)])  4.82 us
  transfers between devices with their start and end apart: 8, of which 6 were waited for; matrix products, arithmetic and copies ran while one was open for 0% of the time, Pallas kernels for 8%

profile of v2, /device:TPU:17, one launch (start us, length us, event | category | flops | bytes accessed | tf_op | source)
XLA Modules:
  0.0 144.4 jit_solution(4873199888039275024)
XLA Ops:
  0.0 1.7 %copy-done.1 = bf16[128,9216]{1,0:T(8,128)(2,1)S(1)} copy-done((bf16[128,9216]{1,0:T(8,128)(2,1)S(1)}, bf16[128,9216]{1,0:T(8,128)(2,1)}, u32[]{:S(2)}) %copy-start.1) | copy-done | bytes 2359320
  1.7 0.8 copy-done.16
  2.5 0.7 copy-done.17
  3.2 0.4 shard_map.55
  3.6 0.0 copy-start.18
  3.6 0.6 copy-done.18
  4.3 3.1 %collective-permute-start = (bf16[3,9216]{1,0:T(4,128)(2,1)S(1)}, bf16[3,9216]{1,0:T(4,128)(2,1)S(1)}, u32[]{:S(2)}, u32[]{:S(2)}) collective-permute-start(bf16[3,9216]{1,0:T(4,128)(2,1)S(1)} %get-tuple-element.42), channel_id=1, source_target_pairs={{0,1},{1,2},{2,3},{3,4},{4,5},{5,6},{6,7},{7,8},{8,9},{9,10},{10,1... | collective-permute-start | bytes 165896 | tf_op jit(solution)/shard_map/ppermute | solution.py:388
  7.4 12.3 %collective-permute-done.edge_ref = bf16[3,9216]{1,0:T(4,128)(2,1)S(1)} collective-permute-done((bf16[3,9216]{1,0:T(4,128)(2,1)S(1)}, bf16[3,9216]{1,0:T(4,128)(2,1)S(1)}, u32[]{:S(2)}, u32[]{:S(2)}) %collective-permute-start) | collective-permute-done | bytes 55328 | tf_op jit(solution)/shard_map/ppermute | solution.py:388
  19.7 0.0 copy-done
  19.7 1.5 %shard_map.59 = (bf16[2096,128]{1,0:T(8,128)(2,1)S(1)}, bf16[128,2048]{1,0:T(8,128)(2,1)S(1)}, bf16[128,128]{1,0:T(8,128)(2,1)S(1)}, bf16[128,128]{1,0:T(8,128)(2,1)S(1)}) custom-call(s32[1]{0:T(128)} %bitcast.x_ref, bf16[128,9216]{1,0:T(8,128)(2,1)S(1)} %get-tuple-element.41.in_ref, bf16[3,9216]{1,0:T(4,128)(2,1)S(1)} %collective-permute-done.edge_ref, ...), custom_call_target="tpu_custom_call" | custom-call | flops 100000000 | bytes 3000000 | tf_op jit(solution)/shard_map/pallas_call | solution.py:151
  21.2 1.9 %collective-permute-start.3 = (bf16[2096,128]{1,0:T(8,128)(2,1)S(1)}, bf16[2096,128]{1,0:T(8,128)(2,1)S(1)}, u32[]{:S(2)}, u32[]{:S(2)}) collective-permute-start(bf16[2096,128]{1,0:T(8,128)(2,1)S(1)} %get-tuple-element.49), channel_id=1, source_target_pairs={{0,3},{1,0},{2,1},{3,2},{4,7},{5,4},{6,5},{7,6},{8,11},{9,8},{10,9... | collective-permute-start | bytes 1609736 | tf_op jit(solution)/shard_map/ppermute | solution.py:380
  23.1 1.5 %shard_map.58 = (bf16[2096,128]{1,0:T(8,128)(2,1)S(1)}, bf16[128,2048]{1,0:T(8,128)(2,1)S(1)}, bf16[128,128]{1,0:T(8,128)(2,1)S(1)}, bf16[128,128]{1,0:T(8,128)(2,1)S(1)}) custom-call(s32[1]{0:T(128)} %bitcast.x_ref, bf16[128,9216]{1,0:T(8,128)(2,1)S(1)} %get-tuple-element.41.in_ref, bf16[3,9216]{1,0:T(4,128)(2,1)S(1)} %collective-permute-done.edge_ref, ...), custom_call_target="tpu_custom_call" | custom-call | flops 100000000 | bytes 3000000 | tf_op jit(solution)/shard_map/pallas_call | solution.py:151
  24.7 0.0 copy-start.19
  24.7 0.0 copy-start.20
  24.7 2.1 %collective-permute-start.2 = (bf16[2096,128]{1,0:T(8,128)(2,1)S(1)}, bf16[2096,128]{1,0:T(8,128)(2,1)S(1)}, u32[]{:S(2)}, u32[]{:S(2)}) collective-permute-start(bf16[2096,128]{1,0:T(8,128)(2,1)S(1)} %get-tuple-element.48), channel_id=1, source_target_pairs={{0,2},{1,3},{2,0},{3,1},{4,6},{5,7},{6,4},{7,5},{8,10},{9,11},{10,... | collective-permute-start | bytes 1609736 | tf_op jit(solution)/shard_map/ppermute | solution.py:380
  26.7 1.5 %shard_map.56 = (bf16[2096,128]{1,0:T(8,128)(2,1)S(1)}, bf16[128,2048]{1,0:T(8,128)(2,1)S(1)}, bf16[128,128]{1,0:T(8,128)(2,1)S(1)}, bf16[128,128]{1,0:T(8,128)(2,1)S(1)}) custom-call(s32[1]{0:T(128)} %bitcast.x_ref, bf16[128,9216]{1,0:T(8,128)(2,1)S(1)} %get-tuple-element.41.in_ref, bf16[3,9216]{1,0:T(4,128)(2,1)S(1)} %collective-permute-done.edge_ref, ...), custom_call_target="tpu_custom_call" | custom-call | flops 100000000 | bytes 3000000 | tf_op jit(solution)/shard_map/pallas_call | solution.py:151
  28.3 3.4 %collective-permute-start.1 = (bf16[2096,128]{1,0:T(8,128)(2,1)S(1)}, bf16[2096,128]{1,0:T(8,128)(2,1)S(1)}, u32[]{:S(2)}, u32[]{:S(2)}) collective-permute-start(bf16[2096,128]{1,0:T(8,128)(2,1)S(1)} %get-tuple-element.47), channel_id=1, source_target_pairs={{0,1},{1,2},{2,3},{3,0},{4,5},{5,6},{6,7},{7,4},{8,9},{9,10},{10,1... | collective-permute-start | bytes 1609736 | tf_op jit(solution)/shard_map/ppermute | solution.py:380
  31.6 1.5 %shard_map.57 = (bf16[2096,128]{1,0:T(8,128)(2,1)S(1)}, bf16[128,2048]{1,0:T(8,128)(2,1)S(1)}, bf16[128,128]{1,0:T(8,128)(2,1)S(1)}, bf16[128,128]{1,0:T(8,128)(2,1)S(1)}) custom-call(s32[1]{0:T(128)} %bitcast.x_ref, bf16[128,9216]{1,0:T(8,128)(2,1)S(1)} %get-tuple-element.41.in_ref, bf16[3,9216]{1,0:T(4,128)(2,1)S(1)} %collective-permute-done.edge_ref, ...), custom_call_target="tpu_custom_call" | custom-call | flops 100000000 | bytes 3000000 | tf_op jit(solution)/shard_map/pallas_call | solution.py:151
  33.1 0.0 copy-start.6
  33.2 0.0 copy-done.19
  33.2 0.0 copy-done.20
  33.2 1.1 shard_map.63.part_ref
  34.2 0.0 copy-start.8
  34.2 1.0 copy-done.8
  35.2 1.0 shard_map.62.part_ref
  36.3 0.0 copy-start.12
  36.3 1.0 copy-done.12
  37.3 1.1 shard_map.60.part_ref
  38.4 0.0 copy-start.14
  38.4 1.0 copy-done.14
  39.3 1.0 shard_map.61.part_ref
  40.4 0.0 copy-start.10
  40.4 0.0 collective-permute-done.3.refs_3_
  40.4 1.9 %collective-permute-done.2.refs_2_ = bf16[2096,128]{1,0:T(8,128)(2,1)S(1)} collective-permute-done((bf16[2096,128]{1,0:T(8,128)(2,1)S(1)}, bf16[2096,128]{1,0:T(8,128)(2,1)S(1)}, u32[]{:S(2)}, u32[]{:S(2)}) %collective-permute-start.2) | collective-permute-done | bytes 536608 | tf_op jit(solution)/shard_map/ppermute | solution.py:380
  42.3 11.6 %collective-permute-done.1.refs_1_ = bf16[2096,128]{1,0:T(8,128)(2,1)S(1)} collective-permute-done((bf16[2096,128]{1,0:T(8,128)(2,1)S(1)}, bf16[2096,128]{1,0:T(8,128)(2,1)S(1)}, u32[]{:S(2)}, u32[]{:S(2)}) %collective-permute-start.1) | collective-permute-done | bytes 536608 | tf_op jit(solution)/shard_map/ppermute | solution.py:380
  53.9 0.0 copy-done.6
  53.9 0.6 shard_map.64
  54.5 0.0 copy-done.10
  54.5 0.0 copy-start.7
  54.5 29.3 %all_to_all.10.rows_ref = bf16[64,40,128]{2,1,0:T(8,128)(2,1)S(1)} all-to-all(bf16[64,40,128]{2,1,0:T(8,128)(2,1)S(1)} %shard_map.64), channel_id=1, replica_groups=mesh['y'=8,'core'=2,'z'=8,'x'=4] {'y','z'}, dimensions={0} | all-to-all | bytes 1310720 | tf_op jit(solution)/shard_map/all_to_all | solution.py:396
  83.8 0.2 shard_map.65.own_ref
  83.9 0.0 copy-done.2
  83.9 0.0 copy-done.4
  84.0 4.8 %collective-permute-start.4 = (f32[8,40,128]{2,1,0:T(8,128)S(1)}, f32[8,40,128]{2,1,0:T(8,128)S(1)}, u32[]{:S(2)}, u32[]{:S(2)}) collective-permute-start(f32[8,40,128]{2,1,0:T(8,128)S(1)} %shard_map.65.own_ref), channel_id=1, source_target_pairs={{0,32},{32,0},{1,33},{33,1},{2,34},{34,2},{3,35},{35,3},{4,36},{36... | collective-permute-start | bytes 491528 | tf_op jit(solution)/shard_map/ppermute | solution.py:398
  88.8 0.0 copy-start.3
  88.8 0.0 copy-start.5
  88.8 1.0 collective-permute-done.4.other_ref
  89.8 0.2 shard_map.66
  90.0 0.0 copy-start.15
  90.0 22.9 %all_to_all.11 = bf16[64,32,128]{2,1,0:T(8,128)(2,1)S(1)} all-to-all(bf16[64,32,128]{2,1,0:T(8,128)(2,1)S(1)} %shard_map.66), channel_id=1, replica_groups=mesh['y'=8,'core'=2,'z'=8,'x'=4] {'y','z'}, dimensions={0} | all-to-all | bytes 1048576 | tf_op jit(solution)/shard_map/all_to_all | solution.py:399
  112.9 0.0 copy-done.7
  112.9 0.5 shard_map.67
  113.4 0.0 copy-start.13
  113.4 2.1 %collective-permute-start.7 = (bf16[2048,128]{1,0:T(8,128)(2,1)S(1)}, bf16[2048,128]{1,0:T(8,128)(2,1)S(1)}, u32[]{:S(2)}, u32[]{:S(2)}) collective-permute-start(bf16[2048,128]{1,0:T(8,128)(2,1)S(1)} %get-tuple-element.73), channel_id=1, source_target_pairs={{0,2},{1,3},{2,0},{3,1},{4,6},{5,7},{6,4},{7,5},{8,10},{9,11},{10,... | collective-permute-start | bytes 1572872 | tf_op jit(solution)/shard_map/ppermute | solution.py:380
  115.4 1.9 %collective-permute-start.6 = (bf16[2048,128]{1,0:T(8,128)(2,1)S(1)}, bf16[2048,128]{1,0:T(8,128)(2,1)S(1)}, u32[]{:S(2)}, u32[]{:S(2)}) collective-permute-start(bf16[2048,128]{1,0:T(8,128)(2,1)S(1)} %get-tuple-element.71), channel_id=1, source_target_pairs={{0,1},{1,2},{2,3},{3,0},{4,5},{5,6},{6,7},{7,4},{8,9},{9,10},{10,1... | collective-permute-start | bytes 1572872 | tf_op jit(solution)/shard_map/ppermute | solution.py:380
  117.4 4.6 %collective-permute-start.5 = (bf16[2048,128]{1,0:T(8,128)(2,1)S(1)}, bf16[2048,128]{1,0:T(8,128)(2,1)S(1)}, u32[]{:S(2)}, u32[]{:S(2)}) collective-permute-start(bf16[2048,128]{1,0:T(8,128)(2,1)S(1)} %get-tuple-element.68), channel_id=1, source_target_pairs={{0,3},{1,0},{2,1},{3,2},{4,7},{5,4},{6,5},{7,6},{8,11},{9,8},{10,9... | collective-permute-start | bytes 1572872 | tf_op jit(solution)/shard_map/ppermute | solution.py:380
  122.0 1.1 shard_map.68.refs_0_
  123.1 4.9 %collective-permute-done.7.state_ref = bf16[2048,128]{1,0:T(8,128)(2,1)S(1)} collective-permute-done((bf16[2048,128]{1,0:T(8,128)(2,1)S(1)}, bf16[2048,128]{1,0:T(8,128)(2,1)S(1)}, u32[]{:S(2)}, u32[]{:S(2)}) %collective-permute-start.7) | collective-permute-done | bytes 524320 | tf_op jit(solution)/shard_map/ppermute | solution.py:380
  128.0 1.1 shard_map.69.refs_0_
  129.1 0.0 copy-start.11
  129.1 12.9 %collective-permute-done.6.state_ref = bf16[2048,128]{1,0:T(8,128)(2,1)S(1)} collective-permute-done((bf16[2048,128]{1,0:T(8,128)(2,1)S(1)}, bf16[2048,128]{1,0:T(8,128)(2,1)S(1)}, u32[]{:S(2)}, u32[]{:S(2)}) %collective-permute-start.6) | collective-permute-done | bytes 524320 | tf_op jit(solution)/shard_map/ppermute | solution.py:380
  142.0 1.1 shard_map.70.refs_0_
  143.1 0.0 collective-permute-done.5.state_ref
  143.1 1.1 shard_map.71
  (13 shorter events, 0.0 us)
Async XLA Ops:
  0.0 19.7 %copy-start = (f32[4,9216]{1,0:T(4,128)S(1)}, f32[4,9216]{1,0:T(4,128)}, u32[]{:S(2)}) copy-start(f32[4,9216]{1,0:T(4,128)} %w_ref.7) | copy-start | bytes 442372
  0.0 1.7 %copy-start.1 = (bf16[128,9216]{1,0:T(8,128)(2,1)S(1)}, bf16[128,9216]{1,0:T(8,128)(2,1)}, u32[]{:S(2)}) copy-start(bf16[128,9216]{1,0:T(8,128)(2,1)} %x_hbm.1) | copy-start | bytes 7077892
  1.7 0.8 copy-start.16
  2.5 0.7 copy-start.17
  3.6 0.6 copy-start.18
  4.3 15.4 %collective-permute-start = (bf16[3,9216]{1,0:T(4,128)(2,1)S(1)}, bf16[3,9216]{1,0:T(4,128)(2,1)S(1)}, u32[]{:S(2)}, u32[]{:S(2)}) collective-permute-start(bf16[3,9216]{1,0:T(4,128)(2,1)S(1)} %get-tuple-element.42), channel_id=1, source_target_pairs={{0,1},{1,2},{2,3},{3,4},{4,5},{5,6},{6,7},{7,8},{8,9},{9,10},{10,1... | collective-permute-start | bytes 165896 | tf_op jit(solution)/shard_map/ppermute | solution.py:388
  21.2 19.2 %collective-permute-start.3 = (bf16[2096,128]{1,0:T(8,128)(2,1)S(1)}, bf16[2096,128]{1,0:T(8,128)(2,1)S(1)}, u32[]{:S(2)}, u32[]{:S(2)}) collective-permute-start(bf16[2096,128]{1,0:T(8,128)(2,1)S(1)} %get-tuple-element.49), channel_id=1, source_target_pairs={{0,3},{1,0},{2,1},{3,2},{4,7},{5,4},{6,5},{7,6},{8,11},{9,8},{10,9... | collective-permute-start | bytes 1609736 | tf_op jit(solution)/shard_map/ppermute | solution.py:380
  24.7 8.5 %copy-start.19 = (f32[128,128]{1,0:T(8,128)S(1)}, f32[128,128]{1,0:T(8,128)}, u32[]{:S(2)}) copy-start(f32[128,128]{1,0:T(8,128)} %copy-done.18) | copy-start | bytes 196612
  24.7 8.5 %copy-start.20 = (f32[128]{0:T(128)S(1)}, f32[128]{0:T(128)}, u32[]{:S(2)}) copy-start(f32[128]{0:T(128)} %param.9) | copy-start | bytes 1540
  24.7 17.6 %collective-permute-start.2 = (bf16[2096,128]{1,0:T(8,128)(2,1)S(1)}, bf16[2096,128]{1,0:T(8,128)(2,1)S(1)}, u32[]{:S(2)}, u32[]{:S(2)}) collective-permute-start(bf16[2096,128]{1,0:T(8,128)(2,1)S(1)} %get-tuple-element.48), channel_id=1, source_target_pairs={{0,2},{1,3},{2,0},{3,1},{4,6},{5,7},{6,4},{7,5},{8,10},{9,11},{10,... | collective-permute-start | bytes 1609736 | tf_op jit(solution)/shard_map/ppermute | solution.py:380
  28.3 25.6 %collective-permute-start.1 = (bf16[2096,128]{1,0:T(8,128)(2,1)S(1)}, bf16[2096,128]{1,0:T(8,128)(2,1)S(1)}, u32[]{:S(2)}, u32[]{:S(2)}) collective-permute-start(bf16[2096,128]{1,0:T(8,128)(2,1)S(1)} %get-tuple-element.47), channel_id=1, source_target_pairs={{0,1},{1,2},{2,3},{3,0},{4,5},{5,6},{6,7},{7,4},{8,9},{9,10},{10,1... | collective-permute-start | bytes 1609736 | tf_op jit(solution)/shard_map/ppermute | solution.py:380
  33.1 20.7 %copy-start.6 = (bf16[2096,128]{1,0:T(8,128)(2,1)}, bf16[2096,128]{1,0:T(8,128)(2,1)S(1)}, u32[]{:S(2)}) copy-start(bf16[2096,128]{1,0:T(8,128)(2,1)S(1)} %get-tuple-element.64.refs_0_) | copy-start | bytes 1609732
  34.2 1.0 copy-start.8
  36.3 1.0 copy-start.12
  38.4 1.0 copy-start.14
  40.4 14.1 %copy-start.10 = (f32[128,2048]{1,0:T(8,128)}, f32[128,2048]{1,0:T(8,128)S(1)}, u32[]{:S(2)}) copy-start(f32[128,2048]{1,0:T(8,128)S(1)} %shard_map.61.part_ref) | copy-start | bytes 3145732
  42.3 41.7 %copy-start.2 = (bf16[2096,128]{1,0:T(8,128)(2,1)}, bf16[2096,128]{1,0:T(8,128)(2,1)S(1)}, u32[]{:S(2)}) copy-start(bf16[2096,128]{1,0:T(8,128)(2,1)S(1)} %collective-permute-done.2.refs_2_) | copy-start | bytes 1609732
  53.9 30.1 %copy-start.4 = (bf16[2096,128]{1,0:T(8,128)(2,1)}, bf16[2096,128]{1,0:T(8,128)(2,1)S(1)}, u32[]{:S(2)}) copy-start(bf16[2096,128]{1,0:T(8,128)(2,1)S(1)} %collective-permute-done.1.refs_1_) | copy-start | bytes 1609732
  54.5 58.4 %copy-start.7 = (bf16[2096,128]{1,0:T(8,128)(2,1)S(1)}, bf16[2096,128]{1,0:T(8,128)(2,1)}, u32[]{:S(2)}) copy-start(bf16[2096,128]{1,0:T(8,128)(2,1)} %copy-done.6) | copy-start | bytes 1609732
  84.0 5.8 %collective-permute-start.4 = (f32[8,40,128]{2,1,0:T(8,128)S(1)}, f32[8,40,128]{2,1,0:T(8,128)S(1)}, u32[]{:S(2)}, u32[]{:S(2)}) collective-permute-start(f32[8,40,128]{2,1,0:T(8,128)S(1)} %shard_map.65.own_ref), channel_id=1, source_target_pairs={{0,32},{32,0},{1,33},{33,1},{2,34},{34,2},{3,35},{35,3},{4,36},{36... | collective-permute-start | bytes 491528 | tf_op jit(solution)/shard_map/ppermute | solution.py:398
  88.8 24.1 %copy-start.3 = (bf16[2096,128]{1,0:T(8,128)(2,1)S(1)}, bf16[2096,128]{1,0:T(8,128)(2,1)}, u32[]{:S(2)}) copy-start(bf16[2096,128]{1,0:T(8,128)(2,1)} %copy-done.2) | copy-start | bytes 1609732
  88.8 24.1 %copy-start.5 = (bf16[2096,128]{1,0:T(8,128)(2,1)S(1)}, bf16[2096,128]{1,0:T(8,128)(2,1)}, u32[]{:S(2)}) copy-start(bf16[2096,128]{1,0:T(8,128)(2,1)} %copy-done.4) | copy-start | bytes 1609732
  90.0 32.0 %copy-start.15 = (f32[128,2048]{1,0:T(8,128)S(1)}, f32[128,2048]{1,0:T(8,128)}, u32[]{:S(2)}) copy-start(f32[128,2048]{1,0:T(8,128)} %copy-done.14) | copy-start | bytes 3145732
  113.4 14.6 %copy-start.13 = (f32[128,2048]{1,0:T(8,128)S(1)}, f32[128,2048]{1,0:T(8,128)}, u32[]{:S(2)}) copy-start(f32[128,2048]{1,0:T(8,128)} %copy-done.12) | copy-start | bytes 3145732
  113.4 14.6 %collective-permute-start.7 = (bf16[2048,128]{1,0:T(8,128)(2,1)S(1)}, bf16[2048,128]{1,0:T(8,128)(2,1)S(1)}, u32[]{:S(2)}, u32[]{:S(2)}) collective-permute-start(bf16[2048,128]{1,0:T(8,128)(2,1)S(1)} %get-tuple-element.73), channel_id=1, source_target_pairs={{0,2},{1,3},{2,0},{3,1},{4,6},{5,7},{6,4},{7,5},{8,10},{9,11},{10,... | collective-permute-start | bytes 1572872 | tf_op jit(solution)/shard_map/ppermute | solution.py:380
  115.4 26.6 %collective-permute-start.6 = (bf16[2048,128]{1,0:T(8,128)(2,1)S(1)}, bf16[2048,128]{1,0:T(8,128)(2,1)S(1)}, u32[]{:S(2)}, u32[]{:S(2)}) collective-permute-start(bf16[2048,128]{1,0:T(8,128)(2,1)S(1)} %get-tuple-element.71), channel_id=1, source_target_pairs={{0,1},{1,2},{2,3},{3,0},{4,5},{5,6},{6,7},{7,4},{8,9},{9,10},{10,1... | collective-permute-start | bytes 1572872 | tf_op jit(solution)/shard_map/ppermute | solution.py:380
  117.4 25.8 %collective-permute-start.5 = (bf16[2048,128]{1,0:T(8,128)(2,1)S(1)}, bf16[2048,128]{1,0:T(8,128)(2,1)S(1)}, u32[]{:S(2)}, u32[]{:S(2)}) collective-permute-start(bf16[2048,128]{1,0:T(8,128)(2,1)S(1)} %get-tuple-element.68), channel_id=1, source_target_pairs={{0,3},{1,0},{2,1},{3,2},{4,7},{5,4},{6,5},{7,6},{8,11},{9,8},{10,9... | collective-permute-start | bytes 1572872 | tf_op jit(solution)/shard_map/ppermute | solution.py:380
  123.1 18.9 %copy-start.9 = (f32[128,2048]{1,0:T(8,128)S(1)}, f32[128,2048]{1,0:T(8,128)}, u32[]{:S(2)}) copy-start(f32[128,2048]{1,0:T(8,128)} %copy-done.8) | copy-start | bytes 3145732
  129.1 14.0 %copy-start.11 = (f32[128,2048]{1,0:T(8,128)S(1)}, f32[128,2048]{1,0:T(8,128)}, u32[]{:S(2)}) copy-start(f32[128,2048]{1,0:T(8,128)} %copy-done.10) | copy-start | bytes 3145732

commit v3 on v2

v3 whole, which is shorter than its diff:
```python
import functools

import jax
import jax.numpy as jnp
from jax import lax
from jax.experimental import pallas as pl
from jax.experimental.pallas import tpu as pltpu
from jax.sharding import Mesh, PartitionSpec as P

HEADS = 128
HEAD_DIM = 64
STATE = 128
GROUPS = 4
KERNEL = 4
TOK = 128
PER = HEADS // GROUPS
GCOLS = PER * HEAD_DIM
NB = GCOLS // 128
HCOLS = HEADS * HEAD_DIM
PARTS = 1
NBP = NB // PARTS
PCOLS = NBP * 128
ROWS = NBP * STATE
TAIL = max(32, 3 * NBP)
PAY = ROWS + TAIL
SHARES = 64
SROWS = ROWS // SHARES
TROWS = SROWS + 8
NX, NY, NZ = 4, 8, 8
F32 = jnp.float32
BF16 = jnp.bfloat16
LIMIT = 12 * 1024 * 1024
AXES = ("y", "core", "z", "x")
SENT = (2, 1, 3, 0)
SMEM = pl.BlockSpec(memory_space=pltpu.SMEM)
VMEM = pl.BlockSpec(memory_space=pltpu.VMEM)
ANY = pl.BlockSpec(memory_space=pl.ANY)


def params():
    return pltpu.CompilerParams(vmem_limit_bytes=LIMIT)


def three(v):
    hi = v.astype(BF16).astype(F32)
    mid = (v - hi).astype(BF16).astype(F32)
    low = (v - hi - mid).astype(BF16).astype(F32)
    return hi, mid, low


def lanes_of(per_head, base, block, rows):
    lane = lax.broadcasted_iota(jnp.int32, (rows, 128), 1)
    pick = base + 2 * block + lane // HEAD_DIM
    return jnp.take_along_axis(per_head, pick, axis=1)


def prep_kernel(x_hbm, raw_ref, log_ref, x_ref, early_ref, late_ref, sem):
    copy = pltpu.make_async_copy(x_hbm, x_ref, sem)
    copy.start()
    raw = raw_ref[...]
    step = jnp.maximum(raw, 0.0) + jnp.log1p(jnp.exp(-jnp.abs(raw)))
    cum = -jnp.exp(log_ref[...]) * step
    row = lax.broadcasted_iota(jnp.int32, (TOK, HEADS), 0)
    shift = 1
    while shift < TOK:
        cum = cum + jnp.where(row >= shift, pltpu.roll(cum, shift, 0), 0.0)
        shift *= 2
    last = cum[TOK - 1 :, :]
    early_ref[:TOK] = jnp.exp(last - cum) * step
    early_ref[TOK:] = jnp.broadcast_to(jnp.exp(last), (8, HEADS))
    late_ref[:TOK] = cum
    late_ref[TOK : 2 * TOK] = cum.T
    late_ref[2 * TOK :] = step.T
    copy.wait()


def prep(conv_input, step_raw, decay_log):
    channels = conv_input.shape[1]
    return pl.pallas_call(
        prep_kernel,
        in_specs=[ANY, VMEM, VMEM],
        out_specs=[VMEM] * 3,
        out_shape=[
            jax.ShapeDtypeStruct((TOK, channels), BF16),
            jax.ShapeDtypeStruct((TOK + 8, HEADS), F32),
            jax.ShapeDtypeStruct((2 * TOK + HEADS, HEADS), F32),
        ],
        scratch_shapes=[pltpu.SemaphoreType.DMA],
        compiler_params=params(),
        cost_estimate=pl.CostEstimate(flops=0, bytes_accessed=0, transcendentals=0),
    )(conv_input, step_raw, decay_log.reshape(1, HEADS))


def convolve(x_ref, edge_ref, w_ref, at):
    cols = pl.ds(pl.multiple_of(at, 128), 128)
    x = x_ref[:, cols].astype(F32)
    edge = edge_ref[:, cols].astype(F32)
    weight = w_ref[:, cols]
    wide = jnp.concatenate([jnp.zeros((8 - KERNEL + 1, 128), F32), edge, x], 0)
    out = None
    for tap in range(KERNEL):
        first = 8 - KERNEL + 1 + tap
        term = wide[first : first + TOK] * weight[tap : tap + 1]
        out = term if out is None else out + term
    return out.astype(BF16)


def group_of(x_ref, ahead):
    return jnp.bitwise_and(x_ref[0] + ahead, NX - 1)


def state_kernel(ahead, part, x_ref, in_ref, edge_ref, w_ref, early_ref, pay_ref):
    group = group_of(x_ref, ahead)
    base = group * PER + part * 2 * NBP
    writers = convolve(in_ref, edge_ref, w_ref, HCOLS + group * STATE).astype(F32).T.astype(BF16)
    decay = early_ref[TOK:]
    rows = [lanes_of(decay, base, b, 8)[:1] for b in range(NBP)]
    terms = three(jnp.concatenate(rows, 0))
    if TAIL > 3 * NBP:
        terms += (jnp.zeros((TAIL - 3 * NBP, 128), F32),)
    pay_ref[ROWS:] = jnp.concatenate(terms, 0).astype(BF16)
    factor = early_ref[:TOK]
    for pair in range(NBP // 2):
        weighted = []
        for b in (2 * pair, 2 * pair + 1):
            value = convolve(in_ref, edge_ref, w_ref, group * GCOLS + part * PCOLS + b * 128)
            fac = lanes_of(factor, base, b, TOK)
            weighted.append((value.astype(F32) * fac).astype(BF16))
        state = jnp.dot(writers, jnp.concatenate(weighted, 1), preferred_element_type=F32)
        for half in range(2):
            b = 2 * pair + half
            pay_ref[b * STATE : (b + 1) * STATE] = state[:, half * 128 : (half + 1) * 128].astype(BF16)


def states(ahead, part, *args):
    return pl.pallas_call(
        functools.partial(state_kernel, ahead, part),
        in_specs=[SMEM] + [VMEM] * 4,
        out_specs=VMEM,
        out_shape=jax.ShapeDtypeStruct((PAY, 128), BF16),
        compiler_params=params(),
        cost_estimate=pl.CostEstimate(flops=10**8, bytes_accessed=3 * 10**6, transcendentals=0),
    )(*args)


def decays_of(ref):
    terms = ref[ROWS:].astype(F32)
    return terms[:NBP] + terms[NBP : 2 * NBP] + terms[2 * NBP : 3 * NBP]


def total_kernel(x_ref, *refs):
    pays, out_ref = refs[:NX], refs[NX]
    for mine in range(NX):

        @pl.when(x_ref[0] == mine)
        def _(mine=mine):
            order = [pays[SENT.index((mine - source) % NX)] for source in range(NX)]
            decays = [decays_of(ref) for ref in order]
            product = decays[0]
            for decay in decays[1:]:
                product = product * decay
            hi, mid, low = three(product)
            for b in range(NBP):
                rows = slice(b * STATE, (b + 1) * STATE)
                total = order[0][rows].astype(F32)
                for source in range(1, NX):
                    total = decays[source][b : b + 1] * total + order[source][rows].astype(F32)
                tail = jnp.concatenate(
                    [hi[b : b + 1], mid[b : b + 1], low[b : b + 1], jnp.zeros((5, 128), F32)], 0
                )
                for part in range(STATE // SROWS):
                    share = jnp.concatenate([total[part * SROWS : (part + 1) * SROWS], tail], 0)
                    out_ref[b * (STATE // SROWS) + part] = share.astype(BF16)


def row_total(x, pays):
    return pl.pallas_call(
        total_kernel,
        in_specs=[SMEM] + [VMEM] * NX,
        out_specs=VMEM,
        out_shape=jax.ShapeDtypeStruct((SHARES, TROWS, 128), BF16),
        compiler_params=params(),
    )(x, *pays)


def row_of(rows_ref, at):
    block = rows_ref[at].astype(F32)
    tail = block[SROWS:]
    return block[:SROWS], tail[:1] + tail[1:2] + tail[2:3]


def group_kernel(rows_ref, out_ref):
    for y in range(NY):
        total, product = row_of(rows_ref, y * NZ)
        for z in range(1, NZ):
            state, decay = row_of(rows_ref, y * NZ + z)
            total = decay * total + state
            product = decay * product
        out_ref[y, :SROWS] = total
        out_ref[y, SROWS:] = jnp.broadcast_to(product, (8, 128))


def group_total(rows):
    return pl.pallas_call(
        group_kernel,
        in_specs=[VMEM],
        out_specs=VMEM,
        out_shape=jax.ShapeDtypeStruct((NY, TROWS, 128), F32),
        compiler_params=params(),
    )(rows)


def scan_kernel(core_ref, rows_ref, own_ref, other_ref, out_ref):
    first = core_ref[0] == 0
    entry = jnp.zeros((SROWS, 128), F32)
    for y in range(NY):
        own, other = own_ref[y], other_ref[y]
        one = jnp.where(first, own, other)
        two = jnp.where(first, other, own)
        middle = one[SROWS : SROWS + 1] * entry + one[:SROWS]
        state = jnp.where(first, entry, middle)
        entry = two[SROWS : SROWS + 1] * middle + two[:SROWS]
        for z in range(NZ):
            out_ref[y * NZ + z] = state.astype(BF16)
            if z < NZ - 1:
                term, decay = row_of(rows_ref, y * NZ + z)
                state = decay * state + term


def scan(core, rows, own, other):
    return pl.pallas_call(
        scan_kernel,
        in_specs=[SMEM] + [VMEM] * 3,
        out_specs=VMEM,
        out_shape=jax.ShapeDtypeStruct((SHARES, SROWS, 128), BF16),
        compiler_params=params(),
    )(core, rows, own, other)


def enter_kernel(x_ref, entry_ref, *refs):
    pays, outs = refs[:NX], refs[NX:]
    for mine in range(NX):

        @pl.when(x_ref[0] == mine)
        def _(mine=mine):
            decays = [decays_of(pays[SENT.index((mine - source) % NX)]) for source in range(NX - 1)]
            for b in range(NBP):
                rows = slice(b * STATE, (b + 1) * STATE)
                state = entry_ref[rows].astype(F32)
                for target in range(NX):
                    outs[(target - mine) % NX][rows] = state.astype(BF16)
                    if target < NX - 1:
                        term = pays[SENT.index((mine - target) % NX)][rows].astype(F32)
                        state = decays[target][b : b + 1] * state + term


def enter(x, entry, pays):
    return pl.pallas_call(
        enter_kernel,
        in_specs=[SMEM] + [VMEM] * (NX + 1),
        out_specs=[VMEM] * NX,
        out_shape=[jax.ShapeDtypeStruct((ROWS, 128), BF16)] * NX,
        compiler_params=params(),
    )(x, entry, *pays)


def local_kernel(ahead, x_ref, in_ref, edge_ref, w_ref, late_ref, gain_ref, out_ref, rea_ref):
    group = group_of(x_ref, ahead)
    base = group * PER
    writers = convolve(in_ref, edge_ref, w_ref, HCOLS + group * STATE)
    readers = convolve(in_ref, edge_ref, w_ref, HCOLS + (GROUPS + group) * STATE)
    rea_ref[...] = readers
    affinity = lax.dot_general(
        readers, writers, (((1,), (1,)), ((), ())), preferred_element_type=F32
    )
    cum = late_ref[:TOK]
    cum_t = late_ref[pl.ds(pl.multiple_of(TOK + base, PER), PER)]
    step_t = late_ref[pl.ds(pl.multiple_of(TOK + HEADS + base, PER), PER)]
    gain = jnp.broadcast_to(gain_ref[...], (8, HEADS))
    row = lax.broadcasted_iota(jnp.int32, (TOK, TOK), 0)
    col = lax.broadcasted_iota(jnp.int32, (TOK, TOK), 1)
    causal = row >= col
    first = col < HEAD_DIM
    for b in range(NB):
        scores = []
        for h in (2 * b, 2 * b + 1):
            here = jnp.take_along_axis(cum, jnp.full((TOK, TOK), base + h, jnp.int32), axis=1)
            span = jnp.where(causal, here - cum_t[h : h + 1], -1e30)
            weight = jnp.exp(span) * step_t[h : h + 1]
            scores.append((weight * affinity).astype(BF16))
        value = convolve(in_ref, edge_ref, w_ref, group * GCOLS + b * 128)
        zero = jnp.zeros_like(value)
        apart = jnp.concatenate([jnp.where(first, value, zero), jnp.where(first, zero, value)], 0)
        local = jnp.dot(jnp.concatenate(scores, 1), apart, preferred_element_type=F32)
        skip = lanes_of(gain, base, b, 8)[:1]
        out_ref[:, b * 128 : (b + 1) * 128] = local + skip * value.astype(F32)


def local(ahead, *args):
    return pl.pallas_call(
        functools.partial(local_kernel, ahead),
        in_specs=[SMEM] + [VMEM] * 5,
        out_specs=[VMEM] * 2,
        out_shape=[
            jax.ShapeDtypeStruct((TOK, GCOLS), F32),
            jax.ShapeDtypeStruct((TOK, STATE), BF16),
        ],
        compiler_params=params(),
        cost_estimate=pl.CostEstimate(flops=10**9, bytes_accessed=8 * 10**6, transcendentals=0),
    )(*args)


PIECES = 4


def final_kernel(ahead, x_ref, rea_ref, late_ref, part_ref, state_ref, *refs):
    out_ref, buf, sems = refs[-3:]
    group = group_of(x_ref, ahead)
    base = group * PER
    growth = jnp.exp(late_ref[:TOK])
    readers = rea_ref[...]
    width = GCOLS // PIECES
    copies = []
    for pair in range(NB // 2):
        at = 2 * pair * STATE
        both = jnp.concatenate([state_ref[at : at + STATE], state_ref[at + STATE : at + 2 * STATE]], 1)
        carried = jnp.dot(readers, both, preferred_element_type=F32)
        for half in range(2):
            b = 2 * pair + half
            cols = slice(b * 128, (b + 1) * 128)
            grow = lanes_of(growth, base, b, TOK)
            result = part_ref[:, cols] + carried[:, half * 128 : (half + 1) * 128] * grow
            buf[:, cols] = result.astype(BF16)
        if (pair + 1) % (NB // 2 // PIECES) == 0:
            piece = len(copies)
            to = pl.multiple_of(group * GCOLS + piece * width, width)
            copies.append(
                pltpu.make_async_copy(
                    buf.at[:, pl.ds(piece * width, width)], out_ref.at[:, pl.ds(to, width)], sems.at[piece]
                )
            )
            copies[-1].start()
    for copy in copies:
        copy.wait()


def final(ahead, so_far, *args):
    extra = [] if so_far is None else [so_far]
    return pl.pallas_call(
        functools.partial(final_kernel, ahead),
        in_specs=[SMEM] + [VMEM] * 4 + [ANY] * len(extra),
        out_specs=ANY,
        out_shape=jax.ShapeDtypeStruct((TOK, HCOLS), BF16),
        scratch_shapes=[pltpu.VMEM((TOK, GCOLS), BF16), pltpu.SemaphoreType.DMA((PIECES,))],
        input_output_aliases={5: 0} if extra else {},
        compiler_params=params(),
        cost_estimate=pl.CostEstimate(flops=10**8, bytes_accessed=2 * 10**6, transcendentals=0),
    )(*args, *extra)


def turned(value, steps):
    return lax.ppermute(value, "x", [(i, (i + steps) % NX) for i in range(NX)])


def body(conv_input, conv_weight, step_raw, decay_log, skip_gain):
    count = lax.axis_size(AXES)
    x = lax.axis_index("x").reshape(1)
    core = lax.axis_index("core").reshape(1)
    edge = lax.ppermute(conv_input[TOK - KERNEL + 1 :], AXES, [(i, i + 1) for i in range(count - 1)])
    held, early, late = prep(conv_input, step_raw, decay_log)
    pays = {}
    for ahead in SENT:
        state = states(ahead, 0, x, held, edge, conv_weight, early)
        pays[ahead] = turned(state, ahead) if ahead else state
    pays = [pays[d] for d in SENT]
    rows = lax.all_to_all(row_total(x, pays), ("y", "z"), 0, 0, tiled=True)
    own = group_total(rows)
    other = lax.ppermute(own, "core", [(0, 1), (1, 0)])
    entry = lax.all_to_all(scan(core, rows, own, other), ("y", "z"), 0, 0, tiled=True)
    entering = enter(x, entry.reshape(ROWS, 128), pays)
    late, entering = lax.optimization_barrier((late, entering))
    gain = skip_gain.reshape(1, HEADS)
    out = None
    for ahead in (0, 2, 1, 3):
        state = turned(entering[ahead], ahead) if ahead else entering[0]
        d = (NX - ahead) % NX
        part, readers = local(d, x, conv_input, edge, conv_weight, late, gain)
        out = final(d, out, x, readers, late, part, state)
    return out


def solution(mesh):
    fine = Mesh(mesh.devices.reshape(NY, 2, NZ, NX), AXES)
    in_specs = (P(AXES, None), P(), P(AXES, None), P(), P())
    return jax.shard_map(body, mesh=fine, in_specs=in_specs, out_specs=P(AXES, None), check_vma=False)
```

time: 145 us -> 137 us (0.945)
  waiting for transfers between devices: 44.5 us -> 36.6 us
  local copies, waits for them, and re-layouts: 6.86 us -> 4.16 us
  starting transfers between devices: 23.8 us -> 25.6 us
    ppermute x6, waiting for transfers between devices: 31.2 us -> 26.8 us  [turned(): return lax.ppermute(value, 'x', [(i, (i + steps) % NX) for i in range(NX)])]
    unnamed x42 -> x12, local copies, waits for them, and re-layouts: 6.86 us -> 3.17 us
    ppermute x1, waiting for transfers between devices: 12.3 us -> 8.84 us  [body(): lax.ppermute(conv_input[TOK - KERNEL + 1:], AXES, [(i, i + 1) for i in ra...]
    pallas_call x4, Pallas kernels: 4.2 us -> 7.35 us  [local(): pl.pallas_call(functools.partial(local_kernel, ahead), in_specs=[SMEM] +...]
    ppermute x6, starting transfers between devices: 15.9 us -> 17.7 us  [turned(): return lax.ppermute(value, 'x', [(i, (i + steps) % NX) for i in range(NX)])]
    pallas_call x5, Pallas kernels: 6.45 us -> 4.79 us  [the longest x4 4.47 us: states(): pl.pallas_call(functools.partial(state_kernel, ahead, part), in_specs=[SM...]
  transfers between devices with their start and end apart: 8 -> 8, of which waited for: 6 -> 5; matrix products, arithmetic and copies ran while one was open for 0% -> 0% of each run, Pallas kernels for 8% -> 11%
where the time goes in v3:
time: 137 us
  blocking collectives  52 us (38%)
  waiting for transfers between devices  36.6 us (27%)
  starting transfers between devices  25.6 us (19%)
  Pallas kernels  17.9 us (13%)
  local copies, waits for them, and re-layouts  4.16 us (3%)
    all_to_all x1, blocking collectives, body(): rows = lax.all_to_all(row_total(x, pays), ('y', 'z'), 0, 0, tiled=True)  29.1 us
    ppermute x6, waiting for transfers between devices, turned(): return lax.ppermute(value, 'x', [(i, (i + steps) % NX) for i in range(NX)])  26.8 us
    all_to_all x1, blocking collectives, body(): lax.all_to_all(scan(core, rows, own, other), ('y', 'z'), 0, 0, tiled=True)  22.9 us
    ppermute x6, starting transfers between devices, turned(): return lax.ppermute(value, 'x', [(i, (i + steps) % NX) for i in range(NX)])  17.7 us
    ppermute x1, waiting for transfers between devices, body(): lax.ppermute(conv_input[TOK - KERNEL + 1:], AXES, [(i, i + 1) for i in ra...  8.84 us
    pallas_call x4, Pallas kernels, local(): pl.pallas_call(functools.partial(local_kernel, ahead), in_specs=[SMEM] +...  7.35 us
    ppermute x1, starting transfers between devices, body(): other = lax.ppermute(own, 'core', [(0, 1), (1, 0)])  4.82 us
    pallas_call x4, Pallas kernels, final(): pl.pallas_call(functools.partial(final_kernel, ahead), in_specs=[SMEM] +...  4.53 us
  transfers between devices with their start and end apart: 8, of which 5 were waited for; matrix products, arithmetic and copies ran while one was open for 0% of the time, Pallas kernels for 11%

profile of v3, /device:TPU:17, one launch (start us, length us, event | category | flops | bytes accessed | tf_op | source)
XLA Modules:
  0.0 136.7 jit_solution(18422294897447085359)
XLA Ops:
  0.0 0.0 copy-start.2
  0.0 1.0 slice.3
  1.0 3.1 %collective-permute-start = (bf16[3,9216]{1,0:T(4,128)(2,1)S(1)}, bf16[3,9216]{1,0:T(4,128)(2,1)S(1)}, u32[]{:S(2)}, u32[]{:S(2)}) collective-permute-start(bf16[3,9216]{1,0:T(4,128)(2,1)S(1)} %slice.3), channel_id=1, source_target_pairs={{0,1},{1,2},{2,3},{3,4},{4,5},{5,6},{6,7},{7,8},{8,9},{9,10},{10,1... | collective-permute-start | bytes 165896 | tf_op jit(solution)/shard_map/ppermute | solution.py:369
  4.1 0.0 copy-start
  4.1 1.7 %copy-done = bf16[128,9216]{1,0:T(8,128)(2,1)S(1)} copy-done((bf16[128,9216]{1,0:T(8,128)(2,1)S(1)}, bf16[128,9216]{1,0:T(8,128)(2,1)}, u32[]{:S(2)}) %copy-start) | copy-done | bytes 2359320
  5.8 0.0 copy-start.3
  5.8 0.8 copy-done.3
  6.6 0.0 copy-start.4
  6.6 0.7 copy-done.4
  7.3 0.3 shard_map.55
  7.6 8.8 %collective-permute-done.edge_ref = bf16[3,9216]{1,0:T(4,128)(2,1)S(1)} collective-permute-done((bf16[3,9216]{1,0:T(4,128)(2,1)S(1)}, bf16[3,9216]{1,0:T(4,128)(2,1)S(1)}, u32[]{:S(2)}, u32[]{:S(2)}) %collective-permute-start) | collective-permute-done | bytes 55328 | tf_op jit(solution)/shard_map/ppermute | solution.py:369
  16.4 0.0 copy-done.2
  16.4 1.1 shard_map.56
  17.6 1.9 %collective-permute-start.1 = (bf16[2096,128]{1,0:T(8,128)(2,1)S(1)}, bf16[2096,128]{1,0:T(8,128)(2,1)S(1)}, u32[]{:S(2)}, u32[]{:S(2)}) collective-permute-start(bf16[2096,128]{1,0:T(8,128)(2,1)S(1)} %shard_map.56), channel_id=1, source_target_pairs={{0,2},{1,3},{2,0},{3,1},{4,6},{5,7},{6,4},{7,5},{8,10},{9,11},{10,... | collective-permute-start | bytes 1609736 | tf_op jit(solution)/shard_map/ppermute | solution.py:362
  19.5 1.1 shard_map.57
  20.6 1.9 %collective-permute-start.2 = (bf16[2096,128]{1,0:T(8,128)(2,1)S(1)}, bf16[2096,128]{1,0:T(8,128)(2,1)S(1)}, u32[]{:S(2)}, u32[]{:S(2)}) collective-permute-start(bf16[2096,128]{1,0:T(8,128)(2,1)S(1)} %shard_map.57), channel_id=1, source_target_pairs={{0,1},{1,2},{2,3},{3,0},{4,5},{5,6},{6,7},{7,4},{8,9},{9,10},{10,1... | collective-permute-start | bytes 1609736 | tf_op jit(solution)/shard_map/ppermute | solution.py:362
  22.6 1.1 shard_map.58
  23.7 4.6 %collective-permute-start.3 = (bf16[2096,128]{1,0:T(8,128)(2,1)S(1)}, bf16[2096,128]{1,0:T(8,128)(2,1)S(1)}, u32[]{:S(2)}, u32[]{:S(2)}) collective-permute-start(bf16[2096,128]{1,0:T(8,128)(2,1)S(1)} %shard_map.58), channel_id=1, source_target_pairs={{0,3},{1,0},{2,1},{3,2},{4,7},{5,4},{6,5},{7,6},{8,11},{9,8},{10,9... | collective-permute-start | bytes 1609736 | tf_op jit(solution)/shard_map/ppermute | solution.py:362
  28.3 1.1 shard_map.59.refs_3_
  29.4 5.6 %collective-permute-done.1.refs_0_ = bf16[2096,128]{1,0:T(8,128)(2,1)S(1)} collective-permute-done((bf16[2096,128]{1,0:T(8,128)(2,1)S(1)}, bf16[2096,128]{1,0:T(8,128)(2,1)S(1)}, u32[]{:S(2)}, u32[]{:S(2)}) %collective-permute-start.1) | collective-permute-done | bytes 536608 | tf_op jit(solution)/shard_map/ppermute | solution.py:362
  35.0 11.6 %collective-permute-done.2.refs_1_ = bf16[2096,128]{1,0:T(8,128)(2,1)S(1)} collective-permute-done((bf16[2096,128]{1,0:T(8,128)(2,1)S(1)}, bf16[2096,128]{1,0:T(8,128)(2,1)S(1)}, u32[]{:S(2)}, u32[]{:S(2)}) %collective-permute-start.2) | collective-permute-done | bytes 536608 | tf_op jit(solution)/shard_map/ppermute | solution.py:362
  46.7 0.0 collective-permute-done.3.refs_2_
  46.7 0.4 shard_map.60
  47.1 29.1 %all_to_all.10.rows_ref = bf16[64,40,128]{2,1,0:T(8,128)(2,1)S(1)} all-to-all(bf16[64,40,128]{2,1,0:T(8,128)(2,1)S(1)} %shard_map.60), channel_id=1, replica_groups=mesh['y'=8,'core'=2,'z'=8,'x'=4] {'y','z'}, dimensions={0} | all-to-all | bytes 1310720 | tf_op jit(solution)/shard_map/all_to_all | solution.py:376
  76.2 0.2 shard_map.61.own_ref
  76.4 4.8 %collective-permute-start.4 = (f32[8,40,128]{2,1,0:T(8,128)S(1)}, f32[8,40,128]{2,1,0:T(8,128)S(1)}, u32[]{:S(2)}, u32[]{:S(2)}) collective-permute-start(f32[8,40,128]{2,1,0:T(8,128)S(1)} %shard_map.61.own_ref), channel_id=1, source_target_pairs={{0,32},{32,0},{1,33},{33,1},{2,34},{34,2},{3,35},{35,3},{4,36},{36... | collective-permute-start | bytes 491528 | tf_op jit(solution)/shard_map/ppermute | solution.py:378
  81.2 1.0 collective-permute-done.4.other_ref
  82.2 0.2 shard_map.62
  82.4 0.0 copy-start.1
  82.4 0.0 copy-start.5
  82.4 22.9 %all_to_all.11 = bf16[64,32,128]{2,1,0:T(8,128)(2,1)S(1)} all-to-all(bf16[64,32,128]{2,1,0:T(8,128)(2,1)S(1)} %shard_map.62), channel_id=1, replica_groups=mesh['y'=8,'core'=2,'z'=8,'x'=4] {'y','z'}, dimensions={0} | all-to-all | bytes 1048576 | tf_op jit(solution)/shard_map/all_to_all | solution.py:379
  105.3 0.5 shard_map.63
  105.8 2.6 %collective-permute-start.7 = (bf16[2048,128]{1,0:T(8,128)(2,1)S(1)}, bf16[2048,128]{1,0:T(8,128)(2,1)S(1)}, u32[]{:S(2)}, u32[]{:S(2)}) collective-permute-start(bf16[2048,128]{1,0:T(8,128)(2,1)S(1)} %get-tuple-element.41), channel_id=1, source_target_pairs={{0,2},{1,3},{2,0},{3,1},{4,6},{5,7},{6,4},{7,5},{8,10},{9,11},{10,... | collective-permute-start | bytes 1572872 | tf_op jit(solution)/shard_map/ppermute | solution.py:362
  108.3 2.2 %collective-permute-start.6 = (bf16[2048,128]{1,0:T(8,128)(2,1)S(1)}, bf16[2048,128]{1,0:T(8,128)(2,1)S(1)}, u32[]{:S(2)}, u32[]{:S(2)}) collective-permute-start(bf16[2048,128]{1,0:T(8,128)(2,1)S(1)} %get-tuple-element.38), channel_id=1, source_target_pairs={{0,1},{1,2},{2,3},{3,0},{4,5},{5,6},{6,7},{7,4},{8,9},{9,10},{10,1... | collective-permute-start | bytes 1572872 | tf_op jit(solution)/shard_map/ppermute | solution.py:362
  110.6 4.5 %collective-permute-start.5 = (bf16[2048,128]{1,0:T(8,128)(2,1)S(1)}, bf16[2048,128]{1,0:T(8,128)(2,1)S(1)}, u32[]{:S(2)}, u32[]{:S(2)}) collective-permute-start(bf16[2048,128]{1,0:T(8,128)(2,1)S(1)} %get-tuple-element.35), channel_id=1, source_target_pairs={{0,3},{1,0},{2,1},{3,2},{4,7},{5,4},{6,5},{7,6},{8,11},{9,8},{10,9... | collective-permute-start | bytes 1572872 | tf_op jit(solution)/shard_map/ppermute | solution.py:362
  115.0 0.0 copy-done.1
  115.0 0.0 copy-done.5
  115.1 1.8 %shard_map.67 = (f32[128,2048]{1,0:T(8,128)S(1)}, bf16[128,128]{1,0:T(8,128)(2,1)S(1)}) custom-call(s32[1]{0:T(128)} %bitcast.x_ref, bf16[128,9216]{1,0:T(8,128)(2,1)S(1)} %copy-done.1, bf16[3,9216]{1,0:T(4,128)(2,1)S(1)} %collective-permute-done.edge_ref, f32[4,9216]{1,0:T(4,128)S(1)} %copy-done.2, f32[384,128]{1,0:T(8,128)S(1)} %get-tuple-element.32.late_ref, ...), custom_call_target="tpu_custom_call" | custom-call | flops 1000000000 | bytes 8000000 | tf_op jit(solution)/shard_map/pallas_call | solution.py:300
  116.9 1.1 shard_map.68.refs_0_
  118.0 1.8 %shard_map.66 = (f32[128,2048]{1,0:T(8,128)S(1)}, bf16[128,128]{1,0:T(8,128)(2,1)S(1)}) custom-call(s32[1]{0:T(128)} %bitcast.x_ref, bf16[128,9216]{1,0:T(8,128)(2,1)S(1)} %copy-done.1, bf16[3,9216]{1,0:T(4,128)(2,1)S(1)} %collective-permute-done.edge_ref, f32[4,9216]{1,0:T(4,128)S(1)} %copy-done.2, f32[384,128]{1,0:T(8,128)S(1)} %get-tuple-element.32.late_ref, ...), custom_call_target="tpu_custom_call" | custom-call | flops 1000000000 | bytes 8000000 | tf_op jit(solution)/shard_map/pallas_call | solution.py:300
  119.9 1.8 %shard_map.65 = (f32[128,2048]{1,0:T(8,128)S(1)}, bf16[128,128]{1,0:T(8,128)(2,1)S(1)}) custom-call(s32[1]{0:T(128)} %bitcast.x_ref, bf16[128,9216]{1,0:T(8,128)(2,1)S(1)} %copy-done.1, bf16[3,9216]{1,0:T(4,128)(2,1)S(1)} %collective-permute-done.edge_ref, f32[4,9216]{1,0:T(4,128)S(1)} %copy-done.2, f32[384,128]{1,0:T(8,128)S(1)} %get-tuple-element.32.late_ref, ...), custom_call_target="tpu_custom_call" | custom-call | flops 1000000000 | bytes 8000000 | tf_op jit(solution)/shard_map/pallas_call | solution.py:300
  121.7 1.8 %shard_map.64 = (f32[128,2048]{1,0:T(8,128)S(1)}, bf16[128,128]{1,0:T(8,128)(2,1)S(1)}) custom-call(s32[1]{0:T(128)} %bitcast.x_ref, bf16[128,9216]{1,0:T(8,128)(2,1)S(1)} %copy-done.1, bf16[3,9216]{1,0:T(4,128)(2,1)S(1)} %collective-permute-done.edge_ref, f32[4,9216]{1,0:T(4,128)S(1)} %copy-done.2, f32[384,128]{1,0:T(8,128)S(1)} %get-tuple-element.32.late_ref, ...), custom_call_target="tpu_custom_call" | custom-call | flops 1000000000 | bytes 8000000 | tf_op jit(solution)/shard_map/pallas_call | solution.py:300
  123.6 0.0 collective-permute-done.7.state_ref
  123.6 1.1 shard_map.69.refs_0_
  124.7 9.5 %collective-permute-done.6.state_ref = bf16[2048,128]{1,0:T(8,128)(2,1)S(1)} collective-permute-done((bf16[2048,128]{1,0:T(8,128)(2,1)S(1)}, bf16[2048,128]{1,0:T(8,128)(2,1)S(1)}, u32[]{:S(2)}, u32[]{:S(2)}) %collective-permute-start.6) | collective-permute-done | bytes 524320 | tf_op jit(solution)/shard_map/ppermute | solution.py:362
  134.2 1.1 shard_map.70.refs_0_
  135.4 0.0 collective-permute-done.5.state_ref
  135.4 1.1 shard_map.71
Async XLA Ops:
  0.0 16.4 %copy-start.2 = (f32[4,9216]{1,0:T(4,128)S(1)}, f32[4,9216]{1,0:T(4,128)}, u32[]{:S(2)}) copy-start(f32[4,9216]{1,0:T(4,128)} %w_ref.15) | copy-start | bytes 442372
  1.0 15.5 %collective-permute-start = (bf16[3,9216]{1,0:T(4,128)(2,1)S(1)}, bf16[3,9216]{1,0:T(4,128)(2,1)S(1)}, u32[]{:S(2)}, u32[]{:S(2)}) collective-permute-start(bf16[3,9216]{1,0:T(4,128)(2,1)S(1)} %slice.3), channel_id=1, source_target_pairs={{0,1},{1,2},{2,3},{3,4},{4,5},{5,6},{6,7},{7,8},{8,9},{9,10},{10,1... | collective-permute-start | bytes 165896 | tf_op jit(solution)/shard_map/ppermute | solution.py:369
  4.1 1.7 %copy-start = (bf16[128,9216]{1,0:T(8,128)(2,1)S(1)}, bf16[128,9216]{1,0:T(8,128)(2,1)}, u32[]{:S(2)}) copy-start(bf16[128,9216]{1,0:T(8,128)(2,1)} %in_ref.7) | copy-start | bytes 7077892
  5.8 0.8 copy-start.3
  6.6 0.7 copy-start.4
  17.6 17.5 %collective-permute-start.1 = (bf16[2096,128]{1,0:T(8,128)(2,1)S(1)}, bf16[2096,128]{1,0:T(8,128)(2,1)S(1)}, u32[]{:S(2)}, u32[]{:S(2)}) collective-permute-start(bf16[2096,128]{1,0:T(8,128)(2,1)S(1)} %shard_map.56), channel_id=1, source_target_pairs={{0,2},{1,3},{2,0},{3,1},{4,6},{5,7},{6,4},{7,5},{8,10},{9,11},{10,... | collective-permute-start | bytes 1609736 | tf_op jit(solution)/shard_map/ppermute | solution.py:362
  20.6 26.0 %collective-permute-start.2 = (bf16[2096,128]{1,0:T(8,128)(2,1)S(1)}, bf16[2096,128]{1,0:T(8,128)(2,1)S(1)}, u32[]{:S(2)}, u32[]{:S(2)}) collective-permute-start(bf16[2096,128]{1,0:T(8,128)(2,1)S(1)} %shard_map.57), channel_id=1, source_target_pairs={{0,1},{1,2},{2,3},{3,0},{4,5},{5,6},{6,7},{7,4},{8,9},{9,10},{10,1... | collective-permute-start | bytes 1609736 | tf_op jit(solution)/shard_map/ppermute | solution.py:362
  23.7 23.0 %collective-permute-start.3 = (bf16[2096,128]{1,0:T(8,128)(2,1)S(1)}, bf16[2096,128]{1,0:T(8,128)(2,1)S(1)}, u32[]{:S(2)}, u32[]{:S(2)}) collective-permute-start(bf16[2096,128]{1,0:T(8,128)(2,1)S(1)} %shard_map.58), channel_id=1, source_target_pairs={{0,3},{1,0},{2,1},{3,2},{4,7},{5,4},{6,5},{7,6},{8,11},{9,8},{10,9... | collective-permute-start | bytes 1609736 | tf_op jit(solution)/shard_map/ppermute | solution.py:362
  76.4 5.8 %collective-permute-start.4 = (f32[8,40,128]{2,1,0:T(8,128)S(1)}, f32[8,40,128]{2,1,0:T(8,128)S(1)}, u32[]{:S(2)}, u32[]{:S(2)}) collective-permute-start(f32[8,40,128]{2,1,0:T(8,128)S(1)} %shard_map.61.own_ref), channel_id=1, source_target_pairs={{0,32},{32,0},{1,33},{33,1},{2,34},{34,2},{3,35},{35,3},{4,36},{36... | collective-permute-start | bytes 491528 | tf_op jit(solution)/shard_map/ppermute | solution.py:378
  82.4 32.7 %copy-start.1 = (bf16[128,9216]{1,0:T(8,128)(2,1)S(1)}, bf16[128,9216]{1,0:T(8,128)(2,1)}, u32[]{:S(2)}) copy-start(bf16[128,9216]{1,0:T(8,128)(2,1)} %in_ref.7) | copy-start | bytes 7077892
  82.4 32.7 %copy-start.5 = (f32[128]{0:T(128)S(1)}, f32[128]{0:T(128)}, u32[]{:S(2)}) copy-start(f32[128]{0:T(128)} %param.9) | copy-start | bytes 1540
  105.8 17.8 %collective-permute-start.7 = (bf16[2048,128]{1,0:T(8,128)(2,1)S(1)}, bf16[2048,128]{1,0:T(8,128)(2,1)S(1)}, u32[]{:S(2)}, u32[]{:S(2)}) collective-permute-start(bf16[2048,128]{1,0:T(8,128)(2,1)S(1)} %get-tuple-element.41), channel_id=1, source_target_pairs={{0,2},{1,3},{2,0},{3,1},{4,6},{5,7},{6,4},{7,5},{8,10},{9,11},{10,... | collective-permute-start | bytes 1572872 | tf_op jit(solution)/shard_map/ppermute | solution.py:362
  108.3 25.9 %collective-permute-start.6 = (bf16[2048,128]{1,0:T(8,128)(2,1)S(1)}, bf16[2048,128]{1,0:T(8,128)(2,1)S(1)}, u32[]{:S(2)}, u32[]{:S(2)}) collective-permute-start(bf16[2048,128]{1,0:T(8,128)(2,1)S(1)} %get-tuple-element.38), channel_id=1, source_target_pairs={{0,1},{1,2},{2,3},{3,0},{4,5},{5,6},{6,7},{7,4},{8,9},{9,10},{10,1... | collective-permute-start | bytes 1572872 | tf_op jit(solution)/shard_map/ppermute | solution.py:362
  110.6 24.8 %collective-permute-start.5 = (bf16[2048,128]{1,0:T(8,128)(2,1)S(1)}, bf16[2048,128]{1,0:T(8,128)(2,1)S(1)}, u32[]{:S(2)}, u32[]{:S(2)}) collective-permute-start(bf16[2048,128]{1,0:T(8,128)(2,1)S(1)} %get-tuple-element.35), channel_id=1, source_target_pairs={{0,3},{1,0},{2,1},{3,2},{4,7},{5,4},{6,5},{7,6},{8,11},{9,8},{10,9... | collective-permute-start | bytes 1572872 | tf_op jit(solution)/shard_map/ppermute | solution.py:362

commit v4 on v3

v4 whole, which is shorter than its diff:
```python
import jax
import jax.numpy as jnp
from jax import lax
from jax.experimental import pallas as pl
from jax.experimental.pallas import tpu as pltpu
from jax.sharding import Mesh, PartitionSpec as P

HEADS = 128
HEAD_DIM = 64
STATE = 128
GROUPS = 4
KERNEL = 4
TOK = 128
PER = HEADS // GROUPS
NB = PER // 2
HCOLS = HEADS * HEAD_DIM
NX, NY, NZ = 4, 8, 8
NZL = 2
NZH = NZ // NZL
NEAR = NZL * NX
OWN = HEADS // NEAR
NBO = OWN // 2
ROWS = NBO * STATE
TAIL = 32
PAY = ROWS + TAIL
SHARES = NY * NZH
SROWS = ROWS // SHARES
TROWS = SROWS + 8
F32 = jnp.float32
BF16 = jnp.bfloat16
LIMIT = 16 * 1024 * 1024
AXES = ("y", "core", "zh", "zl", "x")
NEAR_AXES = ("zl", "x")
FAR_AXES = ("y", "zh")
SMEM = pl.BlockSpec(memory_space=pltpu.SMEM)
VMEM = pl.BlockSpec(memory_space=pltpu.VMEM)
ANY = pl.BlockSpec(memory_space=pl.ANY)


def params():
    return pltpu.CompilerParams(vmem_limit_bytes=LIMIT)


def three(v):
    hi = v.astype(BF16).astype(F32)
    mid = (v - hi).astype(BF16).astype(F32)
    low = (v - hi - mid).astype(BF16).astype(F32)
    return hi, mid, low


def lanes_of(per_head, base, block, rows):
    lane = lax.broadcasted_iota(jnp.int32, (rows, 128), 1)
    pick = base + 2 * block + lane // HEAD_DIM
    return jnp.take_along_axis(per_head, pick, axis=1)


def prep_kernel(x_hbm, raw_ref, log_ref, x_ref, early_ref, late_ref, sem):
    copy = pltpu.make_async_copy(x_hbm, x_ref, sem)
    copy.start()
    raw = raw_ref[...]
    step = jnp.maximum(raw, 0.0) + jnp.log1p(jnp.exp(-jnp.abs(raw)))
    cum = -jnp.exp(log_ref[...]) * step
    row = lax.broadcasted_iota(jnp.int32, (TOK, HEADS), 0)
    shift = 1
    while shift < TOK:
        cum = cum + jnp.where(row >= shift, pltpu.roll(cum, shift, 0), 0.0)
        shift *= 2
    last = cum[TOK - 1 :, :]
    early_ref[:TOK] = jnp.exp(last - cum) * step
    early_ref[TOK:] = jnp.broadcast_to(jnp.exp(last), (8, HEADS))
    late_ref[:TOK] = cum
    late_ref[TOK : 2 * TOK] = cum.T
    late_ref[2 * TOK :] = step.T
    copy.wait()


def prep(conv_input, step_raw, decay_log):
    channels = conv_input.shape[1]
    return pl.pallas_call(
        prep_kernel,
        in_specs=[ANY, VMEM, VMEM],
        out_specs=[VMEM] * 3,
        out_shape=[
            jax.ShapeDtypeStruct((TOK, channels), BF16),
            jax.ShapeDtypeStruct((TOK + 8, HEADS), F32),
            jax.ShapeDtypeStruct((2 * TOK + HEADS, HEADS), F32),
        ],
        scratch_shapes=[pltpu.SemaphoreType.DMA],
        compiler_params=params(),
        cost_estimate=pl.CostEstimate(flops=0, bytes_accessed=0, transcendentals=0),
    )(conv_input, step_raw, decay_log.reshape(1, HEADS))


def convolve(x_ref, edge_ref, w_ref, at):
    cols = pl.ds(pl.multiple_of(at, 128), 128)
    x = x_ref[:, cols].astype(F32)
    edge = edge_ref[:, cols].astype(F32)
    weight = w_ref[:, cols]
    wide = jnp.concatenate([jnp.zeros((8 - KERNEL + 1, 128), F32), edge, x], 0)
    out = None
    for tap in range(KERNEL):
        first = 8 - KERNEL + 1 + tap
        term = wide[first : first + TOK] * weight[tap : tap + 1]
        out = term if out is None else out + term
    return out.astype(BF16)


def state_kernel(in_ref, edge_ref, w_ref, early_ref, pay_ref):
    factor = early_ref[:TOK]
    decay = early_ref[TOK:]
    blank = jnp.zeros((TAIL - 3 * NBO, 128), F32)
    for group in range(GROUPS):
        writers = convolve(in_ref, edge_ref, w_ref, HCOLS + group * STATE).astype(F32).T.astype(BF16)
        for owner in range(group * PER // OWN, (group + 1) * PER // OWN):
            base = owner * OWN
            rows = [lanes_of(decay, base, b, 8)[:1] for b in range(NBO)]
            terms = three(jnp.concatenate(rows, 0))
            pay_ref[owner, ROWS:] = jnp.concatenate([*terms, blank], 0).astype(BF16)
            for pair in range(NBO // 2):
                weighted = []
                for b in (2 * pair, 2 * pair + 1):
                    value = convolve(in_ref, edge_ref, w_ref, base * HEAD_DIM + b * 128)
                    weighted.append((value.astype(F32) * lanes_of(factor, base, b, TOK)).astype(BF16))
                state = jnp.dot(writers, jnp.concatenate(weighted, 1), preferred_element_type=F32)
                for half in range(2):
                    at = (2 * pair + half) * STATE
                    pay_ref[owner, at : at + STATE] = state[:, half * 128 : (half + 1) * 128].astype(BF16)


def states(*args):
    return pl.pallas_call(
        state_kernel,
        in_specs=[VMEM] * 4,
        out_specs=VMEM,
        out_shape=jax.ShapeDtypeStruct((NEAR, PAY, 128), BF16),
        compiler_params=params(),
        cost_estimate=pl.CostEstimate(flops=10**8, bytes_accessed=3 * 10**6, transcendentals=0),
    )(*args)


def decays_of(ref, source):
    terms = ref[source, ROWS:].astype(F32)
    return terms[:NBO] + terms[NBO : 2 * NBO] + terms[2 * NBO : 3 * NBO]


def total_kernel(pay_ref, out_ref):
    decays = [decays_of(pay_ref, source) for source in range(NEAR)]
    product = decays[0]
    for decay in decays[1:]:
        product = product * decay
    hi, mid, low = three(product)
    for b in range(NBO):
        rows = slice(b * STATE, (b + 1) * STATE)
        total = pay_ref[0, rows].astype(F32)
        for source in range(1, NEAR):
            total = decays[source][b : b + 1] * total + pay_ref[source, rows].astype(F32)
        tail = jnp.concatenate(
            [hi[b : b + 1], mid[b : b + 1], low[b : b + 1], jnp.zeros((5, 128), F32)], 0
        )
        for part in range(STATE // SROWS):
            share = jnp.concatenate([total[part * SROWS : (part + 1) * SROWS], tail], 0)
            out_ref[b * (STATE // SROWS) + part] = share.astype(BF16)


def row_total(pays):
    return pl.pallas_call(
        total_kernel,
        in_specs=[VMEM],
        out_specs=VMEM,
        out_shape=jax.ShapeDtypeStruct((SHARES, TROWS, 128), BF16),
        compiler_params=params(),
    )(pays)


def row_of(rows_ref, at):
    block = rows_ref[at].astype(F32)
    tail = block[SROWS:]
    return block[:SROWS], tail[:1] + tail[1:2] + tail[2:3]


def group_kernel(rows_ref, out_ref):
    for y in range(NY):
        total, product = row_of(rows_ref, y * NZH)
        for z in range(1, NZH):
            state, decay = row_of(rows_ref, y * NZH + z)
            total = decay * total + state
            product = decay * product
        out_ref[y, :SROWS] = total
        out_ref[y, SROWS:] = jnp.broadcast_to(product, (8, 128))


def group_total(rows):
    return pl.pallas_call(
        group_kernel,
        in_specs=[VMEM],
        out_specs=VMEM,
        out_shape=jax.ShapeDtypeStruct((NY, TROWS, 128), F32),
        compiler_params=params(),
    )(rows)


def scan_kernel(core_ref, rows_ref, own_ref, other_ref, out_ref):
    first = core_ref[0] == 0
    entry = jnp.zeros((SROWS, 128), F32)
    for y in range(NY):
        own, other = own_ref[y], other_ref[y]
        one = jnp.where(first, own, other)
        two = jnp.where(first, other, own)
        middle = one[SROWS : SROWS + 1] * entry + one[:SROWS]
        state = jnp.where(first, entry, middle)
        entry = two[SROWS : SROWS + 1] * middle + two[:SROWS]
        for z in range(NZH):
            out_ref[y * NZH + z] = state.astype(BF16)
            if z < NZH - 1:
                term, decay = row_of(rows_ref, y * NZH + z)
                state = decay * state + term


def scan(core, rows, own, other):
    return pl.pallas_call(
        scan_kernel,
        in_specs=[SMEM] + [VMEM] * 3,
        out_specs=VMEM,
        out_shape=jax.ShapeDtypeStruct((SHARES, SROWS, 128), BF16),
        compiler_params=params(),
    )(core, rows, own, other)


def enter_kernel(entry_ref, pay_ref, out_ref):
    decays = [decays_of(pay_ref, source) for source in range(NEAR - 1)]
    for b in range(NBO):
        rows = slice(b * STATE, (b + 1) * STATE)
        state = entry_ref[rows].astype(F32)
        for target in range(NEAR):
            out_ref[target, rows] = state.astype(BF16)
            if target < NEAR - 1:
                state = decays[target][b : b + 1] * state + pay_ref[target, rows].astype(F32)


def enter(entry, pays):
    return pl.pallas_call(
        enter_kernel,
        in_specs=[VMEM] * 2,
        out_specs=VMEM,
        out_shape=jax.ShapeDtypeStruct((NEAR, ROWS, 128), BF16),
        compiler_params=params(),
    )(entry, pays)


def local_kernel(in_ref, edge_ref, w_ref, late_ref, gain_ref, out_ref, rea_ref):
    cum = late_ref[:TOK]
    gain = jnp.broadcast_to(gain_ref[...], (8, HEADS))
    row = lax.broadcasted_iota(jnp.int32, (TOK, TOK), 0)
    col = lax.broadcasted_iota(jnp.int32, (TOK, TOK), 1)
    causal = row >= col
    first = col < HEAD_DIM
    for group in range(GROUPS):
        base = group * PER
        writers = convolve(in_ref, edge_ref, w_ref, HCOLS + group * STATE)
        readers = convolve(in_ref, edge_ref, w_ref, HCOLS + (GROUPS + group) * STATE)
        rea_ref[:, group * STATE : (group + 1) * STATE] = readers
        affinity = lax.dot_general(
            readers, writers, (((1,), (1,)), ((), ())), preferred_element_type=F32
        )
        cum_t = late_ref[TOK + base : TOK + base + PER]
        step_t = late_ref[TOK + HEADS + base : TOK + HEADS + base + PER]
        for b in range(NB):
            scores = []
            for h in (2 * b, 2 * b + 1):
                here = jnp.take_along_axis(cum, jnp.full((TOK, TOK), base + h, jnp.int32), axis=1)
                span = jnp.where(causal, here - cum_t[h : h + 1], -1e30)
                weight = jnp.exp(span) * step_t[h : h + 1]
                scores.append((weight * affinity).astype(BF16))
            at = base * HEAD_DIM + b * 128
            value = convolve(in_ref, edge_ref, w_ref, at)
            zero = jnp.zeros_like(value)
            apart = jnp.concatenate([jnp.where(first, value, zero), jnp.where(first, zero, value)], 0)
            local = jnp.dot(jnp.concatenate(scores, 1), apart, preferred_element_type=F32)
            skip = lanes_of(gain, base, b, 8)[:1]
            out_ref[:, at : at + 128] = local + skip * value.astype(F32)


def local(*args):
    return pl.pallas_call(
        local_kernel,
        in_specs=[VMEM] * 5,
        out_specs=[VMEM] * 2,
        out_shape=[
            jax.ShapeDtypeStruct((TOK, HCOLS), F32),
            jax.ShapeDtypeStruct((TOK, GROUPS * STATE), BF16),
        ],
        compiler_params=params(),
        cost_estimate=pl.CostEstimate(flops=10**9, bytes_accessed=8 * 10**6, transcendentals=0),
    )(*args)


def final_kernel(rea_ref, late_ref, part_ref, state_ref, out_ref, buf, sems):
    growth = jnp.exp(late_ref[:TOK])
    width = OWN * HEAD_DIM
    copies = []
    for owner in range(NEAR):
        base = owner * OWN
        group = base // PER
        readers = rea_ref[:, group * STATE : (group + 1) * STATE]
        for pair in range(NBO // 2):
            at = 2 * pair * STATE
            both = jnp.concatenate(
                [state_ref[owner, at : at + STATE], state_ref[owner, at + STATE : at + 2 * STATE]], 1
            )
            carried = jnp.dot(readers, both, preferred_element_type=F32)
            for half in range(2):
                b = 2 * pair + half
                cols = slice(owner * width + b * 128, owner * width + (b + 1) * 128)
                grow = lanes_of(growth, base, b, TOK)
                result = part_ref[:, cols] + carried[:, half * 128 : (half + 1) * 128] * grow
                buf[:, cols] = result.astype(BF16)
        cols = pl.ds(owner * width, width)
        copies.append(pltpu.make_async_copy(buf.at[:, cols], out_ref.at[:, cols], sems.at[owner]))
        copies[-1].start()
    for copy in copies:
        copy.wait()


def final(*args):
    return pl.pallas_call(
        final_kernel,
        in_specs=[VMEM] * 4,
        out_specs=ANY,
        out_shape=jax.ShapeDtypeStruct((TOK, HCOLS), BF16),
        scratch_shapes=[pltpu.VMEM((TOK, HCOLS), BF16), pltpu.SemaphoreType.DMA((NEAR,))],
        compiler_params=params(),
        cost_estimate=pl.CostEstimate(flops=10**8, bytes_accessed=2 * 10**6, transcendentals=0),
    )(*args)


def body(conv_input, conv_weight, step_raw, decay_log, skip_gain):
    count = lax.axis_size(AXES)
    core = lax.axis_index("core").reshape(1)
    edge = lax.ppermute(conv_input[TOK - KERNEL + 1 :], AXES, [(i, i + 1) for i in range(count - 1)])
    held, early, late = prep(conv_input, step_raw, decay_log)
    made = states(held, edge, conv_weight, early)
    pays = lax.all_to_all(made, NEAR_AXES, 0, 0, tiled=True)
    rows = lax.all_to_all(row_total(pays), FAR_AXES, 0, 0, tiled=True)
    own = group_total(rows)
    other = lax.ppermute(own, "core", [(0, 1), (1, 0)])
    entry = lax.all_to_all(scan(core, rows, own, other), FAR_AXES, 0, 0, tiled=True)
    entering = enter(entry.reshape(ROWS, 128), pays)
    late, entering = lax.optimization_barrier((late, entering))
    state = lax.all_to_all(entering, NEAR_AXES, 0, 0, tiled=True)
    part, readers = local(conv_input, edge, conv_weight, late, skip_gain.reshape(1, HEADS))
    return final(readers, late, part, state)


def solution(mesh):
    fine = Mesh(mesh.devices.reshape(NY, 2, NZH, NZL, NX), AXES)
    in_specs = (P(AXES, None), P(), P(AXES, None), P(), P())
    return jax.shard_map(body, mesh=fine, in_specs=in_specs, out_specs=P(AXES, None), check_vma=False)
```

time: 137 us -> 132 us (0.964)
  the two profiles are of different devices: /device:TPU:17 before, /device:TPU:1 now
where the time goes in v4:
time: 132 us
  blocking collectives  66.8 us (51%)
  waiting for transfers between devices  25.1 us (19%)
  Pallas kernels  14.4 us (11%)
  starting transfers between devices  13.8 us (10%)
  local copies, waits for them, and re-layouts  11.3 us (9%)
    all_to_all x1, blocking collectives, body(): pays = lax.all_to_all(made, NEAR_AXES, 0, 0, tiled=True)  27.1 us
    all_to_all x1, blocking collectives, body(): rows = lax.all_to_all(row_total(pays), FAR_AXES, 0, 0, tiled=True)  22.9 us
    all_to_all x1, blocking collectives, body(): lax.all_to_all(scan(core, rows, own, other), FAR_AXES, 0, 0, tiled=True)  16.9 us
    all_to_all x1, waiting for transfers between devices, body(): state = lax.all_to_all(entering, NEAR_AXES, 0, 0, tiled=True)  15.3 us
    unnamed x18, local copies, waits for them, and re-layouts  10.3 us
    ppermute x1, waiting for transfers between devices, body(): lax.ppermute(conv_input[TOK - KERNEL + 1:], AXES, [(i, i + 1) for i in ra...  8.84 us
    pallas_call x1, Pallas kernels, local(): pl.pallas_call(local_kernel, in_specs=[VMEM] * 5, out_specs=[VMEM] * 2, o...  6.97 us
    ppermute x1, starting transfers between devices, body(): other = lax.ppermute(own, 'core', [(0, 1), (1, 0)])  5.96 us
  transfers between devices with their start and end apart: 3, of which 3 were waited for; matrix products, arithmetic and copies ran while one was open for 0% of the time, Pallas kernels for 6%

profile of v4, /device:TPU:1, one launch (start us, length us, event | category | flops | bytes accessed | tf_op | source)
XLA Modules:
  0.0 131.7 jit_solution(1516551174776217261)
XLA Ops:
  0.0 0.0 copy-start.5
  0.0 1.0 slice.3
  1.0 3.9 %collective-permute-start = (bf16[3,9216]{1,0:T(4,128)(2,1)S(1)}, bf16[3,9216]{1,0:T(4,128)(2,1)S(1)}, u32[]{:S(2)}, u32[]{:S(2)}) collective-permute-start(bf16[3,9216]{1,0:T(4,128)(2,1)S(1)} %slice.3), channel_id=1, source_target_pairs={{0,1},{1,2},{2,3},{3,4},{4,5},{5,6},{6,7},{7,8},{8,9},{9,10},{10,1... | collective-permute-start | bytes 165896 | tf_op jit(solution)/shard_map/ppermute | solution.py:339
  4.9 0.0 copy-start.3
  5.0 1.7 %copy-done.3 = bf16[128,9216]{1,0:T(8,128)(2,1)S(1)} copy-done((bf16[128,9216]{1,0:T(8,128)(2,1)S(1)}, bf16[128,9216]{1,0:T(8,128)(2,1)}, u32[]{:S(2)}) %copy-start.3) | copy-done | bytes 2359320
  6.6 0.0 copy-start.6
  6.6 0.8 copy-done.6
  7.5 0.0 copy-start.7
  7.5 0.7 copy-done.7
  8.1 0.3 shard_map.55
  8.4 8.8 %collective-permute-done.edge_ref = bf16[3,9216]{1,0:T(4,128)(2,1)S(1)} collective-permute-done((bf16[3,9216]{1,0:T(4,128)(2,1)S(1)}, bf16[3,9216]{1,0:T(4,128)(2,1)S(1)}, u32[]{:S(2)}, u32[]{:S(2)}) %collective-permute-start) | collective-permute-done | bytes 55328 | tf_op jit(solution)/shard_map/ppermute | solution.py:339
  17.3 0.0 copy-done.5
  17.3 3.9 %shard_map.56 = bf16[8,1056,128]{2,1,0:T(8,128)(2,1)S(1)} custom-call(bf16[128,9216]{1,0:T(8,128)(2,1)S(1)} %get-tuple-element.13.in_ref, bf16[3,9216]{1,0:T(4,128)(2,1)S(1)} %collective-permute-done.edge_ref, f32[4,9216]{1,0:T(4,128)S(1)} %copy-done.5, f32[136,128]{1,0:T(8,128)S(1)} %get-tuple-element.14.early_ref), custom_call_target="tpu_custom_call" | custom-call | flops 100000000 | bytes 3000000 | tf_op jit(solution)/shard_map/pallas_call | solution.py:131
  21.2 27.1 %all_to_all.20.pay_ref = bf16[8,1056,128]{2,1,0:T(8,128)(2,1)S(1)} all-to-all(bf16[8,1056,128]{2,1,0:T(8,128)(2,1)S(1)} %shard_map.56), channel_id=1, replica_groups=mesh['y'=8,'core'=2,'zh'=4,'zl'=2,'x'=4] {'zl','x'}, dimensions={0} | all-to-all | bytes 4325376 | tf_op jit(solution)/shard_map/all_to_all | solution.py:342
  48.2 0.4 shard_map.57
  48.7 22.9 %all_to_all.21.rows_ref = bf16[32,40,128]{2,1,0:T(8,128)(2,1)S(1)} all-to-all(bf16[32,40,128]{2,1,0:T(8,128)(2,1)S(1)} %shard_map.57), channel_id=1, replica_groups=mesh['y'=8,'core'=2,'zh'=4,'zl'=2,'x'=4] {'y','zh'}, dimensions={0} | all-to-all | bytes 655360 | tf_op jit(solution)/shard_map/all_to_all | solution.py:343
  71.5 0.1 shard_map.58.own_ref
  71.6 6.0 %collective-permute-start.1 = (f32[8,40,128]{2,1,0:T(8,128)S(1)}, f32[8,40,128]{2,1,0:T(8,128)S(1)}, u32[]{:S(2)}, u32[]{:S(2)}) collective-permute-start(f32[8,40,128]{2,1,0:T(8,128)S(1)} %shard_map.58.own_ref), channel_id=1, source_target_pairs={{0,32},{32,0},{1,33},{33,1},{2,34},{34,2},{3,35},{35,3},{4,36},{36... | collective-permute-start | bytes 491528 | tf_op jit(solution)/shard_map/ppermute | solution.py:345
  77.6 1.0 collective-permute-done.1.other_ref
  78.6 0.1 shard_map.59
  78.7 16.9 %all_to_all.22 = bf16[32,32,128]{2,1,0:T(8,128)(2,1)S(1)} all-to-all(bf16[32,32,128]{2,1,0:T(8,128)(2,1)S(1)} %shard_map.59), channel_id=1, replica_groups=mesh['y'=8,'core'=2,'zh'=4,'zl'=2,'x'=4] {'y','zh'}, dimensions={0} | all-to-all | bytes 524288 | tf_op jit(solution)/shard_map/all_to_all | solution.py:346
  95.6 0.5 shard_map.60
  96.1 0.0 copy-start
  96.1 1.3 copy-done
  97.4 0.0 copy-start.8
  97.4 3.9 %all-to-all-start.3 = ((bf16[8,1024,128]{2,1,0:T(8,128)(2,1)}), bf16[8,1024,128]{2,1,0:T(8,128)(2,1)S(1)}, u32[]{:S(2)}, u32[]{:S(2)}) async-start(bf16[8,1024,128]{2,1,0:T(8,128)(2,1)} %copy-done), calls=%async_computation.3 | async-start | bytes 4194304 | tf_op jit(solution)/shard_map/all_to_all | solution.py:349
  101.3 0.0 copy-done.8
  101.3 0.0 copy-start.4
  101.3 1.7 %copy-done.4 = bf16[128,9216]{1,0:T(8,128)(2,1)S(1)} copy-done((bf16[128,9216]{1,0:T(8,128)(2,1)S(1)}, bf16[128,9216]{1,0:T(8,128)(2,1)}, u32[]{:S(2)}) %copy-start.4) | copy-done | bytes 2359320
  103.0 7.0 %shard_map.61 = (f32[128,8192]{1,0:T(8,128)S(1)}, bf16[128,512]{1,0:T(8,128)(2,1)S(1)}) custom-call(bf16[128,9216]{1,0:T(8,128)(2,1)S(1)} %copy-done.4, bf16[3,9216]{1,0:T(4,128)(2,1)S(1)} %collective-permute-done.edge_ref, f32[4,9216]{1,0:T(4,128)S(1)} %copy-done.5, f32[384,128]{1,0:T(8,128)S(1)} %get-tuple-element.15.late_ref, f32[1,128]{1,0:T(1,128)S(1)} %bitcast.6), custom_call_target="tpu_custom_call" | custom-call | flops 1000000000 | bytes 8000000 | tf_op jit(solution)/shard_map/pallas_call | solution.py:284
  110.0 0.0 copy-start.1
  110.0 1.9 %copy-done.1 = f32[128,8192]{1,0:T(8,128)} copy-done((f32[128,8192]{1,0:T(8,128)}, f32[128,8192]{1,0:T(8,128)S(1)}, u32[]{:S(2)}) %copy-start.1) | copy-done | bytes 4194328
  111.9 15.3 %all-to-all-done.3.state_ref = bf16[8,1024,128]{2,1,0:T(8,128)(2,1)S(1)} async-done(((bf16[8,1024,128]{2,1,0:T(8,128)(2,1)}), bf16[8,1024,128]{2,1,0:T(8,128)(2,1)S(1)}, u32[]{:S(2)}, u32[]{:S(2)}) %all-to-all-start.3) | async-done | bytes 2097184 | tf_op jit(solution)/shard_map/all_to_all | solution.py:349
  127.2 0.0 copy-start.2
  127.2 2.2 %copy-done.2 = f32[128,8192]{1,0:T(8,128)S(1)} copy-done((f32[128,8192]{1,0:T(8,128)S(1)}, f32[128,8192]{1,0:T(8,128)}, u32[]{:S(2)}) %copy-start.2) | copy-done | bytes 4194328
  129.4 2.2 %shard_map.62 = bf16[128,8192]{1,0:T(8,128)(2,1)} custom-call(bf16[128,512]{1,0:T(8,128)(2,1)S(1)} %get-tuple-element.16.rea_ref, f32[384,128]{1,0:T(8,128)S(1)} %get-tuple-element.15.late_ref, f32[128,8192]{1,0:T(8,128)S(1)} %copy-done.2, bf16[8,1024,128]{2,1,0:T(8,128)(2,1)S(1)} %all-to-all-done.3.state_ref), custom_call_target="tpu_custom_call" | custom-call | flops 100000000 | bytes 2000000 | tf_op jit(solution)/shard_map/pallas_call | solution.py:325
Async XLA Ops:
  0.0 17.3 %copy-start.5 = (f32[4,9216]{1,0:T(4,128)S(1)}, f32[4,9216]{1,0:T(4,128)}, u32[]{:S(2)}) copy-start(f32[4,9216]{1,0:T(4,128)} %w_ref.3) | copy-start | bytes 442372
  1.0 16.3 %collective-permute-start = (bf16[3,9216]{1,0:T(4,128)(2,1)S(1)}, bf16[3,9216]{1,0:T(4,128)(2,1)S(1)}, u32[]{:S(2)}, u32[]{:S(2)}) collective-permute-start(bf16[3,9216]{1,0:T(4,128)(2,1)S(1)} %slice.3), channel_id=1, source_target_pairs={{0,1},{1,2},{2,3},{3,4},{4,5},{5,6},{6,7},{7,8},{8,9},{9,10},{10,1... | collective-permute-start | bytes 165896 | tf_op jit(solution)/shard_map/ppermute | solution.py:339
  4.9 1.7 %copy-start.3 = (bf16[128,9216]{1,0:T(8,128)(2,1)S(1)}, bf16[128,9216]{1,0:T(8,128)(2,1)}, u32[]{:S(2)}) copy-start(bf16[128,9216]{1,0:T(8,128)(2,1)} %in_ref.1) | copy-start | bytes 7077892
  6.6 0.8 copy-start.6
  7.5 0.7 copy-start.7
  71.6 7.0 %collective-permute-start.1 = (f32[8,40,128]{2,1,0:T(8,128)S(1)}, f32[8,40,128]{2,1,0:T(8,128)S(1)}, u32[]{:S(2)}, u32[]{:S(2)}) collective-permute-start(f32[8,40,128]{2,1,0:T(8,128)S(1)} %shard_map.58.own_ref), channel_id=1, source_target_pairs={{0,32},{32,0},{1,33},{33,1},{2,34},{34,2},{3,35},{35,3},{4,36},{36... | collective-permute-start | bytes 491528 | tf_op jit(solution)/shard_map/ppermute | solution.py:345
  96.1 1.3 %copy-start = (bf16[8,1024,128]{2,1,0:T(8,128)(2,1)}, bf16[8,1024,128]{2,1,0:T(8,128)(2,1)S(1)}, u32[]{:S(2)}) copy-start(bf16[8,1024,128]{2,1,0:T(8,128)(2,1)S(1)} %shard_map.60) | copy-start | bytes 6291460
  97.4 3.9 %copy-start.8 = (f32[128]{0:T(128)S(1)}, f32[128]{0:T(128)}, u32[]{:S(2)}) copy-start(f32[128]{0:T(128)} %param.9) | copy-start | bytes 1540
  97.4 29.8 %all-to-all-start.3 = ((bf16[8,1024,128]{2,1,0:T(8,128)(2,1)}), bf16[8,1024,128]{2,1,0:T(8,128)(2,1)S(1)}, u32[]{:S(2)}, u32[]{:S(2)}) async-start(bf16[8,1024,128]{2,1,0:T(8,128)(2,1)} %copy-done), calls=%async_computation.3 | async-start | bytes 4194304 | tf_op jit(solution)/shard_map/all_to_all | solution.py:349
  101.3 1.7 %copy-start.4 = (bf16[128,9216]{1,0:T(8,128)(2,1)S(1)}, bf16[128,9216]{1,0:T(8,128)(2,1)}, u32[]{:S(2)}) copy-start(bf16[128,9216]{1,0:T(8,128)(2,1)} %in_ref.1) | copy-start | bytes 7077892
  110.0 2.0 %copy-start.1 = (f32[128,8192]{1,0:T(8,128)}, f32[128,8192]{1,0:T(8,128)S(1)}, u32[]{:S(2)}) copy-start(f32[128,8192]{1,0:T(8,128)S(1)} %get-tuple-element.17.part_ref) | copy-start | bytes 12582916
  127.2 2.2 %copy-start.2 = (f32[128,8192]{1,0:T(8,128)S(1)}, f32[128,8192]{1,0:T(8,128)}, u32[]{:S(2)}) copy-start(f32[128,8192]{1,0:T(8,128)} %copy-done.1) | copy-start | bytes 12582916

commit v5 on v4

--- a/solution.py
+++ b/solution.py
@@ -105,12 +105,27 @@
     return out.astype(BF16)
 
 
-def state_kernel(in_ref, edge_ref, w_ref, early_ref, pay_ref):
+SLOTS = 4
+
+
+def convolve_by_loads(x_ref, edge_ref, w_ref, at, wide_ref):
+    cols = slice(at, at + 128)
+    wide_ref[8 - KERNEL + 1 : 8] = edge_ref[:, cols].astype(F32)
+    wide_ref[8:] = x_ref[:, cols].astype(F32)
+    out = None
+    for tap in range(KERNEL):
+        first = 8 - KERNEL + 1 + tap
+        term = wide_ref[first : first + TOK] * w_ref[tap : tap + 1, cols]
+        out = term if out is None else out + term
+    return out.astype(BF16)
+
+
+def state_kernel(in_ref, edge_ref, w_ref, early_ref, pay_ref, wide_ref):
     factor = early_ref[:TOK]
     decay = early_ref[TOK:]
     blank = jnp.zeros((TAIL - 3 * NBO, 128), F32)
     for group in range(GROUPS):
-        writers = convolve(in_ref, edge_ref, w_ref, HCOLS + group * STATE).astype(F32).T.astype(BF16)
+        writers = convolve_by_loads(in_ref, edge_ref, w_ref, HCOLS + group * STATE, wide_ref.at[0]).astype(F32).T.astype(BF16)
         for owner in range(group * PER // OWN, (group + 1) * PER // OWN):
             base = owner * OWN
             rows = [lanes_of(decay, base, b, 8)[:1] for b in range(NBO)]
@@ -119,7 +134,9 @@
             for pair in range(NBO // 2):
                 weighted = []
                 for b in (2 * pair, 2 * pair + 1):
-                    value = convolve(in_ref, edge_ref, w_ref, base * HEAD_DIM + b * 128)
+                    value = convolve_by_loads(
+                        in_ref, edge_ref, w_ref, base * HEAD_DIM + b * 128, wide_ref.at[b % SLOTS]
+                    )
                     weighted.append((value.astype(F32) * lanes_of(factor, base, b, TOK)).astype(BF16))
                 state = jnp.dot(writers, jnp.concatenate(weighted, 1), preferred_element_type=F32)
                 for half in range(2):
@@ -133,6 +150,7 @@
         in_specs=[VMEM] * 4,
         out_specs=VMEM,
         out_shape=jax.ShapeDtypeStruct((NEAR, PAY, 128), BF16),
+        scratch_shapes=[pltpu.VMEM((SLOTS, TOK + 8, 128), F32)],
         compiler_params=params(),
         cost_estimate=pl.CostEstimate(flops=10**8, bytes_accessed=3 * 10**6, transcendentals=0),
     )(*args)
@@ -340,14 +358,14 @@
     held, early, late = prep(conv_input, step_raw, decay_log)
     made = states(held, edge, conv_weight, early)
     pays = lax.all_to_all(made, NEAR_AXES, 0, 0, tiled=True)
+    part, readers = local(conv_input, edge, conv_weight, late, skip_gain.reshape(1, HEADS))
+    pays, part, readers = lax.optimization_barrier((pays, part, readers))
     rows = lax.all_to_all(row_total(pays), FAR_AXES, 0, 0, tiled=True)
     own = group_total(rows)
     other = lax.ppermute(own, "core", [(0, 1), (1, 0)])
     entry = lax.all_to_all(scan(core, rows, own, other), FAR_AXES, 0, 0, tiled=True)
     entering = enter(entry.reshape(ROWS, 128), pays)
-    late, entering = lax.optimization_barrier((late, entering))
     state = lax.all_to_all(entering, NEAR_AXES, 0, 0, tiled=True)
-    part, readers = local(conv_input, edge, conv_weight, late, skip_gain.reshape(1, HEADS))
     return final(readers, late, part, state)
 
 

time: 132 us -> 131 us (level)
  the two profiles are of different devices: /device:TPU:1 before, /device:TPU:8 now
where the time goes in v5:
time: 131 us; the launch traced here: 130 us
  blocking collectives  72.4 us (55%)
  waiting for transfers between devices  26.2 us (20%)
  Pallas kernels  13.5 us (10%)
  local copies, waits for them, and re-layouts  9.14 us (7%)
  starting transfers between devices  9.06 us (7%)
    all_to_all x1, blocking collectives, body(): state = lax.all_to_all(entering, NEAR_AXES, 0, 0, tiled=True)  28.8 us
    all_to_all x1, blocking collectives, body(): rows = lax.all_to_all(row_total(pays), FAR_AXES, 0, 0, tiled=True)  24.5 us
    all_to_all x1, blocking collectives, body(): lax.all_to_all(scan(core, rows, own, other), FAR_AXES, 0, 0, tiled=True)  19.2 us
    all_to_all x1, waiting for transfers between devices, body(): pays = lax.all_to_all(made, NEAR_AXES, 0, 0, tiled=True)  17.3 us
    unnamed x18, local copies, waits for them, and re-layouts  8.15 us
    ppermute x1, waiting for transfers between devices, body(): lax.ppermute(conv_input[TOK - KERNEL + 1:], AXES, [(i, i + 1) for i in ra...  7.61 us
    pallas_call x1, Pallas kernels, local(): pl.pallas_call(local_kernel, in_specs=[VMEM] * 5, out_specs=[VMEM] * 2, o...  6.97 us
    all_to_all x1, starting transfers between devices, body(): pays = lax.all_to_all(made, NEAR_AXES, 0, 0, tiled=True)  3.74 us
  transfers between devices with their start and end apart: 3, of which 3 were waited for; matrix products, arithmetic and copies ran while one was open for 0% of the time, Pallas kernels for 6%

profile of v5, /device:TPU:8, one launch (start us, length us, event | category | flops | bytes accessed | tf_op | source)
XLA Modules:
  0.0 130.5 jit_solution(15882512641839165644)
XLA Ops:
  0.0 0.0 copy-start.5
  0.0 1.0 slice.3
  1.0 3.4 %collective-permute-start = (bf16[3,9216]{1,0:T(4,128)(2,1)S(1)}, bf16[3,9216]{1,0:T(4,128)(2,1)S(1)}, u32[]{:S(2)}, u32[]{:S(2)}) collective-permute-start(bf16[3,9216]{1,0:T(4,128)(2,1)S(1)} %slice.3), channel_id=1, source_target_pairs={{0,1},{1,2},{2,3},{3,4},{4,5},{5,6},{6,7},{7,8},{8,9},{9,10},{10,1... | collective-permute-start | bytes 165896 | tf_op jit(solution)/shard_map/ppermute | solution.py:357
  4.4 0.0 copy-start.3
  4.4 1.7 %copy-done.3 = bf16[128,9216]{1,0:T(8,128)(2,1)S(1)} copy-done((bf16[128,9216]{1,0:T(8,128)(2,1)S(1)}, bf16[128,9216]{1,0:T(8,128)(2,1)}, u32[]{:S(2)}) %copy-start.3) | copy-done | bytes 2359320
  6.1 0.0 copy-start.6
  6.1 0.8 copy-done.6
  6.9 0.0 copy-start.7
  6.9 0.7 copy-done.7
  7.6 0.3 shard_map.55
  7.9 7.6 %collective-permute-done.edge_ref = bf16[3,9216]{1,0:T(4,128)(2,1)S(1)} collective-permute-done((bf16[3,9216]{1,0:T(4,128)(2,1)S(1)}, bf16[3,9216]{1,0:T(4,128)(2,1)S(1)}, u32[]{:S(2)}, u32[]{:S(2)}) %collective-permute-start) | collective-permute-done | bytes 55328 | tf_op jit(solution)/shard_map/ppermute | solution.py:357
  15.5 0.0 copy-done.5
  15.5 3.0 %shard_map.56 = bf16[8,1056,128]{2,1,0:T(8,128)(2,1)S(1)} custom-call(bf16[128,9216]{1,0:T(8,128)(2,1)S(1)} %get-tuple-element.13.in_ref, bf16[3,9216]{1,0:T(4,128)(2,1)S(1)} %collective-permute-done.edge_ref, f32[4,9216]{1,0:T(4,128)S(1)} %copy-done.5, f32[136,128]{1,0:T(8,128)S(1)} %get-tuple-element.14.early_ref), custom_call_target="tpu_custom_call" | custom-call | flops 100000000 | bytes 3000000 | tf_op jit(solution)/shard_map/pallas_call | solution.py:148
  18.5 0.0 copy-start
  18.5 1.4 %copy-done = bf16[8,1056,128]{2,1,0:T(8,128)(2,1)} copy-done((bf16[8,1056,128]{2,1,0:T(8,128)(2,1)}, bf16[8,1056,128]{2,1,0:T(8,128)(2,1)S(1)}, u32[]{:S(2)}) %copy-start) | copy-done | bytes 2162712
  19.9 0.0 copy-start.8
  19.9 3.7 %all-to-all-start = ((bf16[8,1056,128]{2,1,0:T(8,128)(2,1)}), bf16[8,1056,128]{2,1,0:T(8,128)(2,1)S(1)}, u32[]{:S(2)}, u32[]{:S(2)}) async-start(bf16[8,1056,128]{2,1,0:T(8,128)(2,1)} %copy-done), calls=%async_computation | async-start | bytes 4325376 | tf_op jit(solution)/shard_map/all_to_all | solution.py:360
  23.6 0.0 copy-done.8
  23.6 0.0 copy-start.4
  23.6 1.7 %copy-done.4 = bf16[128,9216]{1,0:T(8,128)(2,1)S(1)} copy-done((bf16[128,9216]{1,0:T(8,128)(2,1)S(1)}, bf16[128,9216]{1,0:T(8,128)(2,1)}, u32[]{:S(2)}) %copy-start.4) | copy-done | bytes 2359320
  25.3 7.0 %shard_map.57 = (f32[128,8192]{1,0:T(8,128)S(1)}, bf16[128,512]{1,0:T(8,128)(2,1)S(1)}) custom-call(bf16[128,9216]{1,0:T(8,128)(2,1)S(1)} %copy-done.4, bf16[3,9216]{1,0:T(4,128)(2,1)S(1)} %collective-permute-done.edge_ref, f32[4,9216]{1,0:T(4,128)S(1)} %copy-done.5, f32[384,128]{1,0:T(8,128)S(1)} %get-tuple-element.15.late_ref, f32[1,128]{1,0:T(1,128)S(1)} %bitcast.6), custom_call_target="tpu_custom_call" | custom-call | flops 1000000000 | bytes 8000000 | tf_op jit(solution)/shard_map/pallas_call | solution.py:302
  32.3 0.0 copy-start.1
  32.3 1.9 %copy-done.1 = f32[128,8192]{1,0:T(8,128)} copy-done((f32[128,8192]{1,0:T(8,128)}, f32[128,8192]{1,0:T(8,128)S(1)}, u32[]{:S(2)}) %copy-start.1) | copy-done | bytes 4194328
  34.2 17.3 %all-to-all-done.pay_ref = bf16[8,1056,128]{2,1,0:T(8,128)(2,1)S(1)} async-done(((bf16[8,1056,128]{2,1,0:T(8,128)(2,1)}), bf16[8,1056,128]{2,1,0:T(8,128)(2,1)S(1)}, u32[]{:S(2)}, u32[]{:S(2)}) %all-to-all-start) | async-done | bytes 2162720 | tf_op jit(solution)/shard_map/all_to_all | solution.py:360
  51.5 0.4 shard_map.58
  51.9 24.5 %all_to_all.20.rows_ref = bf16[32,40,128]{2,1,0:T(8,128)(2,1)S(1)} all-to-all(bf16[32,40,128]{2,1,0:T(8,128)(2,1)S(1)} %shard_map.58), channel_id=1, replica_groups=mesh['y'=8,'core'=2,'zh'=4,'zl'=2,'x'=4] {'y','zh'}, dimensions={0} | all-to-all | bytes 655360 | tf_op jit(solution)/shard_map/all_to_all | solution.py:363
  76.4 0.1 shard_map.59.own_ref
  76.5 1.9 %collective-permute-start.1 = (f32[8,40,128]{2,1,0:T(8,128)S(1)}, f32[8,40,128]{2,1,0:T(8,128)S(1)}, u32[]{:S(2)}, u32[]{:S(2)}) collective-permute-start(f32[8,40,128]{2,1,0:T(8,128)S(1)} %shard_map.59.own_ref), channel_id=1, source_target_pairs={{0,32},{32,0},{1,33},{33,1},{2,34},{34,2},{3,35},{35,3},{4,36},{36... | collective-permute-start | bytes 491528 | tf_op jit(solution)/shard_map/ppermute | solution.py:365
  78.4 1.4 %collective-permute-done.1.other_ref = f32[8,40,128]{2,1,0:T(8,128)S(1)} collective-permute-done((f32[8,40,128]{2,1,0:T(8,128)S(1)}, f32[8,40,128]{2,1,0:T(8,128)S(1)}, u32[]{:S(2)}, u32[]{:S(2)}) %collective-permute-start.1) | collective-permute-done | bytes 163872 | tf_op jit(solution)/shard_map/ppermute | solution.py:365
  79.8 0.1 shard_map.60
  79.9 19.2 %all_to_all.21 = bf16[32,32,128]{2,1,0:T(8,128)(2,1)S(1)} all-to-all(bf16[32,32,128]{2,1,0:T(8,128)(2,1)S(1)} %shard_map.60), channel_id=1, replica_groups=mesh['y'=8,'core'=2,'zh'=4,'zl'=2,'x'=4] {'y','zh'}, dimensions={0} | all-to-all | bytes 524288 | tf_op jit(solution)/shard_map/all_to_all | solution.py:366
  99.1 0.5 shard_map.61
  99.5 0.0 copy-start.2
  99.5 28.8 %all_to_all.22.state_ref = bf16[8,1024,128]{2,1,0:T(8,128)(2,1)S(1)} all-to-all(bf16[8,1024,128]{2,1,0:T(8,128)(2,1)S(1)} %shard_map.61), channel_id=1, replica_groups=mesh['y'=8,'core'=2,'zh'=4,'zl'=2,'x'=4] {'zl','x'}, dimensions={0} | all-to-all | bytes 4194304 | tf_op jit(solution)/shard_map/all_to_all | solution.py:368
  128.3 0.0 copy-done.2
  128.3 2.2 %shard_map.62 = bf16[128,8192]{1,0:T(8,128)(2,1)} custom-call(bf16[128,512]{1,0:T(8,128)(2,1)S(1)} %get-tuple-element.18.rea_ref, f32[384,128]{1,0:T(8,128)S(1)} %get-tuple-element.15.late_ref, f32[128,8192]{1,0:T(8,128)S(1)} %copy-done.2, bf16[8,1024,128]{2,1,0:T(8,128)(2,1)S(1)} %all_to_all.22.state_ref), custom_call_target="tpu_custom_call" | custom-call | flops 100000000 | bytes 2000000 | tf_op jit(solution)/shard_map/pallas_call | solution.py:343
Async XLA Ops:
  0.0 15.5 %copy-start.5 = (f32[4,9216]{1,0:T(4,128)S(1)}, f32[4,9216]{1,0:T(4,128)}, u32[]{:S(2)}) copy-start(f32[4,9216]{1,0:T(4,128)} %w_ref.3) | copy-start | bytes 442372
  1.0 14.5 %collective-permute-start = (bf16[3,9216]{1,0:T(4,128)(2,1)S(1)}, bf16[3,9216]{1,0:T(4,128)(2,1)S(1)}, u32[]{:S(2)}, u32[]{:S(2)}) collective-permute-start(bf16[3,9216]{1,0:T(4,128)(2,1)S(1)} %slice.3), channel_id=1, source_target_pairs={{0,1},{1,2},{2,3},{3,4},{4,5},{5,6},{6,7},{7,8},{8,9},{9,10},{10,1... | collective-permute-start | bytes 165896 | tf_op jit(solution)/shard_map/ppermute | solution.py:357
  4.4 1.7 %copy-start.3 = (bf16[128,9216]{1,0:T(8,128)(2,1)S(1)}, bf16[128,9216]{1,0:T(8,128)(2,1)}, u32[]{:S(2)}) copy-start(bf16[128,9216]{1,0:T(8,128)(2,1)} %in_ref.1) | copy-start | bytes 7077892
  6.1 0.8 copy-start.6
  6.9 0.7 copy-start.7
  18.5 1.4 %copy-start = (bf16[8,1056,128]{2,1,0:T(8,128)(2,1)}, bf16[8,1056,128]{2,1,0:T(8,128)(2,1)S(1)}, u32[]{:S(2)}) copy-start(bf16[8,1056,128]{2,1,0:T(8,128)(2,1)S(1)} %shard_map.56) | copy-start | bytes 6488068
  19.9 3.7 %copy-start.8 = (f32[128]{0:T(128)S(1)}, f32[128]{0:T(128)}, u32[]{:S(2)}) copy-start(f32[128]{0:T(128)} %param.9) | copy-start | bytes 1540
  19.9 31.6 %all-to-all-start = ((bf16[8,1056,128]{2,1,0:T(8,128)(2,1)}), bf16[8,1056,128]{2,1,0:T(8,128)(2,1)S(1)}, u32[]{:S(2)}, u32[]{:S(2)}) async-start(bf16[8,1056,128]{2,1,0:T(8,128)(2,1)} %copy-done), calls=%async_computation | async-start | bytes 4325376 | tf_op jit(solution)/shard_map/all_to_all | solution.py:360
  23.6 1.7 %copy-start.4 = (bf16[128,9216]{1,0:T(8,128)(2,1)S(1)}, bf16[128,9216]{1,0:T(8,128)(2,1)}, u32[]{:S(2)}) copy-start(bf16[128,9216]{1,0:T(8,128)(2,1)} %in_ref.1) | copy-start | bytes 7077892
  32.3 2.0 %copy-start.1 = (f32[128,8192]{1,0:T(8,128)}, f32[128,8192]{1,0:T(8,128)S(1)}, u32[]{:S(2)}) copy-start(f32[128,8192]{1,0:T(8,128)S(1)} %get-tuple-element.19.part_ref) | copy-start | bytes 12582916
  76.5 3.3 %collective-permute-start.1 = (f32[8,40,128]{2,1,0:T(8,128)S(1)}, f32[8,40,128]{2,1,0:T(8,128)S(1)}, u32[]{:S(2)}, u32[]{:S(2)}) collective-permute-start(f32[8,40,128]{2,1,0:T(8,128)S(1)} %shard_map.59.own_ref), channel_id=1, source_target_pairs={{0,32},{32,0},{1,33},{33,1},{2,34},{34,2},{3,35},{35,3},{4,36},{36... | collective-permute-start | bytes 491528 | tf_op jit(solution)/shard_map/ppermute | solution.py:365
  99.5 28.8 %copy-start.2 = (f32[128,8192]{1,0:T(8,128)S(1)}, f32[128,8192]{1,0:T(8,128)}, u32[]{:S(2)}) copy-start(f32[128,8192]{1,0:T(8,128)} %copy-done.1) | copy-start | bytes 12582916

commit v6 on v5

--- a/solution.py
+++ b/solution.py
@@ -358,9 +358,10 @@
     held, early, late = prep(conv_input, step_raw, decay_log)
     made = states(held, edge, conv_weight, early)
     pays = lax.all_to_all(made, NEAR_AXES, 0, 0, tiled=True)
+    late, pays = lax.optimization_barrier((late, pays))
+    rows = lax.all_to_all(row_total(pays), FAR_AXES, 0, 0, tiled=True)
     part, readers = local(conv_input, edge, conv_weight, late, skip_gain.reshape(1, HEADS))
-    pays, part, readers = lax.optimization_barrier((pays, part, readers))
-    rows = lax.all_to_all(row_total(pays), FAR_AXES, 0, 0, tiled=True)
+    rows, part, readers = lax.optimization_barrier((rows, part, readers))
     own = group_total(rows)
     other = lax.ppermute(own, "core", [(0, 1), (1, 0)])
     entry = lax.all_to_all(scan(core, rows, own, other), FAR_AXES, 0, 0, tiled=True)

time: 131 us -> 132 us (level)
  waiting for transfers between devices: 26.2 us -> 12.7 us
  blocking collectives: 72.4 us -> 82.8 us
  starting transfers between devices: 9.06 us -> 14.4 us
  local copies, waits for them, and re-layouts: 9.14 us -> 7.76 us
    all_to_all x1, waiting for transfers between devices: 17.3 us -> 3.77 us  [body(): rows = lax.all_to_all(row_total(pays), FAR_AXES, 0, 0, tiled=True)]
    all_to_all x1, blocking collectives: 24.5 us -> 31.7 us  [body(): pays = lax.all_to_all(made, NEAR_AXES, 0, 0, tiled=True)]
    all_to_all x1, starting transfers between devices: 3.74 us -> 9.05 us  [body(): rows = lax.all_to_all(row_total(pays), FAR_AXES, 0, 0, tiled=True)]
    all_to_all x1, blocking collectives: 19.2 us -> 23 us  [body(): lax.all_to_all(scan(core, rows, own, other), FAR_AXES, 0, 0, tiled=True)]
    unnamed x18 -> x16, local copies, waits for them, and re-layouts: 8.15 us -> 6.77 us
where the time goes in v6:
time: 132 us
  blocking collectives  82.8 us (63%)
  starting transfers between devices  14.4 us (11%)
  Pallas kernels  14.3 us (11%)
  waiting for transfers between devices  12.7 us (10%)
  local copies, waits for them, and re-layouts  7.76 us (6%)
    all_to_all x1, blocking collectives, body(): pays = lax.all_to_all(made, NEAR_AXES, 0, 0, tiled=True)  31.7 us
    all_to_all x1, blocking collectives, body(): state = lax.all_to_all(entering, NEAR_AXES, 0, 0, tiled=True)  28 us
    all_to_all x1, blocking collectives, body(): lax.all_to_all(scan(core, rows, own, other), FAR_AXES, 0, 0, tiled=True)  23 us
    all_to_all x1, starting transfers between devices, body(): rows = lax.all_to_all(row_total(pays), FAR_AXES, 0, 0, tiled=True)  9.05 us
    ppermute x1, waiting for transfers between devices, body(): lax.ppermute(conv_input[TOK - KERNEL + 1:], AXES, [(i, i + 1) for i in ra...  7.61 us
    pallas_call x1, Pallas kernels, local(): pl.pallas_call(local_kernel, in_specs=[VMEM] * 5, out_specs=[VMEM] * 2, o...  6.97 us
    unnamed x16, local copies, waits for them, and re-layouts  6.77 us
    all_to_all x1, waiting for transfers between devices, body(): rows = lax.all_to_all(row_total(pays), FAR_AXES, 0, 0, tiled=True)  3.77 us
  transfers between devices with their start and end apart: 3, of which 3 were waited for; matrix products, arithmetic and copies ran while one was open for 0% of the time, Pallas kernels for 6%

profile of v6, /device:TPU:8, one launch (start us, length us, event | category | flops | bytes accessed | tf_op | source)
XLA Modules:
  0.0 132.0 jit_solution(18123315855879514311)
XLA Ops:
  0.0 0.0 copy-start.4
  0.0 1.0 slice.3
  1.0 3.4 %collective-permute-start = (bf16[3,9216]{1,0:T(4,128)(2,1)S(1)}, bf16[3,9216]{1,0:T(4,128)(2,1)S(1)}, u32[]{:S(2)}, u32[]{:S(2)}) collective-permute-start(bf16[3,9216]{1,0:T(4,128)(2,1)S(1)} %slice.3), channel_id=1, source_target_pairs={{0,1},{1,2},{2,3},{3,4},{4,5},{5,6},{6,7},{7,8},{8,9},{9,10},{10,1... | collective-permute-start | bytes 165896 | tf_op jit(solution)/shard_map/ppermute | solution.py:357
  4.4 0.0 copy-start.2
  4.4 1.7 %copy-done.2 = bf16[128,9216]{1,0:T(8,128)(2,1)S(1)} copy-done((bf16[128,9216]{1,0:T(8,128)(2,1)S(1)}, bf16[128,9216]{1,0:T(8,128)(2,1)}, u32[]{:S(2)}) %copy-start.2) | copy-done | bytes 2359320
  6.1 0.0 copy-start.5
  6.1 0.8 copy-done.5
  6.9 0.0 copy-start.6
  6.9 0.7 copy-done.6
  7.6 0.3 shard_map.55
  7.9 7.6 %collective-permute-done.edge_ref = bf16[3,9216]{1,0:T(4,128)(2,1)S(1)} collective-permute-done((bf16[3,9216]{1,0:T(4,128)(2,1)S(1)}, bf16[3,9216]{1,0:T(4,128)(2,1)S(1)}, u32[]{:S(2)}, u32[]{:S(2)}) %collective-permute-start) | collective-permute-done | bytes 55328 | tf_op jit(solution)/shard_map/ppermute | solution.py:357
  15.5 0.0 copy-done.4
  15.5 3.1 %shard_map.56 = bf16[8,1056,128]{2,1,0:T(8,128)(2,1)S(1)} custom-call(bf16[128,9216]{1,0:T(8,128)(2,1)S(1)} %get-tuple-element.16.in_ref, bf16[3,9216]{1,0:T(4,128)(2,1)S(1)} %collective-permute-done.edge_ref, f32[4,9216]{1,0:T(4,128)S(1)} %copy-done.4, f32[136,128]{1,0:T(8,128)S(1)} %get-tuple-element.17.early_ref), custom_call_target="tpu_custom_call" | custom-call | flops 100000000 | bytes 3000000 | tf_op jit(solution)/shard_map/pallas_call | solution.py:148
  18.6 31.7 %all_to_all.20.pay_ref = bf16[8,1056,128]{2,1,0:T(8,128)(2,1)S(1)} all-to-all(bf16[8,1056,128]{2,1,0:T(8,128)(2,1)S(1)} %shard_map.56), channel_id=1, replica_groups=mesh['y'=8,'core'=2,'zh'=4,'zl'=2,'x'=4] {'zl','x'}, dimensions={0} | all-to-all | bytes 4325376 | tf_op jit(solution)/shard_map/all_to_all | solution.py:360
  50.3 0.0 copy-start.7
  50.3 1.1 shard_map.57
  51.4 9.1 %all-to-all-start.1 = ((bf16[32,40,128]{2,1,0:T(8,128)(2,1)}), bf16[32,40,128]{2,1,0:T(8,128)(2,1)S(1)}, u32[]{:S(2)}, u32[]{:S(2)}) async-start(bf16[32,40,128]{2,1,0:T(8,128)(2,1)} %shard_map.57), calls=%async_computation.1 | async-start | bytes 655360 | tf_op jit(solution)/shard_map/all_to_all | solution.py:362
  60.5 0.0 copy-done.7
  60.5 0.0 copy-start.3
  60.5 1.7 %copy-done.3 = bf16[128,9216]{1,0:T(8,128)(2,1)S(1)} copy-done((bf16[128,9216]{1,0:T(8,128)(2,1)S(1)}, bf16[128,9216]{1,0:T(8,128)(2,1)}, u32[]{:S(2)}) %copy-start.3) | copy-done | bytes 2359320
  62.2 7.0 %shard_map.58 = (f32[128,8192]{1,0:T(8,128)S(1)}, bf16[128,512]{1,0:T(8,128)(2,1)S(1)}) custom-call(bf16[128,9216]{1,0:T(8,128)(2,1)S(1)} %copy-done.3, bf16[3,9216]{1,0:T(4,128)(2,1)S(1)} %collective-permute-done.edge_ref, f32[4,9216]{1,0:T(4,128)S(1)} %copy-done.4, f32[384,128]{1,0:T(8,128)S(1)} %get-tuple-element.19.late_ref, f32[1,128]{1,0:T(1,128)S(1)} %bitcast.6), custom_call_target="tpu_custom_call" | custom-call | flops 1000000000 | bytes 8000000 | tf_op jit(solution)/shard_map/pallas_call | solution.py:302
  69.1 0.0 copy-start
  69.1 1.9 %copy-done = f32[128,8192]{1,0:T(8,128)} copy-done((f32[128,8192]{1,0:T(8,128)}, f32[128,8192]{1,0:T(8,128)S(1)}, u32[]{:S(2)}) %copy-start) | copy-done | bytes 4194328
  71.1 3.8 %all-to-all-done.1.rows_ref = bf16[32,40,128]{2,1,0:T(8,128)(2,1)S(1)} async-done(((bf16[32,40,128]{2,1,0:T(8,128)(2,1)}), bf16[32,40,128]{2,1,0:T(8,128)(2,1)S(1)}, u32[]{:S(2)}, u32[]{:S(2)}) %all-to-all-start.1) | async-done | bytes 327712 | tf_op jit(solution)/shard_map/all_to_all | solution.py:362
  74.9 0.1 shard_map.59.own_ref
  74.9 1.9 %collective-permute-start.1 = (f32[8,40,128]{2,1,0:T(8,128)S(1)}, f32[8,40,128]{2,1,0:T(8,128)S(1)}, u32[]{:S(2)}, u32[]{:S(2)}) collective-permute-start(f32[8,40,128]{2,1,0:T(8,128)S(1)} %shard_map.59.own_ref), channel_id=1, source_target_pairs={{0,32},{32,0},{1,33},{33,1},{2,34},{34,2},{3,35},{35,3},{4,36},{36... | collective-permute-start | bytes 491528 | tf_op jit(solution)/shard_map/ppermute | solution.py:366
  76.9 1.4 %collective-permute-done.1.other_ref = f32[8,40,128]{2,1,0:T(8,128)S(1)} collective-permute-done((f32[8,40,128]{2,1,0:T(8,128)S(1)}, f32[8,40,128]{2,1,0:T(8,128)S(1)}, u32[]{:S(2)}, u32[]{:S(2)}) %collective-permute-start.1) | collective-permute-done | bytes 163872 | tf_op jit(solution)/shard_map/ppermute | solution.py:366
  78.2 0.1 shard_map.60
  78.3 23.0 %all_to_all.21 = bf16[32,32,128]{2,1,0:T(8,128)(2,1)S(1)} all-to-all(bf16[32,32,128]{2,1,0:T(8,128)(2,1)S(1)} %shard_map.60), channel_id=1, replica_groups=mesh['y'=8,'core'=2,'zh'=4,'zl'=2,'x'=4] {'y','zh'}, dimensions={0} | all-to-all | bytes 524288 | tf_op jit(solution)/shard_map/all_to_all | solution.py:367
  101.4 0.5 shard_map.61
  101.8 0.0 copy-start.1
  101.8 28.0 %all_to_all.22.state_ref = bf16[8,1024,128]{2,1,0:T(8,128)(2,1)S(1)} all-to-all(bf16[8,1024,128]{2,1,0:T(8,128)(2,1)S(1)} %shard_map.61), channel_id=1, replica_groups=mesh['y'=8,'core'=2,'zh'=4,'zl'=2,'x'=4] {'zl','x'}, dimensions={0} | all-to-all | bytes 4194304 | tf_op jit(solution)/shard_map/all_to_all | solution.py:369
  129.8 0.0 copy-done.1
  129.8 2.2 %shard_map.62 = bf16[128,8192]{1,0:T(8,128)(2,1)} custom-call(bf16[128,512]{1,0:T(8,128)(2,1)S(1)} %get-tuple-element.22.rea_ref, f32[384,128]{1,0:T(8,128)S(1)} %get-tuple-element.19.late_ref, f32[128,8192]{1,0:T(8,128)S(1)} %copy-done.1, bf16[8,1024,128]{2,1,0:T(8,128)(2,1)S(1)} %all_to_all.22.state_ref), custom_call_target="tpu_custom_call" | custom-call | flops 100000000 | bytes 2000000 | tf_op jit(solution)/shard_map/pallas_call | solution.py:343
Async XLA Ops:
  0.0 15.5 %copy-start.4 = (f32[4,9216]{1,0:T(4,128)S(1)}, f32[4,9216]{1,0:T(4,128)}, u32[]{:S(2)}) copy-start(f32[4,9216]{1,0:T(4,128)} %w_ref.3) | copy-start | bytes 442372
  1.0 14.5 %collective-permute-start = (bf16[3,9216]{1,0:T(4,128)(2,1)S(1)}, bf16[3,9216]{1,0:T(4,128)(2,1)S(1)}, u32[]{:S(2)}, u32[]{:S(2)}) collective-permute-start(bf16[3,9216]{1,0:T(4,128)(2,1)S(1)} %slice.3), channel_id=1, source_target_pairs={{0,1},{1,2},{2,3},{3,4},{4,5},{5,6},{6,7},{7,8},{8,9},{9,10},{10,1... | collective-permute-start | bytes 165896 | tf_op jit(solution)/shard_map/ppermute | solution.py:357
  4.4 1.7 %copy-start.2 = (bf16[128,9216]{1,0:T(8,128)(2,1)S(1)}, bf16[128,9216]{1,0:T(8,128)(2,1)}, u32[]{:S(2)}) copy-start(bf16[128,9216]{1,0:T(8,128)(2,1)} %in_ref.1) | copy-start | bytes 7077892
  6.1 0.8 copy-start.5
  6.9 0.7 copy-start.6
  50.3 10.2 %copy-start.7 = (f32[128]{0:T(128)S(1)}, f32[128]{0:T(128)}, u32[]{:S(2)}) copy-start(f32[128]{0:T(128)} %param.9) | copy-start | bytes 1540
  51.4 23.4 %all-to-all-start.1 = ((bf16[32,40,128]{2,1,0:T(8,128)(2,1)}), bf16[32,40,128]{2,1,0:T(8,128)(2,1)S(1)}, u32[]{:S(2)}, u32[]{:S(2)}) async-start(bf16[32,40,128]{2,1,0:T(8,128)(2,1)} %shard_map.57), calls=%async_computation.1 | async-start | bytes 655360 | tf_op jit(solution)/shard_map/all_to_all | solution.py:362
  60.5 1.7 %copy-start.3 = (bf16[128,9216]{1,0:T(8,128)(2,1)S(1)}, bf16[128,9216]{1,0:T(8,128)(2,1)}, u32[]{:S(2)}) copy-start(bf16[128,9216]{1,0:T(8,128)(2,1)} %in_ref.1) | copy-start | bytes 7077892
  69.1 2.0 %copy-start = (f32[128,8192]{1,0:T(8,128)}, f32[128,8192]{1,0:T(8,128)S(1)}, u32[]{:S(2)}) copy-start(f32[128,8192]{1,0:T(8,128)S(1)} %get-tuple-element.23.part_ref) | copy-start | bytes 12582916
  74.9 3.3 %collective-permute-start.1 = (f32[8,40,128]{2,1,0:T(8,128)S(1)}, f32[8,40,128]{2,1,0:T(8,128)S(1)}, u32[]{:S(2)}, u32[]{:S(2)}) collective-permute-start(f32[8,40,128]{2,1,0:T(8,128)S(1)} %shard_map.59.own_ref), channel_id=1, source_target_pairs={{0,32},{32,0},{1,33},{33,1},{2,34},{34,2},{3,35},{35,3},{4,36},{36... | collective-permute-start | bytes 491528 | tf_op jit(solution)/shard_map/ppermute | solution.py:366
  101.8 28.0 %copy-start.1 = (f32[128,8192]{1,0:T(8,128)S(1)}, f32[128,8192]{1,0:T(8,128)}, u32[]{:S(2)}) copy-start(f32[128,8192]{1,0:T(8,128)} %copy-done) | copy-start | bytes 12582916

commit v7 on v6

--- a/solution.py
+++ b/solution.py
@@ -265,7 +265,7 @@
     )(entry, pays)
 
 
-def local_kernel(in_ref, edge_ref, w_ref, late_ref, gain_ref, out_ref, rea_ref):
+def local_kernel(in_ref, edge_ref, w_ref, late_ref, gain_ref, out_ref, rea_ref, wide_ref):
     cum = late_ref[:TOK]
     gain = jnp.broadcast_to(gain_ref[...], (8, HEADS))
     row = lax.broadcasted_iota(jnp.int32, (TOK, TOK), 0)
@@ -274,8 +274,10 @@
     first = col < HEAD_DIM
     for group in range(GROUPS):
         base = group * PER
-        writers = convolve(in_ref, edge_ref, w_ref, HCOLS + group * STATE)
-        readers = convolve(in_ref, edge_ref, w_ref, HCOLS + (GROUPS + group) * STATE)
+        writers = convolve_by_loads(in_ref, edge_ref, w_ref, HCOLS + group * STATE, wide_ref.at[0])
+        readers = convolve_by_loads(
+            in_ref, edge_ref, w_ref, HCOLS + (GROUPS + group) * STATE, wide_ref.at[1]
+        )
         rea_ref[:, group * STATE : (group + 1) * STATE] = readers
         affinity = lax.dot_general(
             readers, writers, (((1,), (1,)), ((), ())), preferred_element_type=F32
@@ -290,7 +292,7 @@
                 weight = jnp.exp(span) * step_t[h : h + 1]
                 scores.append((weight * affinity).astype(BF16))
             at = base * HEAD_DIM + b * 128
-            value = convolve(in_ref, edge_ref, w_ref, at)
+            value = convolve_by_loads(in_ref, edge_ref, w_ref, at, wide_ref.at[b % SLOTS])
             zero = jnp.zeros_like(value)
             apart = jnp.concatenate([jnp.where(first, value, zero), jnp.where(first, zero, value)], 0)
             local = jnp.dot(jnp.concatenate(scores, 1), apart, preferred_element_type=F32)
@@ -307,6 +309,7 @@
             jax.ShapeDtypeStruct((TOK, HCOLS), F32),
             jax.ShapeDtypeStruct((TOK, GROUPS * STATE), BF16),
         ],
+        scratch_shapes=[pltpu.VMEM((SLOTS, TOK + 8, 128), F32)],
         compiler_params=params(),
         cost_estimate=pl.CostEstimate(flops=10**9, bytes_accessed=8 * 10**6, transcendentals=0),
     )(*args)

time: 132 us -> 130 us (0.985)
  Pallas kernels: 14.3 us -> 12.3 us
  blocking collectives: 82.8 us -> 80.8 us
  waiting for transfers between devices: 12.7 us -> 14.7 us
    all_to_all x1, waiting for transfers between devices: 3.77 us -> 5.74 us  [body(): rows = lax.all_to_all(row_total(pays), FAR_AXES, 0, 0, tiled=True)]
    pallas_call x1, Pallas kernels: 6.97 us -> 5 us  [local(): pl.pallas_call(local_kernel, in_specs=[VMEM] * 5, out_specs=[VMEM] * 2, o...]
    all_to_all x1, blocking collectives: 23 us -> 21.1 us  [body(): lax.all_to_all(scan(core, rows, own, other), FAR_AXES, 0, 0, tiled=True)]
  transfers between devices with their start and end apart: 3 -> 3, of which waited for: 3 -> 3; matrix products, arithmetic and copies ran while one was open for 0% -> 0% of each run, Pallas kernels for 6% -> 4%
where the time goes in v7:
time: 130 us
  blocking collectives  80.8 us (62%)
  waiting for transfers between devices  14.7 us (11%)
  starting transfers between devices  14.4 us (11%)
  Pallas kernels  12.3 us (9%)
  local copies, waits for them, and re-layouts  7.75 us (6%)
    all_to_all x1, blocking collectives, body(): pays = lax.all_to_all(made, NEAR_AXES, 0, 0, tiled=True)  31.7 us
    all_to_all x1, blocking collectives, body(): state = lax.all_to_all(entering, NEAR_AXES, 0, 0, tiled=True)  28 us
    all_to_all x1, blocking collectives, body(): lax.all_to_all(scan(core, rows, own, other), FAR_AXES, 0, 0, tiled=True)  21.1 us
    all_to_all x1, starting transfers between devices, body(): rows = lax.all_to_all(row_total(pays), FAR_AXES, 0, 0, tiled=True)  9.05 us
    ppermute x1, waiting for transfers between devices, body(): lax.ppermute(conv_input[TOK - KERNEL + 1:], AXES, [(i, i + 1) for i in ra...  7.61 us
    unnamed x16, local copies, waits for them, and re-layouts  6.77 us
    all_to_all x1, waiting for transfers between devices, body(): rows = lax.all_to_all(row_total(pays), FAR_AXES, 0, 0, tiled=True)  5.74 us
    pallas_call x1, Pallas kernels, local(): pl.pallas_call(local_kernel, in_specs=[VMEM] * 5, out_specs=[VMEM] * 2, o...  5 us
  transfers between devices with their start and end apart: 3, of which 3 were waited for; matrix products, arithmetic and copies ran while one was open for 0% of the time, Pallas kernels for 4%

profile of v7, /device:TPU:8, one launch (start us, length us, event | category | flops | bytes accessed | tf_op | source)
XLA Modules:
  0.0 130.1 jit_solution(15230604574776608683)
XLA Ops:
  0.0 0.0 copy-start.4
  0.0 1.0 slice.3
  1.0 3.4 %collective-permute-start = (bf16[3,9216]{1,0:T(4,128)(2,1)S(1)}, bf16[3,9216]{1,0:T(4,128)(2,1)S(1)}, u32[]{:S(2)}, u32[]{:S(2)}) collective-permute-start(bf16[3,9216]{1,0:T(4,128)(2,1)S(1)} %slice.3), channel_id=1, source_target_pairs={{0,1},{1,2},{2,3},{3,4},{4,5},{5,6},{6,7},{7,8},{8,9},{9,10},{10,1... | collective-permute-start | bytes 165896 | tf_op jit(solution)/shard_map/ppermute | solution.py:360
  4.4 0.0 copy-start.2
  4.4 1.7 %copy-done.2 = bf16[128,9216]{1,0:T(8,128)(2,1)S(1)} copy-done((bf16[128,9216]{1,0:T(8,128)(2,1)S(1)}, bf16[128,9216]{1,0:T(8,128)(2,1)}, u32[]{:S(2)}) %copy-start.2) | copy-done | bytes 2359320
  6.1 0.0 copy-start.5
  6.1 0.8 copy-done.5
  6.9 0.0 copy-start.6
  6.9 0.7 copy-done.6
  7.6 0.3 shard_map.55
  7.9 7.6 %collective-permute-done.edge_ref = bf16[3,9216]{1,0:T(4,128)(2,1)S(1)} collective-permute-done((bf16[3,9216]{1,0:T(4,128)(2,1)S(1)}, bf16[3,9216]{1,0:T(4,128)(2,1)S(1)}, u32[]{:S(2)}, u32[]{:S(2)}) %collective-permute-start) | collective-permute-done | bytes 55328 | tf_op jit(solution)/shard_map/ppermute | solution.py:360
  15.5 0.0 copy-done.4
  15.5 3.1 %shard_map.56 = bf16[8,1056,128]{2,1,0:T(8,128)(2,1)S(1)} custom-call(bf16[128,9216]{1,0:T(8,128)(2,1)S(1)} %get-tuple-element.16.in_ref, bf16[3,9216]{1,0:T(4,128)(2,1)S(1)} %collective-permute-done.edge_ref, f32[4,9216]{1,0:T(4,128)S(1)} %copy-done.4, f32[136,128]{1,0:T(8,128)S(1)} %get-tuple-element.17.early_ref), custom_call_target="tpu_custom_call" | custom-call | flops 100000000 | bytes 3000000 | tf_op jit(solution)/shard_map/pallas_call | solution.py:148
  18.6 31.7 %all_to_all.20.pay_ref = bf16[8,1056,128]{2,1,0:T(8,128)(2,1)S(1)} all-to-all(bf16[8,1056,128]{2,1,0:T(8,128)(2,1)S(1)} %shard_map.56), channel_id=1, replica_groups=mesh['y'=8,'core'=2,'zh'=4,'zl'=2,'x'=4] {'zl','x'}, dimensions={0} | all-to-all | bytes 4325376 | tf_op jit(solution)/shard_map/all_to_all | solution.py:363
  50.3 0.0 copy-start.7
  50.3 1.1 shard_map.57
  51.4 9.1 %all-to-all-start.1 = ((bf16[32,40,128]{2,1,0:T(8,128)(2,1)}), bf16[32,40,128]{2,1,0:T(8,128)(2,1)S(1)}, u32[]{:S(2)}, u32[]{:S(2)}) async-start(bf16[32,40,128]{2,1,0:T(8,128)(2,1)} %shard_map.57), calls=%async_computation.1 | async-start | bytes 655360 | tf_op jit(solution)/shard_map/all_to_all | solution.py:365
  60.5 0.0 copy-done.7
  60.5 0.0 copy-start.3
  60.5 1.7 %copy-done.3 = bf16[128,9216]{1,0:T(8,128)(2,1)S(1)} copy-done((bf16[128,9216]{1,0:T(8,128)(2,1)S(1)}, bf16[128,9216]{1,0:T(8,128)(2,1)}, u32[]{:S(2)}) %copy-start.3) | copy-done | bytes 2359320
  62.2 5.0 %shard_map.58 = (f32[128,8192]{1,0:T(8,128)S(1)}, bf16[128,512]{1,0:T(8,128)(2,1)S(1)}) custom-call(bf16[128,9216]{1,0:T(8,128)(2,1)S(1)} %copy-done.3, bf16[3,9216]{1,0:T(4,128)(2,1)S(1)} %collective-permute-done.edge_ref, f32[4,9216]{1,0:T(4,128)S(1)} %copy-done.4, f32[384,128]{1,0:T(8,128)S(1)} %get-tuple-element.19.late_ref, f32[1,128]{1,0:T(1,128)S(1)} %bitcast.6), custom_call_target="tpu_custom_call" | custom-call | flops 1000000000 | bytes 8000000 | tf_op jit(solution)/shard_map/pallas_call | solution.py:304
  67.2 0.0 copy-start
  67.2 1.9 %copy-done = f32[128,8192]{1,0:T(8,128)} copy-done((f32[128,8192]{1,0:T(8,128)}, f32[128,8192]{1,0:T(8,128)S(1)}, u32[]{:S(2)}) %copy-start) | copy-done | bytes 4194328
  69.1 5.7 %all-to-all-done.1.rows_ref = bf16[32,40,128]{2,1,0:T(8,128)(2,1)S(1)} async-done(((bf16[32,40,128]{2,1,0:T(8,128)(2,1)}), bf16[32,40,128]{2,1,0:T(8,128)(2,1)S(1)}, u32[]{:S(2)}, u32[]{:S(2)}) %all-to-all-start.1) | async-done | bytes 327712 | tf_op jit(solution)/shard_map/all_to_all | solution.py:365
  74.9 0.1 shard_map.59.own_ref
  74.9 1.9 %collective-permute-start.1 = (f32[8,40,128]{2,1,0:T(8,128)S(1)}, f32[8,40,128]{2,1,0:T(8,128)S(1)}, u32[]{:S(2)}, u32[]{:S(2)}) collective-permute-start(f32[8,40,128]{2,1,0:T(8,128)S(1)} %shard_map.59.own_ref), channel_id=1, source_target_pairs={{0,32},{32,0},{1,33},{33,1},{2,34},{34,2},{3,35},{35,3},{4,36},{36... | collective-permute-start | bytes 491528 | tf_op jit(solution)/shard_map/ppermute | solution.py:369
  76.9 1.4 %collective-permute-done.1.other_ref = f32[8,40,128]{2,1,0:T(8,128)S(1)} collective-permute-done((f32[8,40,128]{2,1,0:T(8,128)S(1)}, f32[8,40,128]{2,1,0:T(8,128)S(1)}, u32[]{:S(2)}, u32[]{:S(2)}) %collective-permute-start.1) | collective-permute-done | bytes 163872 | tf_op jit(solution)/shard_map/ppermute | solution.py:369
  78.2 0.1 shard_map.60
  78.3 21.1 %all_to_all.21 = bf16[32,32,128]{2,1,0:T(8,128)(2,1)S(1)} all-to-all(bf16[32,32,128]{2,1,0:T(8,128)(2,1)S(1)} %shard_map.60), channel_id=1, replica_groups=mesh['y'=8,'core'=2,'zh'=4,'zl'=2,'x'=4] {'y','zh'}, dimensions={0} | all-to-all | bytes 524288 | tf_op jit(solution)/shard_map/all_to_all | solution.py:370
  99.4 0.5 shard_map.61
  99.9 0.0 copy-start.1
  99.9 28.0 %all_to_all.22.state_ref = bf16[8,1024,128]{2,1,0:T(8,128)(2,1)S(1)} all-to-all(bf16[8,1024,128]{2,1,0:T(8,128)(2,1)S(1)} %shard_map.61), channel_id=1, replica_groups=mesh['y'=8,'core'=2,'zh'=4,'zl'=2,'x'=4] {'zl','x'}, dimensions={0} | all-to-all | bytes 4194304 | tf_op jit(solution)/shard_map/all_to_all | solution.py:372
  127.9 0.0 copy-done.1
  127.9 2.2 %shard_map.62 = bf16[128,8192]{1,0:T(8,128)(2,1)} custom-call(bf16[128,512]{1,0:T(8,128)(2,1)S(1)} %get-tuple-element.22.rea_ref, f32[384,128]{1,0:T(8,128)S(1)} %get-tuple-element.19.late_ref, f32[128,8192]{1,0:T(8,128)S(1)} %copy-done.1, bf16[8,1024,128]{2,1,0:T(8,128)(2,1)S(1)} %all_to_all.22.state_ref), custom_call_target="tpu_custom_call" | custom-call | flops 100000000 | bytes 2000000 | tf_op jit(solution)/shard_map/pallas_call | solution.py:346
Async XLA Ops:
  0.0 15.5 %copy-start.4 = (f32[4,9216]{1,0:T(4,128)S(1)}, f32[4,9216]{1,0:T(4,128)}, u32[]{:S(2)}) copy-start(f32[4,9216]{1,0:T(4,128)} %w_ref.3) | copy-start | bytes 442372
  1.0 14.5 %collective-permute-start = (bf16[3,9216]{1,0:T(4,128)(2,1)S(1)}, bf16[3,9216]{1,0:T(4,128)(2,1)S(1)}, u32[]{:S(2)}, u32[]{:S(2)}) collective-permute-start(bf16[3,9216]{1,0:T(4,128)(2,1)S(1)} %slice.3), channel_id=1, source_target_pairs={{0,1},{1,2},{2,3},{3,4},{4,5},{5,6},{6,7},{7,8},{8,9},{9,10},{10,1... | collective-permute-start | bytes 165896 | tf_op jit(solution)/shard_map/ppermute | solution.py:360
  4.4 1.7 %copy-start.2 = (bf16[128,9216]{1,0:T(8,128)(2,1)S(1)}, bf16[128,9216]{1,0:T(8,128)(2,1)}, u32[]{:S(2)}) copy-start(bf16[128,9216]{1,0:T(8,128)(2,1)} %in_ref.1) | copy-start | bytes 7077892
  6.1 0.8 copy-start.5
  6.9 0.7 copy-start.6
  50.3 10.2 %copy-start.7 = (f32[128]{0:T(128)S(1)}, f32[128]{0:T(128)}, u32[]{:S(2)}) copy-start(f32[128]{0:T(128)} %param.9) | copy-start | bytes 1540
  51.4 23.4 %all-to-all-start.1 = ((bf16[32,40,128]{2,1,0:T(8,128)(2,1)}), bf16[32,40,128]{2,1,0:T(8,128)(2,1)S(1)}, u32[]{:S(2)}, u32[]{:S(2)}) async-start(bf16[32,40,128]{2,1,0:T(8,128)(2,1)} %shard_map.57), calls=%async_computation.1 | async-start | bytes 655360 | tf_op jit(solution)/shard_map/all_to_all | solution.py:365
  60.5 1.7 %copy-start.3 = (bf16[128,9216]{1,0:T(8,128)(2,1)S(1)}, bf16[128,9216]{1,0:T(8,128)(2,1)}, u32[]{:S(2)}) copy-start(bf16[128,9216]{1,0:T(8,128)(2,1)} %in_ref.1) | copy-start | bytes 7077892
  67.2 1.9 %copy-start = (f32[128,8192]{1,0:T(8,128)}, f32[128,8192]{1,0:T(8,128)S(1)}, u32[]{:S(2)}) copy-start(f32[128,8192]{1,0:T(8,128)S(1)} %get-tuple-element.23.part_ref) | copy-start | bytes 12582916
  74.9 3.3 %collective-permute-start.1 = (f32[8,40,128]{2,1,0:T(8,128)S(1)}, f32[8,40,128]{2,1,0:T(8,128)S(1)}, u32[]{:S(2)}, u32[]{:S(2)}) collective-permute-start(f32[8,40,128]{2,1,0:T(8,128)S(1)} %shard_map.59.own_ref), channel_id=1, source_target_pairs={{0,32},{32,0},{1,33},{33,1},{2,34},{34,2},{3,35},{35,3},{4,36},{36... | collective-permute-start | bytes 491528 | tf_op jit(solution)/shard_map/ppermute | solution.py:369
  99.9 28.0 %copy-start.1 = (f32[128,8192]{1,0:T(8,128)S(1)}, f32[128,8192]{1,0:T(8,128)}, u32[]{:S(2)}) copy-start(f32[128,8192]{1,0:T(8,128)} %copy-done) | copy-start | bytes 12582916
